TPU v7x, 32 devices: a whole 2x2x4 slice. The times are simulated.
32 devices in a mesh: gz: 8 (over z, y), phi: 4 (over x, core).
Axes of the slice: x: 2, y: 2, z: 4, core: 2. Of those that a mesh axis runs over, the one named last changes fastest.
Arguments:
- field: float32 [16, 4, 2048, 1024], P(None, None, 'gz', 'phi'), may hold values from -6 to 6
- field_tangent: float32 [16, 4, 2048, 1024], P(None, None, 'gz', 'phi'), may hold values from -6 to 6
- spectral_weight: float32 [2, 16, 16, 64, 64], P(None, None, None, 'gz', 'phi'), may hold values from -1 to 1
- local_weight: float32 [16, 16], replicated, may hold values from -1.5 to 1.5
- bias_term: float32 [16], replicated, may hold values from -3 to 3
- z_modes: int32 [64], replicated, may hold values from 0 to 1023, as said below
- phi_modes: int32 [64], replicated, may hold values from 0 to 1023, as said below
Outputs:
- output: float32 [16, 4, 2048, 1024], P(None, None, 'gz', 'phi')
- output_tangent: float32 [16, 4, 2048, 1024], P(None, None, 'gz', 'phi')
Inputs may be any that keep to these rules, and one draw needn't show every extreme that they name: `z_modes`: entries may repeat; 0 and 1023 both occur. `phi_modes`: entries may repeat; 0 and 1023 both occur.
All inputs are finite; a program needn't handle non-finite values.
Results may differ from a plain program's by a relative error of at most 0.000078.
Values sent between devices are 32-bit elements; how exact they have to be, the bound alone decides.
No kernel may reach another device: no remote copies, remote signals or barrier semaphores. Data moves between devices by JAX's collectives and lax.ppermute only.
A program may use at most 256 MiB of HBM per device.

v0:
```python
import functools
import math

import jax
import jax.numpy as jnp
from jax import lax
from jax.sharding import PartitionSpec as P

precise = lax.Precision.HIGHEST


def angle_table(positions, modes, length):
    product = positions[:, None] * modes[None, :] % length
    angle = product.astype(jnp.float32) * (2.0 * math.pi / length)
    return (jnp.cos(angle), jnp.sin(angle))


def phi_transform(real_src, imag_src, form, phi_modes, phi_global, phi_total):
    spec_in = form + ",fq->"
    spec_out = "q" + form.replace("f", "").replace("k", "").replace("z", "")
    lead = "k" if "k" in form else "z"
    spec = spec_in + "q" + lead + spec_out[1:]
    p_cosine, p_sine = angle_table(phi_global, phi_modes, phi_total)
    real_part = jnp.einsum(spec, real_src, p_cosine, precision=precise)
    imag_part = -jnp.einsum(spec, real_src, p_sine, precision=precise)
    real_part = real_part + jnp.einsum(spec, imag_src, p_sine, precision=precise)
    imag_part = imag_part + jnp.einsum(spec, imag_src, p_cosine, precision=precise)
    return lax.psum_scatter(
        jnp.stack([real_part, imag_part], axis=1), "phi", scatter_dimension=0, tiled=True
    )


def body(field, field_tangent, spectral_weight, local_weight, bias_term, z_modes, phi_modes):
    channels, cycles, z_local, phi_local = field.shape
    z_count = lax.axis_size("gz")
    phi_count = lax.axis_size("phi")
    z_total = z_local * z_count
    phi_total = phi_local * phi_count
    kz_total = z_modes.shape[0]
    kp_total = phi_modes.shape[0]
    z_global = lax.axis_index("gz") * z_local + jnp.arange(z_local, dtype=jnp.int32)
    phi_global = lax.axis_index("phi") * phi_local + jnp.arange(phi_local, dtype=jnp.int32)
    stacked = jnp.stack([field, field_tangent])
    modes = z_modes
    z_cosine, z_sine = angle_table(z_global, modes, z_total)
    real_part = jnp.einsum("pcrzf,zk->kpcrf", stacked, z_cosine, precision=precise)
    imag_part = -jnp.einsum("pcrzf,zk->kpcrf", stacked, z_sine, precision=precise)
    zspectra = lax.psum_scatter(
        jnp.stack([real_part, imag_part], axis=1), "gz", scatter_dimension=0, tiled=True
    )
    spectra = phi_transform(
        zspectra[:, 0], zspectra[:, 1], "kpcrf", phi_modes, phi_global, phi_total
    )
    spectra = spectra * (1.0 / math.sqrt(z_total * phi_total))
    freal = spectra[:, 0]
    fimag = spectra[:, 1]
    wreal = spectral_weight[0]
    wimag = spectral_weight[1]
    greal = jnp.einsum("qkpcr,cokq->qkpor", freal, wreal, precision=precise) - jnp.einsum(
        "qkpcr,cokq->qkpor", fimag, wimag, precision=precise
    )
    gimag = jnp.einsum("qkpcr,cokq->qkpor", fimag, wreal, precision=precise) + jnp.einsum(
        "qkpcr,cokq->qkpor", freal, wimag, precision=precise
    )
    mixed = jnp.stack([greal, gimag], axis=1)
    initial = jnp.zeros((2, channels, cycles, z_local, phi_local), jnp.float32)
    whole = lax.all_gather(mixed, "phi", axis=0, tiled=True)
    p_cosine, p_sine = angle_table(phi_global, phi_modes, phi_total)
    hreal = jnp.einsum("qkpor,fq->kporf", whole[:, 0], p_cosine, precision=precise) - jnp.einsum(
        "qkpor,fq->kporf", whole[:, 1], p_sine, precision=precise
    )
    himag = jnp.einsum("qkpor,fq->kporf", whole[:, 0], p_sine, precision=precise) + jnp.einsum(
        "qkpor,fq->kporf", whole[:, 1], p_cosine, precision=precise
    )
    columns = jnp.stack([hreal, himag], axis=1)
    piece = lax.all_gather(columns, "gz", axis=0, tiled=True)
    modes = lax.slice_in_dim(z_modes, 0, piece.shape[0], axis=0)
    z_cosine, z_sine = angle_table(z_global, modes, z_total)
    spectral = (
        initial
        + jnp.einsum("kporf,zk->porzf", piece[:, 0], z_cosine, precision=precise)
        - jnp.einsum("kporf,zk->porzf", piece[:, 1], z_sine, precision=precise)
    )
    spectral = spectral * (2.0 / math.sqrt(kz_total * kp_total))
    mixing = jnp.einsum("pcrzf,co->porzf", stacked, local_weight, precision=precise)
    preact = spectral[0] + mixing[0] + bias_term[:, None, None, None]
    tangent = spectral[1] + mixing[1]
    output, output_tangent = jax.jvp(
        functools.partial(jax.nn.gelu, approximate=True), (preact,), (tangent,)
    )
    return (output, output_tangent)


def solution(mesh):
    return jax.shard_map(
        body,
        mesh=mesh,
        in_specs=(
            P(None, None, "gz", "phi"),
            P(None, None, "gz", "phi"),
            P(None, None, None, "gz", "phi"),
            P(),
            P(),
            P(),
            P(),
        ),
        out_specs=(P(None, None, "gz", "phi"), P(None, None, "gz", "phi")),
        check_vma=False,
    )
```

profile of v0, /device:TPU:0, one launch (start us, length us, event | category | flops | bytes accessed | tf_op | source)
XLA Modules:
  0.0 808.2 jit_solution(1955773198153253634)
XLA Ops:
  7.2 0.0 copy-start
  7.2 0.0 reduce-scatter.5.cloned.1.call-start
  7.2 0.0 copy-start.3
  7.3 28.5 %negate_bitcast_fusion = f32[64,1,2,16,4,256]{5,0,4,3,2,1:T(8,128)} fusion(s32[64]{0:T(128)} %param.12, s32[256]{0:T(256)S(1)} %iota_add_fusion.1, f32[1,16,4,256,256]{4,3,2,1,0:T(8,128)} %bitcast.123, f32[1,16,4,256,256]{4,3,2,1,0:T(8,128)} %bitcast.126), kind=kOutput, calls=%fused_computation.31 | convolution fusion | flops 6453166080 | bytes 41944320 | tf_op jit(solution)/shard_map/pcrzf,zk->kpcrf/dot_general | solution.py:47
  35.7 0.0 copy-done.3
  35.7 26.7 %convolution_bitcast_fusion = f32[64,1,2,16,4,256]{5,0,4,3,2,1:T(8,128)} fusion(s32[64]{0:T(128)S(1)} %copy-done.3, s32[256]{0:T(256)S(1)} %iota_add_fusion.1, f32[1,16,4,256,256]{4,3,2,1,0:T(8,128)} %bitcast.124, f32[1,16,4,256,256]{4,3,2,1,0:T(8,128)} %bitcast.127), kind=kOutput, calls=%fused_computation.32 | convolution fusion | flops 6451068928 | bytes 41944320 | tf_op jit(solution)/shard_map/pcrzf,zk->kpcrf/dot_general | solution.py:46
  62.5 11.9 %pad_maximum_fusion.1 = f32[64,2,2,16,4,256]{5,0,4,3,2,1:T(8,128)} fusion(f32[64,1,2,16,4,256]{5,0,4,3,2,1:T(8,128)} %negate_bitcast_fusion, f32[64,1,2,16,4,256]{5,0,4,3,2,1:T(8,128)} %convolution_bitcast_fusion), kind=kLoop, calls=%fused_computation.24 | loop fusion | flops 4194304 | bytes 33554432 | tf_op jit(solution)/shard_map/stack | solution.py:49
  74.3 0.0 copy-start.2
  74.3 0.0 reduce-scatter.5.cloned.1.call-update
  74.3 0.3 reduce-scatter.7.cloned.1.call-start
  74.6 285.3 %reduce-scatter.5.cloned.1.call-done = f32[8,2,2,16,4,256]{5,0,4,3,2,1:T(8,128)} async-done(((f32[64,2,2,16,4,256]{5,0,4,3,2,1:T(8,128)}), f32[8,2,2,16,4,256]{5,0,4,3,2,1:T(8,128)}) %reduce-scatter.5.cloned.1.call-update) | async-done | bytes 2097168 | tf_op jit(solution)/shard_map/reduce_scatter | solution.py:48
  359.9 1.7 slice_bitcast_fusion.4
  361.6 0.0 copy-done.2
  361.6 1.7 convolution_negate_fusion
  363.3 1.7 fusion.35
  365.0 1.7 fusion.25
  366.7 1.7 fusion.24
  368.4 0.1 pad_maximum_fusion.3
  368.5 4.4 copy.52
  372.9 6.5 reshape.24
  379.4 0.0 reduce-scatter.7.cloned.1.call-update
  379.5 0.3 all-gather.2.cloned.1.call-start
  379.8 1.7 fusion.122
  381.5 0.9 copy.56
  382.4 0.9 copy.55
  383.3 17.0 %reduce-scatter.7.cloned.1.call-done = f32[16,2048]{1,0:T(8,128)} async-done(((f32[64,2048]{1,0:T(8,128)}), f32[16,2048]{1,0:T(8,128)}) %reduce-scatter.7.cloned.1.call-update) | async-done | bytes 131088
  400.3 1.6 reshape.25
  402.0 0.4 copy_multiply_fusion
  402.4 1.1 fusion.28
  403.5 1.1 fusion.30
  404.6 1.2 fusion.23
  405.8 1.2 fusion.22
  407.0 0.4 pad_maximum_fusion.4
  407.4 27.2 %all_gather.6 = f32[64,2,8,2,16,4]{4,5,3,2,0,1:T(4,128)S(1)} all-gather(f32[16,2,8,2,16,4]{4,5,3,2,0,1:T(4,128)S(1)} %pad_maximum_fusion.4), channel_id=1, replica_groups=mesh['gz'=8,'phi'=4] {'phi'}, dimensions={0}, use_global_device_ids=true | all-gather | bytes 655360 | tf_op jit(solution)/shard_map/all_gather | solution.py:67
  434.6 2.3 slice_bitcast_fusion.2
  436.8 2.3 copy.35
  439.2 2.3 fusion.50
  441.4 2.2 fusion.46
  443.7 1.2 copy.36
  444.9 2.5 fusion.20
  447.4 2.5 fusion.21
  449.9 1.5 pad_maximum_fusion.2
  451.4 0.0 all-gather.2.cloned.1.call-update
  451.4 23.5 %pad_maximum_fusion = f32[2,16,4,256,256]{4,3,2,1,0:T(8,128)} fusion(f32[1,16,4,256,256]{4,3,2,1,0:T(8,128)} %bitcast.125, f32[1,16,4,256,256]{4,3,2,1,0:T(8,128)} %bitcast.128), kind=kLoop, calls=%fused_computation | loop fusion | flops 8388608 | bytes 67108864 | tf_op jit(solution)/shard_map/stack | solution.py:43
  474.9 0.0 copy-done
  474.9 57.5 %fusion = f32[2,4,256,256,16]{3,4,2,1,0:T(8,128)} fusion(f32[2,16,4,256,256]{4,3,2,1,0:T(8,128)} %pad_maximum_fusion, f32[16,16]{1,0:T(8,128)S(1)} %copy-done), kind=kOutput, calls=%fused_computation.2 | convolution fusion | flops 1610612736 | bytes 67109888 | tf_op jit(solution)/shard_map/pcrzf,co->porzf/dot_general | solution.py:85
  532.5 30.9 %copy.73 = f32[2,4,256,256,16]{3,2,1,4,0:T(8,128)} copy(f32[2,4,256,256,16]{3,4,2,1,0:T(8,128)} %fusion) | data formatting | bytes 67108864 | tf_op jit(solution)/shard_map/pcrzf,co->porzf/dot_general | solution.py:85
  563.4 116.2 %all-gather.2.cloned.1.call-done = f32[64,2,2,16,4,256]{5,3,4,2,0,1:T(8,128)} async-done(((f32[8,2,2,16,4,256]{5,3,4,2,0,1:T(8,128)}), f32[64,2,2,16,4,256]{5,3,4,2,0,1:T(8,128)}) %all-gather.2.cloned.1.call-update) | async-done | bytes 16777232 | tf_op jit(solution)/shard_map/all_gather | solution.py:76
  679.6 9.3 %slice_bitcast_fusion = (f32[64,2,16,4,256]{4,2,3,1,0:T(8,128)S(1)}, f32[64,2,16,4,256]{4,2,3,1,0:T(8,128)}) fusion(f32[64,2,2,16,4,256]{5,3,4,2,0,1:T(8,128)} %all-gather.2.cloned.1.call-done), kind=kLoop, calls=%fused_computation.26 | loop fusion | bytes 33554432 | tf_op jit(solution)/shard_map/squeeze | solution.py:82
  688.9 37.7 %fusion.18 = f32[256,2,16,4,256]{4,0,3,2,1:T(8,128)} fusion(f32[64,2,16,4,256]{4,2,3,1,0:T(8,128)} %get-tuple-element.5, s32[64]{0:T(128)S(1)} %copy-done.3, s32[256]{0:T(256)S(1)} %iota_add_fusion.1), kind=kOutput, calls=%fused_computation.29 | convolution fusion | flops 6442680320 | bytes 41944320 | tf_op jit(solution)/shard_map/kporf,zk->porzf/dot_general | solution.py:81
  726.6 0.0 copy-start.4
  726.6 40.8 %multiply_bitcast_fusion = f32[2,16,4,256,256]{4,3,2,1,0:T(8,128)} fusion(f32[256,2,16,4,256]{4,0,3,2,1:T(8,128)} %fusion.18, f32[64,2,16,4,256]{4,2,3,1,0:T(8,128)S(1)} %get-tuple-element.4, s32[64]{0:T(128)S(1)} %copy-done.3, s32[256]{0:T(256)S(1)} %iota_add_fusion.1), kind=kOutput, calls=%fused_computation.4 | convolution fusion | flops 6459457536 | bytes 75498752 | tf_op jit(solution)/shard_map/kporf,zk->porzf/dot_general | solution.py:82
  767.4 0.0 copy-done.4
  767.4 0.0 copy-start.1
  767.4 33.8 %fusion.13 = (f32[16,4,256,256]{3,2,1,0:T(8,128)}, f32[16,4,256,256]{3,2,1,0:T(8,128)}) fusion(f32[2,16,4,256,256]{4,3,2,1,0:T(8,128)} %bitcast.129, f32[2,16,4,256,256]{4,3,2,1,0:T(8,128)} %multiply_bitcast_fusion, f32[16]{0:T(128)S(1)} %copy-done.4), kind=kLoop, calls=%fused_computation.18 | loop fusion | flops 96468992 | bytes 100663360 | tf_op jit(solution)/shard_map/jvp()/add_any | solution.py:88
  801.3 0.0 copy-done.1
  (2 shorter events, 0.0 us)
Async XLA Ops:
  7.2 467.8 %copy-start = (f32[16,16]{1,0:T(8,128)S(1)}, f32[16,16]{1,0:T(8,128)}, u32[]{:S(2)}) copy-start(f32[16,16]{1,0:T(8,128)} %param.10) | copy-start | bytes 3076
  7.2 352.7 %reduce-scatter.5.cloned.1.call-start = ((), (), s32[]{:S(2)}) async-start(), calls=%async_computation.2 | async-start | bytes 18874368 | tf_op jit(solution)/shard_map/reduce_scatter | solution.py:48
  7.2 28.5 %copy-start.3 = (s32[64]{0:T(128)S(1)}, s32[64]{0:T(128)}, u32[]{:S(2)}) copy-start(s32[64]{0:T(128)} %param.12) | copy-start | bytes 772
  74.3 287.2 %copy-start.2 = (s32[64]{0:T(128)S(1)}, s32[64]{0:T(128)}, u32[]{:S(2)}) copy-start(s32[64]{0:T(128)} %param.13) | copy-start | bytes 772
  74.3 326.0 %reduce-scatter.7.cloned.1.call-start = ((), (), s32[]{:S(2)}) async-start(), calls=%async_computation.4 | async-start | bytes 655360
  379.5 300.1 %all-gather.2.cloned.1.call-start = ((), (), s32[]{:S(2)}) async-start(), calls=%async_computation.3 | async-start | bytes 18874368 | tf_op jit(solution)/shard_map/all_gather | solution.py:76
  726.6 40.9 %copy-start.4 = (f32[16]{0:T(128)S(1)}, f32[16]{0:T(128)}, u32[]{:S(2)}) copy-start(f32[16]{0:T(128)} %param.11) | copy-start | bytes 196
  767.4 33.8 %copy-start.1 = (f32[16,16]{1,0:T(8,128)S(1)}, f32[16,16]{1,0:T(8,128)}, u32[]{:S(2)}) copy-start(f32[16,16]{1,0:T(8,128)} %param.10) | copy-start | bytes 3076
Sparse Core Ops, SparseCore 0:
  74.5 285.3 reduce-scatter.4
  379.6 20.6 reduce-scatter.6
  451.6 227.9 all-gather.1
where the time goes:
time: 816 us; the launch traced here: 808 us
  waiting for transfers between devices  419 us (51%)
  matrix products  212 us (26%)
  other arithmetic  71.6 us (9%)
  local copies, waits for them, and re-layouts  63.7 us (8%)
  blocking collectives  27.2 us (3%)
  between operations  14.4 us (2%)
    reduce_scatter x1, waiting for transfers between devices, body(): lax.psum_scatter(jnp.stack([real_part, imag_part], axis=1), 'gz', scatter...  285 us
    all_gather x1, waiting for transfers between devices, body(): piece = lax.all_gather(columns, 'gz', axis=0, tiled=True)  116 us
    dot_general x1, matrix products, body(): jnp.einsum('pcrzf,co->porzf', stacked, local_weight, precision=precise)  57.5 us
    dot_general x1, matrix products, body(): jnp.einsum('kporf,zk->porzf', piece[:, 1], z_sine, precision=precise)  40.8 us
    dot_general x1, matrix products, body(): jnp.einsum('kporf,zk->porzf', piece[:, 0], z_cosine, precision=precise)  37.7 us
    add_any x1, other arithmetic, body(): jax.jvp(functools.partial(jax.nn.gelu, approximate=True), (preact,), (tan...  33.8 us
    dot_general x1, local copies, waits for them, and re-layouts, body(): jnp.einsum('pcrzf,co->porzf', stacked, local_weight, precision=precise)  30.9 us
    dot_general x1, matrix products, body(): jnp.einsum('pcrzf,zk->kpcrf', stacked, z_sine, precision=precise)  28.5 us
  transfers between devices with their start and end apart: 3, of which 3 were waited for; matrix products, arithmetic and copies ran while one was open for 14% of the time, Pallas kernels for 0%

commit v1 on v0

v1 whole, which is shorter than its diff:
```python
import functools
import itertools
import math

import jax
import jax.numpy as jnp
from jax import lax
from jax.experimental import pallas as pl
from jax.experimental.pallas import tpu as pltpu
from jax.sharding import PartitionSpec as P

f32 = jnp.float32
bf16 = jnp.bfloat16
VMEM_LIMIT = 56 * 1024 * 1024


def split(x):
    high = lax.reduce_precision(x, 8, 7)
    return high.astype(bf16), (x - high).astype(bf16)


def halves(x):
    high = x.astype(bf16)
    return high, (x - high.astype(f32)).astype(bf16)


def dot(a, b):
    return lax.dot_general(a, b, (((1,), (0,)), ((), ())), preferred_element_type=f32)


def angles(positions, modes, length):
    product = positions[:, None] * modes[None, :] % length
    angle = product.astype(f32) * (2.0 * math.pi / length)
    return jnp.cos(angle), jnp.sin(angle)


def exchange(items, width):
    items = list(items)
    count = len(items)
    lanes = items[0].shape[-1]
    lane = lax.broadcasted_iota(jnp.int32, items[0].shape, items[0].ndim - 1)
    step = 1
    while step < count:
        shift = width * step
        low = (lane // shift) % 2 == 0
        for i in range(count):
            if i & step:
                continue
            a, b = items[i], items[i | step]
            items[i] = jnp.where(low, a, pltpu.roll(b, shift, 1))
            items[i | step] = jnp.where(low, pltpu.roll(a, lanes - shift, 1), b)
        step *= 2
    return items


def forward_kernel(x_ref, t_ref, phi_ref, z_ref, keep_ref, send_ref, *, n_phi, width):
    cycles, z_local, _ = x_ref.shape[1:]
    modes2 = z_ref.shape[0] // 2
    modes = modes2 // 2
    lanes = phi_ref.shape[1] // 2
    lane = lax.broadcasted_iota(jnp.int32, (modes, lanes), 1)
    sign = jnp.where(lane < lanes // 2, 1.0, -1.0).astype(f32)
    batch = [(ref, r) for ref in (x_ref, t_ref) for r in range(cycles)]
    for group in range(len(batch) // n_phi):
        items = []
        for ref, r in batch[group * n_phi : (group + 1) * n_phi]:
            high, low = halves(ref[0, r])
            y = dot(jnp.concatenate([high, low], axis=1), phi_ref[...])
            y = y[:, :lanes] + y[:, lanes:]
            y_high, y_low = halves(y)
            m = dot(z_ref[...], jnp.concatenate([y_high, y_low], axis=1))
            m = m[:modes2, :lanes] + (m[:modes2, lanes:] + m[modes2:, :lanes])
            items.append(m[:modes] + sign * pltpu.roll(m[modes:], lanes // 2, 1))
        items = exchange(items, width)
        shape = keep_ref.shape[1:-4] + keep_ref.shape[-2:]
        for slot, item in enumerate(items):
            out = keep_ref if slot % 2 == 0 else send_ref
            out[slot // 2, ..., 0, group, :, :] = item.reshape(shape)


def forward(field, tangent, phi_table, z_table, n_phi, n_gz, width):
    channels, cycles, z_local, phi_local = field.shape
    groups = 2 * cycles // n_phi
    modes = z_table.shape[0] // 4
    lanes = phi_table.shape[1] // 2
    out = jax.ShapeDtypeStruct((n_phi // 2, n_gz, channels, groups, modes // n_gz, lanes), f32)
    block = pl.BlockSpec((1, cycles, z_local, phi_local), lambda c: (c, 0, 0, 0))
    out_block = pl.BlockSpec(
        (n_phi // 2, n_gz, 1, groups, modes // n_gz, lanes), lambda c: (0, 0, c, 0, 0, 0)
    )
    return pl.pallas_call(
        functools.partial(forward_kernel, n_phi=n_phi, width=width),
        grid=(channels,),
        in_specs=[
            block,
            block,
            pl.BlockSpec(phi_table.shape, lambda c: (0, 0)),
            pl.BlockSpec(z_table.shape, lambda c: (0, 0)),
        ],
        out_specs=[out_block, out_block],
        out_shape=[out, out],
        compiler_params=pltpu.CompilerParams(vmem_limit_bytes=VMEM_LIMIT),
        cost_estimate=pl.CostEstimate(
            flops=12 * field.size * phi_table.shape[1],
            bytes_accessed=8 * field.size,
            transcendentals=0,
        ),
        name="forward_transform",
    )(field, tangent, phi_table, z_table)


def local_kernel(x_ref, t_ref, w_ref, xo_ref, to_ref):
    channels, _, rows, columns = x_ref.shape
    for ref, out in ((x_ref, xo_ref), (t_ref, to_ref)):
        for start in range(0, rows, 8):
            x = ref[:, 0, start : start + 8, :].reshape(channels * 8, columns)
            high, low = halves(x)
            mixed = dot(w_ref[...], jnp.concatenate([high, low], axis=0))
            mixed = mixed[: channels * 8] + mixed[channels * 8 :]
            out[:, start : start + 8, :] = mixed.reshape(channels, 8, columns)


def local_mix(field, tangent, weight, cycle):
    channels, _, z_local, phi_local = field.shape
    rows = 32
    out = jax.ShapeDtypeStruct((channels, z_local, phi_local), f32)
    block = pl.BlockSpec((channels, 1, rows, phi_local), lambda z: (0, cycle, z, 0))
    out_block = pl.BlockSpec((channels, rows, phi_local), lambda z: (0, z, 0))
    size = channels * z_local * phi_local
    return pl.pallas_call(
        local_kernel,
        grid=(z_local // rows,),
        in_specs=[block, block, pl.BlockSpec(weight.shape, lambda z: (0, 0))],
        out_specs=[out_block, out_block],
        out_shape=[out, out],
        compiler_params=pltpu.CompilerParams(vmem_limit_bytes=VMEM_LIMIT),
        cost_estimate=pl.CostEstimate(flops=1024 * size, bytes_accessed=16 * size, transcendentals=0),
        name="local_mix",
    )(field, tangent, weight)


def mix_kernel(s_ref, wr_ref, wi_ref, out_ref):
    channels = s_ref.shape[0]
    lanes = s_ref.shape[-1]
    total = jnp.zeros(out_ref.shape, f32)
    for c in range(channels):
        s = s_ref[c]
        turned = jnp.concatenate([s[..., lanes // 2 :], s[..., : lanes // 2]], axis=-1)
        total = total + s[None] * wr_ref[c][:, None] + turned[None] * wi_ref[c][:, None]
    out_ref[...] = total


def mix(spectrum, wr, wi):
    return pl.pallas_call(
        mix_kernel,
        out_shape=jax.ShapeDtypeStruct((wr.shape[1],) + spectrum.shape[1:], f32),
        compiler_params=pltpu.CompilerParams(vmem_limit_bytes=VMEM_LIMIT),
        name="mode_mix",
    )(spectrum, wr, wi)


def gelu_pair(x, t):
    a = math.sqrt(2.0 / math.pi)
    b = a * 0.044715
    square = x * x
    th = jnp.tanh(x * (a + b * square))
    half = 0.5 * x
    slope = 0.5 + 0.5 * th + half * (1.0 - th * th) * (a + (3.0 * b) * square)
    return half + half * th, slope * t


def inverse_kernel(own_ref, got_ref, bias_ref, phi_ref, z_ref, *refs, n_phi, width):
    cycles = (len(refs) - 2) // 2
    lx, lt = refs[:cycles], refs[cycles : 2 * cycles]
    out_ref, out_t_ref = refs[2 * cycles :]
    groups, _, lanes = own_ref.shape[-3:]
    modes = z_ref.shape[1] // 6
    phi_local = phi_ref.shape[1] // 2
    bias = bias_ref[pl.program_id(0)]
    spectral = []
    for group in range(groups):
        items = [
            (own_ref if slot % 2 == 0 else got_ref)[slot // 2, ..., 0, group, :, :].reshape(modes, lanes)
            for slot in range(n_phi)
        ]
        g = jnp.concatenate(exchange(items, width), axis=0)
        g_high, g_low = halves(g)
        h = dot(jnp.concatenate([g_high, g_low, g_high], axis=1), phi_ref[...])
        for b in range(n_phi):
            part = h[b * modes : (b + 1) * modes]
            part = jnp.concatenate([part[:, :phi_local], part[:, phi_local:]], axis=0)
            spectral.append(halves(part))
    for r in range(cycles):
        values = []
        for high, low in (spectral[r], spectral[cycles + r]):
            values.append(dot(z_ref[...], jnp.concatenate([high, high, low], axis=0)))
        x = values[0] + (lx[r][0] + bias)
        t = values[1] + lt[r][0]
        out, out_t = gelu_pair(x, t)
        out_ref[0, r] = out
        out_t_ref[0, r] = out_t


def inverse(own, got, bias, phi_table, z_table, local_x, local_t, n_phi, width):
    channels, z_local, phi_local = local_x[0].shape
    cycles = len(local_x)
    lead = own.shape[:-4]
    block = pl.BlockSpec(lead + (1,) + own.shape[-3:], lambda o: (0,) * len(lead) + (o, 0, 0, 0))
    local_block = pl.BlockSpec((1, z_local, phi_local), lambda o: (o, 0, 0))
    out = jax.ShapeDtypeStruct((channels, cycles, z_local, phi_local), f32)
    out_block = pl.BlockSpec((1, cycles, z_local, phi_local), lambda o: (o, 0, 0, 0))
    size = channels * cycles * z_local * phi_local
    return pl.pallas_call(
        functools.partial(inverse_kernel, n_phi=n_phi, width=width),
        grid=(channels,),
        in_specs=[
            block,
            block,
            pl.BlockSpec(memory_space=pltpu.SMEM),
            pl.BlockSpec(phi_table.shape, lambda o: (0, 0)),
            pl.BlockSpec(z_table.shape, lambda o: (0, 0)),
        ]
        + [local_block] * (2 * cycles),
        out_specs=[out_block, out_block],
        out_shape=[out, out],
        compiler_params=pltpu.CompilerParams(vmem_limit_bytes=VMEM_LIMIT),
        cost_estimate=pl.CostEstimate(
            flops=1600 * size, bytes_accessed=16 * size, transcendentals=size
        ),
        name="inverse_transform",
    )(own, got, bias, phi_table, z_table, *local_x, *local_t)


def swap(x, axis, bit):
    count = lax.axis_size(axis)
    return lax.ppermute(x, axis, [(i, i ^ bit) for i in range(count)])


def reduce_scatter(keep, send, n_phi, n_gz):
    got = swap(send, "phi", 1)
    half = keep.shape[2] // 2
    total = keep + got
    a, b = total[:, :, :half], total[:, :, half:]
    a_got = swap(a[1], "phi", 2)
    b_got = swap(b[:, n_gz // 2 :], "gz", 1)
    a = a[0] + a_got
    b = b[:, : n_gz // 2] + b_got
    a_got = swap(a[n_gz // 2 :], "gz", 1)
    b_got = swap(b[1], "phi", 2)
    a = a[: n_gz // 2] + a_got
    b = b[0] + b_got
    v = jnp.concatenate([a, b], axis=1)
    bit = 2
    while bit < n_gz:
        middle = v.shape[0] // 2
        v = v[:middle] + swap(v[middle:], "gz", bit)
        bit *= 2
    return v[0]


def all_gather(v, n_phi, n_gz):
    v = v[None]
    bit = n_gz // 2
    while bit > 1:
        v = jnp.concatenate([v, swap(v, "gz", bit)], axis=0)
        bit //= 2
    half = v.shape[1] // 2
    a, b = v[None, :, :half], v[None, :, half:]
    a_got = swap(a, "gz", 1)
    b_got = swap(b, "phi", 2)
    a = jnp.concatenate([a, a_got], axis=1)
    b = jnp.concatenate([b, b_got], axis=0)
    a_got = swap(a, "phi", 2)
    b_got = swap(b, "gz", 1)
    a = jnp.concatenate([a, a_got], axis=0)
    b = jnp.concatenate([b, b_got], axis=1)
    own = jnp.concatenate([a, b], axis=2)
    return own, swap(own, "phi", 1)


def gz_order(n_gz):
    bits = n_gz.bit_length() - 1
    return [
        sum(digit << i for i, digit in enumerate(digits))
        for digits in itertools.product((0, 1), repeat=bits)
    ]


def body(field, field_tangent, spectral_weight, local_weight, bias_term, z_modes, phi_modes):
    channels, cycles, z_local, phi_local = field.shape
    n_gz = lax.axis_size("gz")
    n_phi = lax.axis_size("phi")
    z_total = z_local * n_gz
    phi_total = phi_local * n_phi
    kz = z_modes.shape[0]
    kp = phi_modes.shape[0]
    width = kp // n_phi
    my_gz = lax.axis_index("gz")
    my_phi = lax.axis_index("phi")

    z_global = my_gz * z_local + jnp.arange(z_local, dtype=jnp.int32)
    phi_global = my_phi * phi_local + jnp.arange(phi_local, dtype=jnp.int32)
    z_kept = z_modes.reshape(n_gz, -1)[my_gz ^ jnp.array(gz_order(n_gz), jnp.int32)].reshape(-1)
    phi_kept = phi_modes.reshape(n_phi, -1)[my_phi ^ jnp.arange(n_phi, dtype=jnp.int32)].reshape(-1)
    zc, zs = angles(z_global, z_kept, z_total)
    pc, ps = angles(phi_global, phi_kept, phi_total)

    high, low = split(jnp.concatenate([pc, -ps], axis=1))
    phi_table = jnp.concatenate(
        [jnp.concatenate([high, low], 1), jnp.concatenate([high, jnp.zeros_like(low)], 1)], 0
    )
    high, low = split(jnp.concatenate([zc, zs], axis=1).T)
    z_table = jnp.concatenate([high, low], 0)
    high, low = split(jnp.concatenate([zc, -zs], axis=1))
    z_back = jnp.concatenate([high, low, high], 1)
    high, low = split(
        jnp.concatenate(
            [jnp.concatenate([pc.T, ps.T], 1), jnp.concatenate([-ps.T, pc.T], 1)], 0
        )
    )
    phi_back = jnp.concatenate([high, high, low], 0)

    high, low = split(jnp.kron(local_weight.T, jnp.eye(8, dtype=f32)))
    local_table = jnp.concatenate(
        [jnp.concatenate([high, high], 1), jnp.concatenate([low, low], 1)], 0
    )

    scale = (1.0 / math.sqrt(z_total * phi_total)) * (2.0 / math.sqrt(kz * kp))
    spread = jnp.tile(jnp.eye(width, dtype=f32), (1, 2 * n_phi)) * scale
    sign = jnp.where(jnp.arange(2 * kp) < kp, -1.0, 1.0).astype(f32)
    wide = jnp.dot(spectral_weight, spread, precision=lax.Precision.HIGHEST)
    wr, wi = wide[0], wide[1] * sign

    keep, send = forward(field, field_tangent, phi_table, z_table, n_phi, n_gz, width)
    spectrum = reduce_scatter(keep, send, n_phi, n_gz)
    local = [local_mix(field, field_tangent, local_table, r) for r in range(cycles)]
    mixed = mix(spectrum, wr, wi)
    own, got = all_gather(mixed, n_phi, n_gz)
    return inverse(
        own,
        got,
        bias_term,
        phi_back,
        z_back,
        [x for x, _ in local],
        [t for _, t in local],
        n_phi,
        width,
    )


def solution(mesh):
    return jax.shard_map(
        body,
        mesh=mesh,
        in_specs=(
            P(None, None, "gz", "phi"),
            P(None, None, "gz", "phi"),
            P(None, None, None, "gz", "phi"),
            P(),
            P(),
            P(),
            P(),
        ),
        out_specs=(P(None, None, "gz", "phi"), P(None, None, "gz", "phi")),
        check_vma=False,
    )
```

time: 816 us -> 225 us (0.28)
  waiting for transfers between devices: 419 us -> 53.2 us
  matrix products: 212 us -> 1.77 us
  Pallas kernels: 0 us -> 128 us
  other arithmetic: 71.6 us -> 11.8 us
  local copies, waits for them, and re-layouts: 63.7 us -> 8.57 us
  blocking collectives: 27.2 us -> 0 us
  starting transfers between devices: 0.59 us -> 18.6 us
  between operations: 14.4 us -> 0.92 us
    reduce_scatter x1 -> x0, waiting for transfers between devices: 285 us -> none  [body(): lax.psum_scatter(jnp.stack([real_part, imag_part], axis=1), 'gz', scatter...]
    dot_general x17 -> x1, matrix products: 212 us -> 1.77 us  [body(): wide = jnp.dot(spectral_weight, spread, precision=lax.Precision.HIGHEST)]
    pallas_call x0 -> x7, Pallas kernels: none -> 128 us  [the longest x1 50.2 us: forward(): pl.pallas_call(functools.partial(forward_kernel, n_phi=n_phi, width=width...]
    all_gather x1 -> x0, waiting for transfers between devices: 116 us -> none  [body(): piece = lax.all_gather(columns, 'gz', axis=0, tiled=True)]
    ppermute x0 -> x14, waiting for transfers between devices: none -> 53.2 us  [swap(): return lax.ppermute(x, axis, [(i, i ^ bit) for i in range(count)])]
    another operation x5 -> x0, other arithmetic: 37.3 us -> none  [the longest x1 23.5 us: body(): stacked = jnp.stack([field, field_tangent])]
    add_any x1 -> x0, other arithmetic: 33.8 us -> none  [body(): jax.jvp(functools.partial(jax.nn.gelu, approximate=True), (preact,), (tan...]
    dot_general x1 -> x0, local copies, waits for them, and re-layouts: 30.9 us -> none  [body(): jnp.einsum('pcrzf,co->porzf', stacked, local_weight, precision=precise)]
  transfers between devices with their start and end apart: 3 -> 14, of which waited for: 3 -> 12; matrix products, arithmetic and copies ran while one was open for 14% -> 4% of each run, Pallas kernels for 0% -> 19%
where the time goes in v1:
time: 225 us; the launch traced here: 223 us
  Pallas kernels  128 us (57%)
  waiting for transfers between devices  53.2 us (24%)
  starting transfers between devices  18.6 us (8%)
  other arithmetic  11.8 us (5%)
  local copies, waits for them, and re-layouts  8.57 us (4%)
    ppermute x14, waiting for transfers between devices, swap(): return lax.ppermute(x, axis, [(i, i ^ bit) for i in range(count)])  53.2 us
    pallas_call x1, Pallas kernels, forward(): pl.pallas_call(functools.partial(forward_kernel, n_phi=n_phi, width=width...  50.2 us
    pallas_call x4, Pallas kernels, local_mix(): pl.pallas_call(local_kernel, grid=(z_local // rows,), in_specs=[block, bl...  41.5 us
    pallas_call x1, Pallas kernels, inverse(): pl.pallas_call(functools.partial(inverse_kernel, n_phi=n_phi, width=width...  33.9 us
    ppermute x14, starting transfers between devices, swap(): return lax.ppermute(x, axis, [(i, i ^ bit) for i in range(count)])  18.6 us
  transfers between devices with their start and end apart: 14, of which 12 were waited for; matrix products, arithmetic and copies ran while one was open for 4% of the time, Pallas kernels for 19%

profile of v1, /device:TPU:0, one launch (start us, length us, event | category | flops | bytes accessed | tf_op | source)
XLA Modules:
  0.0 222.9 jit_solution(1491617570453553314)
XLA Ops:
  0.7 0.8 compare_select_fusion
  1.5 0.7 reshape.68
  2.2 0.6 gather_fusion
  2.8 0.1 mul.106
  2.9 0.7 reshape.69
  3.6 0.6 gather_fusion.1
  4.2 0.1 mul.113
  4.3 0.6 fusion.25
  4.9 0.1 reduce-precision_convert_fusion.2
  5.0 0.8 copy.14.z_ref
  5.8 0.6 fusion.24
  6.4 0.1 fusion.8
  6.5 0.7 fusion.4.phi_ref
  7.2 50.2 %forward_transform.1 = (f32[2,8,16,2,8,128]{5,4,3,2,1,0:T(8,128)}, f32[2,8,16,2,8,128]{5,4,3,2,1,0:T(8,128)}) custom-call(f32[16,4,256,256]{3,2,1,0:T(8,128)} %x_ref.9, f32[16,4,256,256]{3,2,1,0:T(8,128)} %t_ref.9, bf16[512,256]{1,0:T(8,128)(2,1)} %fusion.4.phi_ref, bf16[256,256]{1,0:T(8,128)(2,1)} %copy.14.z_ref), custom_call_target="tpu_custom_call" | custom-call | flops 12884901888 | bytes 33554432 | tf_op jit(solution)/shard_map/forward_transform/pallas_call | solution.py:91
  57.3 0.5 collective-permute-start
  57.8 4.0 %collective-permute-done = f32[2,8,16,2,8,128]{5,4,3,2,1,0:T(8,128)S(1)} collective-permute-done((f32[2,8,16,2,8,128]{5,4,3,2,1,0:T(8,128)}, f32[2,8,16,2,8,128]{5,4,3,2,1,0:T(8,128)S(1)}, u32[]{:S(2)}, u32[]{:S(2)}) %collective-permute-start) | collective-permute-done | bytes 2097184 | tf_op jit(solution)/shard_map/ppermute | solution.py:236
  61.8 2.0 add.78
  63.8 1.3 copy-done.2
  65.1 0.8 slice_bitcast_fusion.2
  66.0 2.9 %collective-permute-start.1 = (f32[8,8,2,8,128]{4,3,2,1,0:T(8,128)}, f32[8,8,2,8,128]{4,3,2,1,0:T(8,128)S(1)}, u32[]{:S(2)}, u32[]{:S(2)}) collective-permute-start(f32[8,8,2,8,128]{4,3,2,1,0:T(8,128)} %slice_bitcast_fusion.2), channel_id=1, source_target_pairs={{0,2},{1,3},{2,0},{3,1},{4,6},{5,7},{6,4},{7,5},{8,10},{9,11},{10,... | collective-permute-start | bytes 1572872 | tf_op jit(solution)/shard_map/ppermute | solution.py:236
  68.9 0.1 reshape.87
  68.9 1.1 slice.79
  70.0 1.6 collective-permute-start.3
  71.6 1.8 convolution_bitcast_fusion
  73.4 7.9 %collective-permute-done.1 = f32[8,8,2,8,128]{4,3,2,1,0:T(8,128)S(1)} collective-permute-done((f32[8,8,2,8,128]{4,3,2,1,0:T(8,128)}, f32[8,8,2,8,128]{4,3,2,1,0:T(8,128)S(1)}, u32[]{:S(2)}, u32[]{:S(2)}) %collective-permute-start.1) | collective-permute-done | bytes 524320 | tf_op jit(solution)/shard_map/ppermute | solution.py:236
  81.4 1.8 collective-permute-start.2
  83.2 0.6 collective-permute-done.3
  84.0 0.9 collective-permute-start.4
  84.9 4.5 %collective-permute-done.2 = f32[4,8,2,8,128]{4,3,2,1,0:T(8,128)S(1)} collective-permute-done((f32[4,8,2,8,128]{4,3,2,1,0:T(8,128)S(1)}, f32[4,8,2,8,128]{4,3,2,1,0:T(8,128)S(1)}, u32[]{:S(2)}, u32[]{:S(2)}) %collective-permute-start.2) | collective-permute-done | bytes 262176 | tf_op jit(solution)/shard_map/ppermute | solution.py:236
  89.4 1.7 collective-permute-done.4
  91.2 1.6 collective-permute-start.5
  92.9 1.1 fusion.wi_ref
  93.9 3.7 %collective-permute-done.5 = f32[2,16,2,8,128]{4,3,2,1,0:T(8,128)S(1)} collective-permute-done((f32[2,16,2,8,128]{4,3,2,1,0:T(8,128)S(1)}, f32[2,16,2,8,128]{4,3,2,1,0:T(8,128)S(1)}, u32[]{:S(2)}, u32[]{:S(2)}) %collective-permute-start.5) | collective-permute-done | bytes 262176 | tf_op jit(solution)/shard_map/ppermute | solution.py:236
  97.7 3.2 %collective-permute-start.6 = (f32[1,16,2,8,128]{4,3,2,1,0:T(8,128)S(1)}, f32[1,16,2,8,128]{4,3,2,1,0:T(8,128)S(1)}, u32[]{:S(2)}, u32[]{:S(2)}) collective-permute-start(f32[1,16,2,8,128]{4,3,2,1,0:T(8,128)S(1)} %slice.85), channel_id=1, source_target_pairs={{0,16},{4,20},{8,24},{12,28},{16,0},{20,4},{24,8},{28,12},{1,17},{... | collective-permute-start | bytes 393224 | tf_op jit(solution)/shard_map/ppermute | solution.py:236
  100.9 1.0 slice_bitcast_fusion.1.wr_ref
  102.0 3.3 %collective-permute-done.6 = f32[1,16,2,8,128]{4,3,2,1,0:T(8,128)S(1)} collective-permute-done((f32[1,16,2,8,128]{4,3,2,1,0:T(8,128)S(1)}, f32[1,16,2,8,128]{4,3,2,1,0:T(8,128)S(1)}, u32[]{:S(2)}, u32[]{:S(2)}) %collective-permute-start.6) | collective-permute-done | bytes 131104 | tf_op jit(solution)/shard_map/ppermute | solution.py:236
  105.3 0.7 fusion.17.s_ref
  105.9 2.6 %mode_mix.1 = f32[16,2,8,128]{3,2,1,0:T(8,128)} custom-call(f32[16,2,8,128]{3,2,1,0:T(8,128)} %fusion.17.s_ref, f32[16,16,8,128]{3,2,1,0:T(8,128)} %slice_bitcast_fusion.1.wr_ref, f32[16,16,8,128]{3,2,1,0:T(8,128)} %fusion.wi_ref), custom_call_target="tpu_custom_call" | custom-call | tf_op jit(solution)/shard_map/mode_mix/pallas_call | solution.py:154
  108.5 1.6 collective-permute-start.7
  110.1 6.0 %collective-permute-done.7 = f32[1,16,2,8,128]{4,3,2,1,0:T(8,128)S(1)} collective-permute-done((f32[1,16,2,8,128]{4,3,2,1,0:T(8,128)}, f32[1,16,2,8,128]{4,3,2,1,0:T(8,128)S(1)}, u32[]{:S(2)}, u32[]{:S(2)}) %collective-permute-start.7) | collective-permute-done | bytes 131104 | tf_op jit(solution)/shard_map/ppermute | solution.py:236
  116.1 0.9 pad_maximum_fusion.5
  117.0 0.4 collective-permute-start.8
  117.4 6.0 %collective-permute-done.8 = f32[2,16,2,8,128]{4,3,2,1,0:T(8,128)S(1)} collective-permute-done((f32[2,16,2,8,128]{4,3,2,1,0:T(8,128)S(1)}, f32[2,16,2,8,128]{4,3,2,1,0:T(8,128)S(1)}, u32[]{:S(2)}, u32[]{:S(2)}) %collective-permute-start.8) | collective-permute-done | bytes 262176 | tf_op jit(solution)/shard_map/ppermute | solution.py:236
  123.5 0.9 pad_maximum_fusion
  124.5 1.6 collective-permute-start.9
  126.0 0.4 collective-permute-start.11
  126.5 7.3 %collective-permute-done.9 = f32[1,4,8,2,8,128]{5,4,3,2,1,0:T(8,128)S(1)} collective-permute-done((f32[1,4,8,2,8,128]{5,4,3,2,1,0:T(8,128)S(1)}, f32[1,4,8,2,8,128]{5,4,3,2,1,0:T(8,128)S(1)}, u32[]{:S(2)}, u32[]{:S(2)}) %collective-permute-start.9) | collective-permute-done | bytes 262176 | tf_op jit(solution)/shard_map/ppermute | solution.py:236
  133.8 0.9 collective-permute-start.10
  134.7 1.2 collective-permute-start.12
  135.9 7.2 %collective-permute-done.10 = f32[1,8,8,2,8,128]{5,4,3,2,1,0:T(8,128)S(1)} collective-permute-done((f32[1,8,8,2,8,128]{5,4,3,2,1,0:T(8,128)S(1)}, f32[1,8,8,2,8,128]{5,4,3,2,1,0:T(8,128)S(1)}, u32[]{:S(2)}, u32[]{:S(2)}) %collective-permute-start.10) | collective-permute-done | bytes 524320 | tf_op jit(solution)/shard_map/ppermute | solution.py:236
  143.0 0.9 collective-permute-done.12
  144.0 0.1 maximum_maximum_fusion.own_ref
  144.3 0.1 broadcast_multiply_fusion
  144.4 0.5 mul.131
  145.0 0.7 maximum_maximum_fusion.2.w_ref
  145.6 10.3 %local_mix.7 = (f32[16,256,256]{2,1,0:T(8,128)}, f32[16,256,256]{2,1,0:T(8,128)}) custom-call(f32[16,4,256,256]{3,2,1,0:T(8,128)} %x_ref.9, f32[16,4,256,256]{3,2,1,0:T(8,128)} %t_ref.9, bf16[256,256]{1,0:T(8,128)(2,1)} %maximum_maximum_fusion.2.w_ref), custom_call_target="tpu_custom_call" | custom-call | flops 1073741824 | bytes 16777216 | tf_op jit(solution)/shard_map/local_mix/pallas_call | solution.py:130
  156.0 10.4 %local_mix.6 = (f32[16,256,256]{2,1,0:T(8,128)}, f32[16,256,256]{2,1,0:T(8,128)}) custom-call(f32[16,4,256,256]{3,2,1,0:T(8,128)} %x_ref.9, f32[16,4,256,256]{3,2,1,0:T(8,128)} %t_ref.9, bf16[256,256]{1,0:T(8,128)(2,1)} %maximum_maximum_fusion.2.w_ref), custom_call_target="tpu_custom_call" | custom-call | flops 1073741824 | bytes 16777216 | tf_op jit(solution)/shard_map/local_mix/pallas_call | solution.py:130
  166.3 10.4 %local_mix.5 = (f32[16,256,256]{2,1,0:T(8,128)}, f32[16,256,256]{2,1,0:T(8,128)}) custom-call(f32[16,4,256,256]{3,2,1,0:T(8,128)} %x_ref.9, f32[16,4,256,256]{3,2,1,0:T(8,128)} %t_ref.9, bf16[256,256]{1,0:T(8,128)(2,1)} %maximum_maximum_fusion.2.w_ref), custom_call_target="tpu_custom_call" | custom-call | flops 1073741824 | bytes 16777216 | tf_op jit(solution)/shard_map/local_mix/pallas_call | solution.py:130
  176.7 10.4 %local_mix.4 = (f32[16,256,256]{2,1,0:T(8,128)}, f32[16,256,256]{2,1,0:T(8,128)}) custom-call(f32[16,4,256,256]{3,2,1,0:T(8,128)} %x_ref.9, f32[16,4,256,256]{3,2,1,0:T(8,128)} %t_ref.9, bf16[256,256]{1,0:T(8,128)(2,1)} %maximum_maximum_fusion.2.w_ref), custom_call_target="tpu_custom_call" | custom-call | flops 1073741824 | bytes 16777216 | tf_op jit(solution)/shard_map/local_mix/pallas_call | solution.py:130
  187.1 0.1 fusion.10
  187.2 0.7 pad_maximum_fusion.6.z_ref
  187.9 0.3 fusion.26
  188.3 0.8 pad_maximum_fusion.3.phi_ref
  189.0 33.9 %inverse_transform.1 = (f32[16,4,256,256]{3,2,1,0:T(8,128)}, f32[16,4,256,256]{3,2,1,0:T(8,128)}) custom-call(f32[2,8,16,2,8,128]{5,4,3,2,1,0:T(8,128)} %copy-done.4, f32[2,8,16,2,8,128]{5,4,3,2,1,0:T(8,128)} %collective-permute-done.13.got_ref, f32[16]{0:T(128)} %bias_ref.1, bf16[384,512]{1,0:T(8,128)(2,1)} %pad_maximum_fusion.3.phi_ref, ...), custom_call_target="tpu_custom_call" | custom-call | flops 6710886400 | bytes 67108864 | tf_op jit(solution)/shard_map/inverse_transform/pallas_call | solution.py:213
  (39 shorter events, 0.7 us)
Async XLA Ops:
  0.6 71.0 %copy-start = (f32[2,16,16,8,16]{4,3,2,1,0:T(8,128)S(1)}, f32[2,16,16,8,16]{4,3,2,1,0:T(8,128)}, u32[]{:S(2)}) copy-start(f32[2,16,16,8,16]{4,3,2,1,0:T(8,128)} %param.10) | copy-start | bytes 786436
  57.3 4.4 %collective-permute-start = (f32[2,8,16,2,8,128]{5,4,3,2,1,0:T(8,128)}, f32[2,8,16,2,8,128]{5,4,3,2,1,0:T(8,128)S(1)}, u32[]{:S(2)}, u32[]{:S(2)}) collective-permute-start(f32[2,8,16,2,8,128]{5,4,3,2,1,0:T(8,128)} %get-tuple-element.13), channel_id=1, source_target_pairs={{0,1},{1,0},{2,3},{3,2},{4,5},{5,4},{6,7},{7,6},{8,9},{9,8},{10,11... | collective-permute-start | bytes 6291464 | tf_op jit(solution)/shard_map/ppermute | solution.py:236
  63.8 1.3 copy-start.2
  66.0 15.3 %collective-permute-start.1 = (f32[8,8,2,8,128]{4,3,2,1,0:T(8,128)}, f32[8,8,2,8,128]{4,3,2,1,0:T(8,128)S(1)}, u32[]{:S(2)}, u32[]{:S(2)}) collective-permute-start(f32[8,8,2,8,128]{4,3,2,1,0:T(8,128)} %slice_bitcast_fusion.2), channel_id=1, source_target_pairs={{0,2},{1,3},{2,0},{3,1},{4,6},{5,7},{6,4},{7,5},{8,10},{9,11},{10,... | collective-permute-start | bytes 1572872 | tf_op jit(solution)/shard_map/ppermute | solution.py:236
  70.0 11.2 %copy-start.3 = (f32[2,8,16,2,8,128]{5,4,3,2,1,0:T(8,128)S(1)}, f32[2,8,16,2,8,128]{5,4,3,2,1,0:T(8,128)}, u32[]{:S(2)}) copy-start(f32[2,8,16,2,8,128]{5,4,3,2,1,0:T(8,128)} %copy-done.2) | copy-start | bytes 6291460
  70.0 13.8 %collective-permute-start.3 = (f32[2,4,8,2,8,128]{5,4,3,2,1,0:T(8,128)S(1)}, f32[2,4,8,2,8,128]{5,4,3,2,1,0:T(8,128)S(1)}, u32[]{:S(2)}, u32[]{:S(2)}) collective-permute-start(f32[2,4,8,2,8,128]{5,4,3,2,1,0:T(8,128)S(1)} %slice.79), channel_id=1, source_target_pairs={{0,4},{4,0},{8,12},{12,8},{16,20},{20,16},{24,28},{28,24},{1,5},{5... | collective-permute-start | bytes 1572872 | tf_op jit(solution)/shard_map/ppermute | solution.py:236
  81.4 8.0 %collective-permute-start.2 = (f32[4,8,2,8,128]{4,3,2,1,0:T(8,128)S(1)}, f32[4,8,2,8,128]{4,3,2,1,0:T(8,128)S(1)}, u32[]{:S(2)}, u32[]{:S(2)}) collective-permute-start(f32[4,8,2,8,128]{4,3,2,1,0:T(8,128)S(1)} %slice.77), channel_id=1, source_target_pairs={{0,4},{4,0},{8,12},{12,8},{16,20},{20,16},{24,28},{28,24},{1,5},{5... | collective-permute-start | bytes 786440 | tf_op jit(solution)/shard_map/ppermute | solution.py:236
  84.0 7.2 %collective-permute-start.4 = (f32[4,8,2,8,128]{4,3,2,1,0:T(8,128)S(1)}, f32[4,8,2,8,128]{4,3,2,1,0:T(8,128)S(1)}, u32[]{:S(2)}, u32[]{:S(2)}) collective-permute-start(f32[4,8,2,8,128]{4,3,2,1,0:T(8,128)S(1)} %slice_bitcast_fusion.6), channel_id=1, source_target_pairs={{0,2},{1,3},{2,0},{3,1},{4,6},{5,7},{6,4},{7,5},{8,10},{9,11},{10,... | collective-permute-start | bytes 786440 | tf_op jit(solution)/shard_map/ppermute | solution.py:236
  91.2 6.4 %collective-permute-start.5 = (f32[2,16,2,8,128]{4,3,2,1,0:T(8,128)S(1)}, f32[2,16,2,8,128]{4,3,2,1,0:T(8,128)S(1)}, u32[]{:S(2)}, u32[]{:S(2)}) collective-permute-start(f32[2,16,2,8,128]{4,3,2,1,0:T(8,128)S(1)} %pad_maximum_fusion.4), channel_id=1, source_target_pairs={{0,8},{4,12},{8,0},{12,4},{16,24},{20,28},{24,16},{28,20},{1,9},{5... | collective-permute-start | bytes 786440 | tf_op jit(solution)/shard_map/ppermute | solution.py:236
  97.7 7.5 %collective-permute-start.6 = (f32[1,16,2,8,128]{4,3,2,1,0:T(8,128)S(1)}, f32[1,16,2,8,128]{4,3,2,1,0:T(8,128)S(1)}, u32[]{:S(2)}, u32[]{:S(2)}) collective-permute-start(f32[1,16,2,8,128]{4,3,2,1,0:T(8,128)S(1)} %slice.85), channel_id=1, source_target_pairs={{0,16},{4,20},{8,24},{12,28},{16,0},{20,4},{24,8},{28,12},{1,17},{... | collective-permute-start | bytes 393224 | tf_op jit(solution)/shard_map/ppermute | solution.py:236
  108.5 7.6 %collective-permute-start.7 = (f32[1,16,2,8,128]{4,3,2,1,0:T(8,128)}, f32[1,16,2,8,128]{4,3,2,1,0:T(8,128)S(1)}, u32[]{:S(2)}, u32[]{:S(2)}) collective-permute-start(f32[1,16,2,8,128]{4,3,2,1,0:T(8,128)} %bitcast.42), channel_id=1, source_target_pairs={{0,16},{4,20},{8,24},{12,28},{16,0},{20,4},{24,8},{28,12},{1,17},{... | collective-permute-start | bytes 393224 | tf_op jit(solution)/shard_map/ppermute | solution.py:236
  117.0 6.4 %collective-permute-start.8 = (f32[2,16,2,8,128]{4,3,2,1,0:T(8,128)S(1)}, f32[2,16,2,8,128]{4,3,2,1,0:T(8,128)S(1)}, u32[]{:S(2)}, u32[]{:S(2)}) collective-permute-start(f32[2,16,2,8,128]{4,3,2,1,0:T(8,128)S(1)} %pad_maximum_fusion.5), channel_id=1, source_target_pairs={{0,8},{4,12},{8,0},{12,4},{16,24},{20,28},{24,16},{28,20},{1,9},{5... | collective-permute-start | bytes 786440 | tf_op jit(solution)/shard_map/ppermute | solution.py:236
  124.5 9.3 %collective-permute-start.9 = (f32[1,4,8,2,8,128]{5,4,3,2,1,0:T(8,128)S(1)}, f32[1,4,8,2,8,128]{5,4,3,2,1,0:T(8,128)S(1)}, u32[]{:S(2)}, u32[]{:S(2)}) collective-permute-start(f32[1,4,8,2,8,128]{5,4,3,2,1,0:T(8,128)S(1)} %get-tuple-element.22), channel_id=1, source_target_pairs={{0,4},{4,0},{8,12},{12,8},{16,20},{20,16},{24,28},{28,24},{1,5},{5... | collective-permute-start | bytes 786440 | tf_op jit(solution)/shard_map/ppermute | solution.py:236
  126.0 8.6 %collective-permute-start.11 = (f32[1,4,8,2,8,128]{5,4,3,2,1,0:T(8,128)S(1)}, f32[1,4,8,2,8,128]{5,4,3,2,1,0:T(8,128)S(1)}, u32[]{:S(2)}, u32[]{:S(2)}) collective-permute-start(f32[1,4,8,2,8,128]{5,4,3,2,1,0:T(8,128)S(1)} %get-tuple-element.23), channel_id=1, source_target_pairs={{0,2},{1,3},{2,0},{3,1},{4,6},{5,7},{6,4},{7,5},{8,10},{9,11},{10,... | collective-permute-start | bytes 786440 | tf_op jit(solution)/shard_map/ppermute | solution.py:236
  133.8 9.2 %collective-permute-start.10 = (f32[1,8,8,2,8,128]{5,4,3,2,1,0:T(8,128)S(1)}, f32[1,8,8,2,8,128]{5,4,3,2,1,0:T(8,128)S(1)}, u32[]{:S(2)}, u32[]{:S(2)}) collective-permute-start(f32[1,8,8,2,8,128]{5,4,3,2,1,0:T(8,128)S(1)} %pad_maximum_fusion.1), channel_id=1, source_target_pairs={{0,2},{1,3},{2,0},{3,1},{4,6},{5,7},{6,4},{7,5},{8,10},{9,11},{10,... | collective-permute-start | bytes 1572872 | tf_op jit(solution)/shard_map/ppermute | solution.py:236
  134.7 9.5 %copy-start.5 = (f32[16,16]{1,0:T(8,128)S(1)}, f32[16,16]{1,0:T(8,128)}, u32[]{:S(2)}) copy-start(f32[16,16]{1,0:T(8,128)} %param.11) | copy-start | bytes 3076
  134.7 9.2 %collective-permute-start.12 = (f32[2,4,8,2,8,128]{5,4,3,2,1,0:T(8,128)S(1)}, f32[2,4,8,2,8,128]{5,4,3,2,1,0:T(8,128)S(1)}, u32[]{:S(2)}, u32[]{:S(2)}) collective-permute-start(f32[2,4,8,2,8,128]{5,4,3,2,1,0:T(8,128)S(1)} %pad_maximum_fusion.2), channel_id=1, source_target_pairs={{0,4},{4,0},{8,12},{12,8},{16,20},{20,16},{24,28},{28,24},{1,5},{5... | collective-permute-start | bytes 1572872 | tf_op jit(solution)/shard_map/ppermute | solution.py:236
  144.1 11.8 %copy-start.4 = (f32[2,8,16,2,8,128]{5,4,3,2,1,0:T(8,128)}, f32[2,8,16,2,8,128]{5,4,3,2,1,0:T(8,128)S(1)}, u32[]{:S(2)}) copy-start(f32[2,8,16,2,8,128]{5,4,3,2,1,0:T(8,128)S(1)} %maximum_maximum_fusion.own_ref) | copy-start | bytes 6291460
  144.1 44.9 %collective-permute-start.13 = (f32[2,8,16,2,8,128]{5,4,3,2,1,0:T(8,128)S(1)}, f32[2,8,16,2,8,128]{5,4,3,2,1,0:T(8,128)}, u32[]{:S(2)}, u32[]{:S(2)}) collective-permute-start(f32[2,8,16,2,8,128]{5,4,3,2,1,0:T(8,128)S(1)} %maximum_maximum_fusion.own_ref), channel_id=1, source_target_pairs={{0,1},{1,0},{2,3},{3,2},{4,5},{5,4},{6,7},{7,6},{8,9},{9,8},{10,11... | collective-permute-start | bytes 6291464 | tf_op jit(solution)/shard_map/ppermute | solution.py:236
  189.0 33.9 %copy-start.1 = (f32[2,16,16,8,16]{4,3,2,1,0:T(8,128)S(1)}, f32[2,16,16,8,16]{4,3,2,1,0:T(8,128)}, u32[]{:S(2)}) copy-start(f32[2,16,16,8,16]{4,3,2,1,0:T(8,128)} %param.10) | copy-start | bytes 786436

commit v2 on v1

--- a/solution.py
+++ b/solution.py
@@ -54,28 +54,46 @@
 
 
 def forward_kernel(x_ref, t_ref, phi_ref, z_ref, keep_ref, send_ref, *, n_phi, width):
-    cycles, z_local, _ = x_ref.shape[1:]
+    block, cycles, z_local, phi_local = x_ref.shape
     modes2 = z_ref.shape[0] // 2
     modes = modes2 // 2
     lanes = phi_ref.shape[1] // 2
+    shape = keep_ref.shape[1:-4] + keep_ref.shape[-2:]
     lane = lax.broadcasted_iota(jnp.int32, (modes, lanes), 1)
     sign = jnp.where(lane < lanes // 2, 1.0, -1.0).astype(f32)
-    batch = [(ref, r) for ref in (x_ref, t_ref) for r in range(cycles)]
-    for group in range(len(batch) // n_phi):
+
+    def along_phi(c, part):
+        x = (x_ref, t_ref)[part][c].reshape(cycles * z_local, phi_local)
+        high, low = halves(x)
+        y = dot(jnp.concatenate([high, low], axis=1), phi_ref[...])
+        high, low = halves(y[:, :lanes] + y[:, lanes:])
+        return jnp.concatenate([high, low], axis=1)
+
+    def along_z(y):
+        return [dot(z_ref[...], y[r * z_local : (r + 1) * z_local]) for r in range(cycles)]
+
+    def finish(c, products):
         items = []
-        for ref, r in batch[group * n_phi : (group + 1) * n_phi]:
-            high, low = halves(ref[0, r])
-            y = dot(jnp.concatenate([high, low], axis=1), phi_ref[...])
-            y = y[:, :lanes] + y[:, lanes:]
-            y_high, y_low = halves(y)
-            m = dot(z_ref[...], jnp.concatenate([y_high, y_low], axis=1))
+        for m in products:
             m = m[:modes2, :lanes] + (m[:modes2, lanes:] + m[modes2:, :lanes])
             items.append(m[:modes] + sign * pltpu.roll(m[modes:], lanes // 2, 1))
-        items = exchange(items, width)
-        shape = keep_ref.shape[1:-4] + keep_ref.shape[-2:]
-        for slot, item in enumerate(items):
-            out = keep_ref if slot % 2 == 0 else send_ref
-            out[slot // 2, ..., 0, group, :, :] = item.reshape(shape)
+        for group in range(len(items) // n_phi):
+            part = exchange(items[group * n_phi : (group + 1) * n_phi], width)
+            for slot, item in enumerate(part):
+                out = keep_ref if slot % 2 == 0 else send_ref
+                out[slot // 2, ..., c, group, :, :] = item.reshape(shape)
+
+    steps = [(c, part) for c in range(block) for part in range(2)]
+    ahead = along_phi(*steps[0])
+    products = []
+    for i, (c, part) in enumerate(steps):
+        y = ahead
+        if i + 1 < len(steps):
+            ahead = along_phi(*steps[i + 1])
+        products.append(along_z(y))
+        if part == 0 and c:
+            finish(c - 1, products[-3] + products[-2])
+    finish(block - 1, products[-2] + products[-1])
 
 
 def forward(field, tangent, phi_table, z_table, n_phi, n_gz, width):
@@ -84,13 +102,14 @@
     modes = z_table.shape[0] // 4
     lanes = phi_table.shape[1] // 2
     out = jax.ShapeDtypeStruct((n_phi // 2, n_gz, channels, groups, modes // n_gz, lanes), f32)
-    block = pl.BlockSpec((1, cycles, z_local, phi_local), lambda c: (c, 0, 0, 0))
+    step = 4
+    block = pl.BlockSpec((step, cycles, z_local, phi_local), lambda c: (c, 0, 0, 0))
     out_block = pl.BlockSpec(
-        (n_phi // 2, n_gz, 1, groups, modes // n_gz, lanes), lambda c: (0, 0, c, 0, 0, 0)
+        (n_phi // 2, n_gz, step, groups, modes // n_gz, lanes), lambda c: (0, 0, c, 0, 0, 0)
     )
     return pl.pallas_call(
         functools.partial(forward_kernel, n_phi=n_phi, width=width),
-        grid=(channels,),
+        grid=(channels // step,),
         in_specs=[
             block,
             block,
@@ -111,25 +130,31 @@
 
 def local_kernel(x_ref, t_ref, w_ref, xo_ref, to_ref):
     channels, _, rows, columns = x_ref.shape
-    for ref, out in ((x_ref, xo_ref), (t_ref, to_ref)):
-        for start in range(0, rows, 8):
-            x = ref[:, 0, start : start + 8, :].reshape(channels * 8, columns)
-            high, low = halves(x)
-            mixed = dot(w_ref[...], jnp.concatenate([high, low], axis=0))
-            mixed = mixed[: channels * 8] + mixed[channels * 8 :]
-            out[:, start : start + 8, :] = mixed.reshape(channels, 8, columns)
-
-
-def local_mix(field, tangent, weight, cycle):
+    tiles = [
+        (ref, out, start) for ref, out in ((x_ref, xo_ref), (t_ref, to_ref)) for start in range(0, rows, 8)
+    ]
+    for at in range(0, len(tiles), 4):
+        products = []
+        for ref, _, start in tiles[at : at + 4]:
+            high, low = halves(ref[:, 0, start : start + 8, :].reshape(channels * 8, columns))
+            products.append(dot(w_ref[...], jnp.concatenate([high, low], axis=0)))
+        for (_, out, start), m in zip(tiles[at : at + 4], products):
+            m = m[: channels * 8] + m[channels * 8 :]
+            out[:, start : start + 8, :] = m.reshape(channels, 8, columns)
+
+
+def local_mix(field, tangent, weight, cycle, part, parts):
     channels, _, z_local, phi_local = field.shape
-    rows = 32
-    out = jax.ShapeDtypeStruct((channels, z_local, phi_local), f32)
-    block = pl.BlockSpec((channels, 1, rows, phi_local), lambda z: (0, cycle, z, 0))
+    span = z_local // parts
+    rows = min(64, span)
+    steps = span // rows
+    out = jax.ShapeDtypeStruct((channels, span, phi_local), f32)
+    block = pl.BlockSpec((channels, 1, rows, phi_local), lambda z: (0, cycle, part * steps + z, 0))
     out_block = pl.BlockSpec((channels, rows, phi_local), lambda z: (0, z, 0))
-    size = channels * z_local * phi_local
+    size = channels * span * phi_local
     return pl.pallas_call(
         local_kernel,
-        grid=(z_local // rows,),
+        grid=(steps,),
         in_specs=[block, block, pl.BlockSpec(weight.shape, lambda z: (0, 0))],
         out_specs=[out_block, out_block],
         out_shape=[out, out],
@@ -170,49 +195,50 @@
 
 
 def inverse_kernel(own_ref, got_ref, bias_ref, phi_ref, z_ref, *refs, n_phi, width):
-    cycles = (len(refs) - 2) // 2
-    lx, lt = refs[:cycles], refs[cycles : 2 * cycles]
-    out_ref, out_t_ref = refs[2 * cycles :]
+    out_ref, out_t_ref = refs[-2:]
+    block, cycles, z_local, phi_local = out_ref.shape
+    parts = (len(refs) - 2) // (2 * cycles)
+    span = z_local // parts
     groups, _, lanes = own_ref.shape[-3:]
     modes = z_ref.shape[1] // 6
-    phi_local = phi_ref.shape[1] // 2
-    bias = bias_ref[pl.program_id(0)]
-    spectral = []
-    for group in range(groups):
-        items = [
-            (own_ref if slot % 2 == 0 else got_ref)[slot // 2, ..., 0, group, :, :].reshape(modes, lanes)
-            for slot in range(n_phi)
-        ]
-        g = jnp.concatenate(exchange(items, width), axis=0)
-        g_high, g_low = halves(g)
-        h = dot(jnp.concatenate([g_high, g_low, g_high], axis=1), phi_ref[...])
-        for b in range(n_phi):
-            part = h[b * modes : (b + 1) * modes]
-            part = jnp.concatenate([part[:, :phi_local], part[:, phi_local:]], axis=0)
-            spectral.append(halves(part))
-    for r in range(cycles):
-        values = []
-        for high, low in (spectral[r], spectral[cycles + r]):
-            values.append(dot(z_ref[...], jnp.concatenate([high, high, low], axis=0)))
-        x = values[0] + (lx[r][0] + bias)
-        t = values[1] + lt[r][0]
-        out, out_t = gelu_pair(x, t)
-        out_ref[0, r] = out
-        out_t_ref[0, r] = out_t
-
-
-def inverse(own, got, bias, phi_table, z_table, local_x, local_t, n_phi, width):
-    channels, z_local, phi_local = local_x[0].shape
-    cycles = len(local_x)
+    for c in range(block):
+        bias = bias_ref[pl.program_id(0) * block + c]
+        spectral = []
+        for group in range(groups):
+            items = [
+                (own_ref if slot % 2 == 0 else got_ref)[slot // 2, ..., c, group, :, :].reshape(modes, lanes)
+                for slot in range(n_phi)
+            ]
+            high, low = halves(jnp.concatenate(exchange(items, width), axis=0))
+            h = dot(jnp.concatenate([high, low, high], axis=1), phi_ref[...])
+            for b in range(n_phi):
+                part = h[b * modes : (b + 1) * modes]
+                part = jnp.concatenate([part[:, :phi_local], part[:, phi_local:]], axis=0)
+                high, low = halves(part)
+                spectral.append(jnp.concatenate([high, high, low], axis=0))
+        values = [dot(z_ref[...], part) for part in spectral]
+        for r in range(cycles):
+            for p in range(parts):
+                rows = slice(p * span, (p + 1) * span)
+                lx, lt = refs[2 * (r * parts + p) : 2 * (r * parts + p) + 2]
+                x = values[r][rows] + (lx[c] + bias)
+                t = values[cycles + r][rows] + lt[c]
+                out_ref[c, r, rows], out_t_ref[c, r, rows] = gelu_pair(x, t)
+
+
+def inverse(own, got, bias, phi_table, z_table, local, cycles, n_phi, width):
+    channels, span, phi_local = local[0].shape
+    z_local = span * len(local) // (2 * cycles)
     lead = own.shape[:-4]
-    block = pl.BlockSpec(lead + (1,) + own.shape[-3:], lambda o: (0,) * len(lead) + (o, 0, 0, 0))
-    local_block = pl.BlockSpec((1, z_local, phi_local), lambda o: (o, 0, 0))
+    step = 2
+    block = pl.BlockSpec(lead + (step,) + own.shape[-3:], lambda o: (0,) * len(lead) + (o, 0, 0, 0))
+    local_block = pl.BlockSpec((step, span, phi_local), lambda o: (o, 0, 0))
     out = jax.ShapeDtypeStruct((channels, cycles, z_local, phi_local), f32)
-    out_block = pl.BlockSpec((1, cycles, z_local, phi_local), lambda o: (o, 0, 0, 0))
+    out_block = pl.BlockSpec((step, cycles, z_local, phi_local), lambda o: (o, 0, 0, 0))
     size = channels * cycles * z_local * phi_local
     return pl.pallas_call(
         functools.partial(inverse_kernel, n_phi=n_phi, width=width),
-        grid=(channels,),
+        grid=(channels // step,),
         in_specs=[
             block,
             block,
@@ -220,7 +246,7 @@
             pl.BlockSpec(phi_table.shape, lambda o: (0, 0)),
             pl.BlockSpec(z_table.shape, lambda o: (0, 0)),
         ]
-        + [local_block] * (2 * cycles),
+        + [local_block] * len(local),
         out_specs=[out_block, out_block],
         out_shape=[out, out],
         compiler_params=pltpu.CompilerParams(vmem_limit_bytes=VMEM_LIMIT),
@@ -228,7 +254,7 @@
             flops=1600 * size, bytes_accessed=16 * size, transcendentals=size
         ),
         name="inverse_transform",
-    )(own, got, bias, phi_table, z_table, *local_x, *local_t)
+    )(own, got, bias, phi_table, z_table, *local)
 
 
 def swap(x, axis, bit):
@@ -236,42 +262,63 @@
     return lax.ppermute(x, axis, [(i, i ^ bit) for i in range(count)])
 
 
-def reduce_scatter(keep, send, n_phi, n_gz):
+class Filler:
+    def __init__(self, field, tangent, table, parts):
+        self.inputs = (field, tangent)
+        self.table = table
+        self.parts = parts
+        self.todo = [(r, p) for r in range(field.shape[1]) for p in range(parts)]
+        self.done = []
+
+    def beside(self, sent, got, count=1):
+        for _ in range(min(count, len(self.todo))):
+            r, p = self.todo.pop(0)
+            inputs, _ = lax.optimization_barrier((self.inputs, sent))
+            piece = local_mix(*inputs, self.table, r, p, self.parts)
+            got, piece = lax.optimization_barrier((got, piece))
+            self.done += piece
+        return got
+
+
+def reduce_scatter(keep, send, n_phi, n_gz, filler):
     got = swap(send, "phi", 1)
     half = keep.shape[2] // 2
     total = keep + got
     a, b = total[:, :, :half], total[:, :, half:]
-    a_got = swap(a[1], "phi", 2)
-    b_got = swap(b[:, n_gz // 2 :], "gz", 1)
+    sent = (a[1], b[:, n_gz // 2 :])
+    got = (swap(sent[0], "phi", 2), swap(sent[1], "gz", 1))
+    a_got, b_got = filler.beside(sent, got, 2)
     a = a[0] + a_got
     b = b[:, : n_gz // 2] + b_got
-    a_got = swap(a[n_gz // 2 :], "gz", 1)
-    b_got = swap(b[1], "phi", 2)
+    sent = (a[n_gz // 2 :], b[1])
+    got = (swap(sent[0], "gz", 1), swap(sent[1], "phi", 2))
+    a_got, b_got = filler.beside(sent, got)
     a = a[: n_gz // 2] + a_got
     b = b[0] + b_got
     v = jnp.concatenate([a, b], axis=1)
     bit = 2
     while bit < n_gz:
         middle = v.shape[0] // 2
-        v = v[:middle] + swap(v[middle:], "gz", bit)
+        sent = v[middle:]
+        v = v[:middle] + filler.beside(sent, swap(sent, "gz", bit))
         bit *= 2
     return v[0]
 
 
-def all_gather(v, n_phi, n_gz):
+def all_gather(v, n_phi, n_gz, filler):
     v = v[None]
     bit = n_gz // 2
     while bit > 1:
-        v = jnp.concatenate([v, swap(v, "gz", bit)], axis=0)
+        v = jnp.concatenate([v, filler.beside(v, swap(v, "gz", bit))], axis=0)
         bit //= 2
     half = v.shape[1] // 2
     a, b = v[None, :, :half], v[None, :, half:]
-    a_got = swap(a, "gz", 1)
-    b_got = swap(b, "phi", 2)
+    got = (swap(a, "gz", 1), swap(b, "phi", 2))
+    a_got, b_got = filler.beside((a, b), got)
     a = jnp.concatenate([a, a_got], axis=1)
     b = jnp.concatenate([b, b_got], axis=0)
-    a_got = swap(a, "phi", 2)
-    b_got = swap(b, "gz", 1)
+    got = (swap(a, "phi", 2), swap(b, "gz", 1))
+    a_got, b_got = filler.beside((a, b), got, len(filler.todo))
     a = jnp.concatenate([a, a_got], axis=0)
     b = jnp.concatenate([b, b_got], axis=1)
     own = jnp.concatenate([a, b], axis=2)
@@ -332,21 +379,11 @@
     wr, wi = wide[0], wide[1] * sign
 
     keep, send = forward(field, field_tangent, phi_table, z_table, n_phi, n_gz, width)
-    spectrum = reduce_scatter(keep, send, n_phi, n_gz)
-    local = [local_mix(field, field_tangent, local_table, r) for r in range(cycles)]
+    filler = Filler(field, field_tangent, local_table, 2)
+    spectrum = reduce_scatter(keep, send, n_phi, n_gz, filler)
     mixed = mix(spectrum, wr, wi)
-    own, got = all_gather(mixed, n_phi, n_gz)
-    return inverse(
-        own,
-        got,
-        bias_term,
-        phi_back,
-        z_back,
-        [x for x, _ in local],
-        [t for _, t in local],
-        n_phi,
-        width,
-    )
+    own, got = all_gather(mixed, n_phi, n_gz, filler)
+    return inverse(own, got, bias_term, phi_back, z_back, filler.done, cycles, n_phi, width)
 
 
 def solution(mesh):

time: 225 us -> 154 us (0.68)
  Pallas kernels: 128 us -> 88.5 us
  waiting for transfers between devices: 53.2 us -> 25.3 us
  starting transfers between devices: 18.6 us -> 14.7 us
    pallas_call x1, Pallas kernels: 50.2 us -> 19.6 us  [forward(): pl.pallas_call(functools.partial(forward_kernel, n_phi=n_phi, width=width...]
    ppermute x14, waiting for transfers between devices: 53.2 us -> 25.3 us  [swap(): return lax.ppermute(x, axis, [(i, i ^ bit) for i in range(count)])]
    pallas_call x4 -> x8, Pallas kernels: 41.5 us -> 35.6 us  [local_mix(): pl.pallas_call(local_kernel, grid=(steps,), in_specs=[block, block, pl.Bl...]
    ppermute x14, starting transfers between devices: 18.6 us -> 14.7 us  [swap(): return lax.ppermute(x, axis, [(i, i ^ bit) for i in range(count)])]
    pallas_call x1, Pallas kernels: 33.9 us -> 30.7 us  [inverse(): pl.pallas_call(functools.partial(inverse_kernel, n_phi=n_phi, width=width...]
  transfers between devices with their start and end apart: 14 -> 14, of which waited for: 12 -> 11; matrix products, arithmetic and copies ran while one was open for 4% -> 5% of each run, Pallas kernels for 19% -> 23%
where the time goes in v2:
time: 154 us; the launch traced here: 153 us
  Pallas kernels  88.5 us (57%)
  waiting for transfers between devices  25.3 us (16%)
  starting transfers between devices  14.7 us (10%)
  other arithmetic  12.9 us (8%)
  local copies, waits for them, and re-layouts  9.02 us (6%)
  matrix products  1.77 us (1%)
    pallas_call x8, Pallas kernels, local_mix(): pl.pallas_call(local_kernel, grid=(steps,), in_specs=[block, block, pl.Bl...  35.6 us
    pallas_call x1, Pallas kernels, inverse(): pl.pallas_call(functools.partial(inverse_kernel, n_phi=n_phi, width=width...  30.7 us
    ppermute x14, waiting for transfers between devices, swap(): return lax.ppermute(x, axis, [(i, i ^ bit) for i in range(count)])  25.3 us
    pallas_call x1, Pallas kernels, forward(): pl.pallas_call(functools.partial(forward_kernel, n_phi=n_phi, width=width...  19.6 us
    ppermute x14, starting transfers between devices, swap(): return lax.ppermute(x, axis, [(i, i ^ bit) for i in range(count)])  14.7 us
  transfers between devices with their start and end apart: 14, of which 11 were waited for; matrix products, arithmetic and copies ran while one was open for 5% of the time, Pallas kernels for 23%

profile of v2, /device:TPU:0, one launch (start us, length us, event | category | flops | bytes accessed | tf_op | source)
XLA Modules:
  0.0 153.2 jit_solution(6185313604230727355)
XLA Ops:
  0.7 0.8 compare_select_fusion
  1.5 0.7 reshape.68
  2.2 0.6 gather_fusion
  2.9 0.7 reshape.69
  3.6 0.6 gather_fusion.1
  4.3 0.6 fusion.25
  4.9 0.1 reduce-precision_convert_fusion.2
  5.0 0.8 copy.14.z_ref
  5.8 0.6 fusion.24
  6.4 0.1 fusion.8
  6.5 0.7 fusion.4.phi_ref
  7.2 19.6 %forward_transform.1 = (f32[2,8,16,2,8,128]{5,4,3,2,1,0:T(8,128)}, f32[2,8,16,2,8,128]{5,4,3,2,1,0:T(8,128)}) custom-call(f32[16,4,256,256]{3,2,1,0:T(8,128)} %x_ref.9, f32[16,4,256,256]{3,2,1,0:T(8,128)} %t_ref.9, bf16[512,256]{1,0:T(8,128)(2,1)} %fusion.4.phi_ref, bf16[256,256]{1,0:T(8,128)(2,1)} %copy.14.z_ref), custom_call_target="tpu_custom_call" | custom-call | flops 12884901888 | bytes 33554432 | tf_op jit(solution)/shard_map/forward_transform/pallas_call | solution.py:110
  26.8 0.5 collective-permute-start
  27.3 0.1 broadcast_multiply_fusion
  27.5 3.9 %collective-permute-done = f32[2,8,16,2,8,128]{5,4,3,2,1,0:T(8,128)} collective-permute-done((f32[2,8,16,2,8,128]{5,4,3,2,1,0:T(8,128)}, f32[2,8,16,2,8,128]{5,4,3,2,1,0:T(8,128)}, u32[]{:S(2)}, u32[]{:S(2)}) %collective-permute-start) | collective-permute-done | bytes 2097184 | tf_op jit(solution)/shard_map/ppermute | solution.py:262
  31.4 2.6 %add.78 = f32[2,8,16,2,8,128]{5,4,3,2,1,0:T(8,128)S(1)} add(f32[2,8,16,2,8,128]{5,4,3,2,1,0:T(8,128)} %get-tuple-element.62, f32[2,8,16,2,8,128]{5,4,3,2,1,0:T(8,128)} %collective-permute-done) | non-fusion elementwise | flops 524288 | bytes 6291456 | tf_op jit(solution)/shard_map/add | solution.py:286
  34.0 1.0 slice.76
  34.9 0.5 copy-done.2
  35.5 0.9 slice_bitcast_fusion.2
  36.3 2.9 %collective-permute-start.1 = (f32[8,8,2,8,128]{4,3,2,1,0:T(8,128)}, f32[8,8,2,8,128]{4,3,2,1,0:T(8,128)}, u32[]{:S(2)}, u32[]{:S(2)}) collective-permute-start(f32[8,8,2,8,128]{4,3,2,1,0:T(8,128)} %slice_bitcast_fusion.2), channel_id=1, source_target_pairs={{0,2},{1,3},{2,0},{3,1},{4,6},{5,7},{6,4},{7,5},{8,10},{9,11},{10,... | collective-permute-start | bytes 1572872 | tf_op jit(solution)/shard_map/ppermute | solution.py:262
  39.2 1.5 collective-permute-start.2
  40.8 0.5 mul.121
  41.3 0.7 maximum_maximum_fusion.2.w_ref
  42.0 4.4 %local_mix.9 = (f32[16,128,256]{2,1,0:T(8,128)}, f32[16,128,256]{2,1,0:T(8,128)}) custom-call(f32[16,4,256,256]{3,2,1,0:T(8,128)} %x_ref.9, f32[16,4,256,256]{3,2,1,0:T(8,128)} %t_ref.9, bf16[256,256]{1,0:T(8,128)(2,1)} %maximum_maximum_fusion.2.w_ref), custom_call_target="tpu_custom_call" | custom-call | flops 536870912 | bytes 8388608 | tf_op jit(solution)/shard_map/local_mix/pallas_call | solution.py:155
  46.4 4.5 %local_mix.8 = (f32[16,128,256]{2,1,0:T(8,128)}, f32[16,128,256]{2,1,0:T(8,128)}) custom-call(f32[16,4,256,256]{3,2,1,0:T(8,128)} %x_ref.9, f32[16,4,256,256]{3,2,1,0:T(8,128)} %t_ref.9, bf16[256,256]{1,0:T(8,128)(2,1)} %maximum_maximum_fusion.2.w_ref), custom_call_target="tpu_custom_call" | custom-call | flops 536870912 | bytes 8388608 | tf_op jit(solution)/shard_map/local_mix/pallas_call | solution.py:155
  50.9 0.8 collective-permute-done.1
  51.7 1.5 collective-permute-done.2
  53.2 1.1 fusion.1
  54.3 1.1 slice_add_fusion
  55.5 1.6 %collective-permute-start.3 = (f32[4,8,2,8,128]{4,3,2,1,0:T(8,128)S(1)}, f32[4,8,2,8,128]{4,3,2,1,0:T(8,128)S(1)}, u32[]{:S(2)}, u32[]{:S(2)}) collective-permute-start(f32[4,8,2,8,128]{4,3,2,1,0:T(8,128)S(1)} %slice.78), channel_id=1, source_target_pairs={{0,4},{4,0},{8,12},{12,8},{16,20},{20,16},{24,28},{28,24},{1,5},{5... | collective-permute-start | bytes 786440 | tf_op jit(solution)/shard_map/ppermute | solution.py:262
  57.0 0.5 collective-permute-start.4
  57.6 1.8 %convolution_bitcast_fusion = f32[2,16,16,8,128]{4,3,2,1,0:T(8,128)S(1)} fusion(f32[2,16,16,8,16]{4,3,2,1,0:T(8,128)S(1)} %copy-done, f32[16,128,1,1,1]{1,0,2,3,4:T(8,128)S(1)} %reshape.87), kind=kOutput, calls=%fused_computation.3 | convolution fusion | flops 100663296 | bytes 2367488 | tf_op jit(solution)/shard_map/dot_general | solution.py:378
  59.4 4.4 %local_mix.10 = (f32[16,128,256]{2,1,0:T(8,128)}, f32[16,128,256]{2,1,0:T(8,128)}) custom-call(f32[16,4,256,256]{3,2,1,0:T(8,128)} %x_ref.9, f32[16,4,256,256]{3,2,1,0:T(8,128)} %t_ref.9, bf16[256,256]{1,0:T(8,128)(2,1)} %maximum_maximum_fusion.2.w_ref), custom_call_target="tpu_custom_call" | custom-call | flops 536870912 | bytes 8388608 | tf_op jit(solution)/shard_map/local_mix/pallas_call | solution.py:155
  63.8 0.1 collective-permute-done.4
  64.1 1.6 %collective-permute-start.5 = (f32[2,16,2,8,128]{4,3,2,1,0:T(8,128)S(1)}, f32[2,16,2,8,128]{4,3,2,1,0:T(8,128)S(1)}, u32[]{:S(2)}, u32[]{:S(2)}) collective-permute-start(f32[2,16,2,8,128]{4,3,2,1,0:T(8,128)S(1)} %pad_maximum_fusion.4), channel_id=1, source_target_pairs={{0,8},{4,12},{8,0},{12,4},{16,24},{20,28},{24,16},{28,20},{1,9},{5... | collective-permute-start | bytes 786440 | tf_op jit(solution)/shard_map/ppermute | solution.py:262
  65.7 1.1 fusion.wi_ref
  66.8 4.4 %local_mix.11 = (f32[16,128,256]{2,1,0:T(8,128)}, f32[16,128,256]{2,1,0:T(8,128)}) custom-call(f32[16,4,256,256]{3,2,1,0:T(8,128)} %x_ref.9, f32[16,4,256,256]{3,2,1,0:T(8,128)} %t_ref.9, bf16[256,256]{1,0:T(8,128)(2,1)} %maximum_maximum_fusion.2.w_ref), custom_call_target="tpu_custom_call" | custom-call | flops 536870912 | bytes 8388608 | tf_op jit(solution)/shard_map/local_mix/pallas_call | solution.py:155
  71.3 2.7 %collective-permute-start.6 = (f32[1,16,2,8,128]{4,3,2,1,0:T(8,128)S(1)}, f32[1,16,2,8,128]{4,3,2,1,0:T(8,128)S(1)}, u32[]{:S(2)}, u32[]{:S(2)}) collective-permute-start(f32[1,16,2,8,128]{4,3,2,1,0:T(8,128)S(1)} %slice.85), channel_id=1, source_target_pairs={{0,16},{4,20},{8,24},{12,28},{16,0},{20,4},{24,8},{28,12},{1,17},{... | collective-permute-start | bytes 393224 | tf_op jit(solution)/shard_map/ppermute | solution.py:262
  73.9 1.1 slice_bitcast_fusion.1.wr_ref
  75.0 4.4 %local_mix.12 = (f32[16,128,256]{2,1,0:T(8,128)}, f32[16,128,256]{2,1,0:T(8,128)}) custom-call(f32[16,4,256,256]{3,2,1,0:T(8,128)} %x_ref.9, f32[16,4,256,256]{3,2,1,0:T(8,128)} %t_ref.9, bf16[256,256]{1,0:T(8,128)(2,1)} %maximum_maximum_fusion.2.w_ref), custom_call_target="tpu_custom_call" | custom-call | flops 536870912 | bytes 8388608 | tf_op jit(solution)/shard_map/local_mix/pallas_call | solution.py:155
  79.4 0.7 fusion.17.s_ref
  80.1 2.6 %mode_mix.1 = f32[16,2,8,128]{3,2,1,0:T(8,128)} custom-call(f32[16,2,8,128]{3,2,1,0:T(8,128)} %fusion.17.s_ref, f32[16,16,8,128]{3,2,1,0:T(8,128)} %slice_bitcast_fusion.1.wr_ref, f32[16,16,8,128]{3,2,1,0:T(8,128)} %fusion.wi_ref), custom_call_target="tpu_custom_call" | custom-call | tf_op jit(solution)/shard_map/mode_mix/pallas_call | solution.py:179
  82.6 0.5 collective-permute-start.7
  83.1 4.4 %local_mix.13 = (f32[16,128,256]{2,1,0:T(8,128)}, f32[16,128,256]{2,1,0:T(8,128)}) custom-call(f32[16,4,256,256]{3,2,1,0:T(8,128)} %x_ref.9, f32[16,4,256,256]{3,2,1,0:T(8,128)} %t_ref.9, bf16[256,256]{1,0:T(8,128)(2,1)} %maximum_maximum_fusion.2.w_ref), custom_call_target="tpu_custom_call" | custom-call | flops 536870912 | bytes 8388608 | tf_op jit(solution)/shard_map/local_mix/pallas_call | solution.py:155
  87.5 2.7 %collective-permute-done.7 = f32[1,16,2,8,128]{4,3,2,1,0:T(8,128)S(1)} collective-permute-done((f32[1,16,2,8,128]{4,3,2,1,0:T(8,128)}, f32[1,16,2,8,128]{4,3,2,1,0:T(8,128)S(1)}, u32[]{:S(2)}, u32[]{:S(2)}) %collective-permute-start.7) | collective-permute-done | bytes 131104 | tf_op jit(solution)/shard_map/ppermute | solution.py:262
  90.3 4.6 %local_mix.14 = (f32[16,128,256]{2,1,0:T(8,128)}, f32[16,128,256]{2,1,0:T(8,128)}) custom-call(f32[16,4,256,256]{3,2,1,0:T(8,128)} %x_ref.9, f32[16,4,256,256]{3,2,1,0:T(8,128)} %t_ref.9, bf16[256,256]{1,0:T(8,128)(2,1)} %maximum_maximum_fusion.2.w_ref), custom_call_target="tpu_custom_call" | custom-call | flops 536870912 | bytes 8388608 | tf_op jit(solution)/shard_map/local_mix/pallas_call | solution.py:155
  94.9 1.7 %collective-permute-done.8 = f32[2,16,2,8,128]{4,3,2,1,0:T(8,128)S(1)} collective-permute-done((f32[2,16,2,8,128]{4,3,2,1,0:T(8,128)S(1)}, f32[2,16,2,8,128]{4,3,2,1,0:T(8,128)S(1)}, u32[]{:S(2)}, u32[]{:S(2)}) %collective-permute-start.8) | collective-permute-done | bytes 262176 | tf_op jit(solution)/shard_map/ppermute | solution.py:262
  96.8 1.4 collective-permute-start.10
  98.2 0.5 collective-permute-start.9
  98.7 4.4 %local_mix.15 = (f32[16,128,256]{2,1,0:T(8,128)}, f32[16,128,256]{2,1,0:T(8,128)}) custom-call(f32[16,4,256,256]{3,2,1,0:T(8,128)} %x_ref.9, f32[16,4,256,256]{3,2,1,0:T(8,128)} %t_ref.9, bf16[256,256]{1,0:T(8,128)(2,1)} %maximum_maximum_fusion.2.w_ref), custom_call_target="tpu_custom_call" | custom-call | flops 536870912 | bytes 8388608 | tf_op jit(solution)/shard_map/local_mix/pallas_call | solution.py:155
  103.1 0.7 collective-permute-done.10
  103.7 3.4 %collective-permute-done.9 = f32[1,4,8,2,8,128]{5,4,3,2,1,0:T(8,128)S(1)} collective-permute-done((f32[1,4,8,2,8,128]{5,4,3,2,1,0:T(8,128)S(1)}, f32[1,4,8,2,8,128]{5,4,3,2,1,0:T(8,128)S(1)}, u32[]{:S(2)}, u32[]{:S(2)}) %collective-permute-start.9) | collective-permute-done | bytes 262176 | tf_op jit(solution)/shard_map/ppermute | solution.py:262
  107.2 0.2 collective-permute-start.12
  107.4 0.7 collective-permute-start.11
  108.1 8.4 %collective-permute-done.12 = f32[2,4,8,2,8,128]{5,4,3,2,1,0:T(8,128)S(1)} collective-permute-done((f32[2,4,8,2,8,128]{5,4,3,2,1,0:T(8,128)S(1)}, f32[2,4,8,2,8,128]{5,4,3,2,1,0:T(8,128)S(1)}, u32[]{:S(2)}, u32[]{:S(2)}) %collective-permute-start.12) | collective-permute-done | bytes 524320 | tf_op jit(solution)/shard_map/ppermute | solution.py:262
  116.5 0.1 collective-permute-done.11
  116.6 0.2 maximum_maximum_fusion.own_ref
  116.8 0.1 fusion.10
  117.0 0.9 pad_maximum_fusion.6.z_ref
  117.8 0.3 fusion.26
  118.2 0.8 pad_maximum_fusion.3.phi_ref
  119.0 2.0 %collective-permute-done.13.got_ref = f32[2,8,16,2,8,128]{5,4,3,2,1,0:T(8,128)S(1)} collective-permute-done((f32[2,8,16,2,8,128]{5,4,3,2,1,0:T(8,128)S(1)}, f32[2,8,16,2,8,128]{5,4,3,2,1,0:T(8,128)S(1)}, u32[]{:S(2)}, u32[]{:S(2)}) %collective-permute-start.13) | collective-permute-done | bytes 2097184 | tf_op jit(solution)/shard_map/ppermute | solution.py:262
  121.0 1.3 copy-done.5
  122.3 30.7 %inverse_transform.1 = (f32[16,4,256,256]{3,2,1,0:T(8,128)}, f32[16,4,256,256]{3,2,1,0:T(8,128)}) custom-call(f32[2,8,16,2,8,128]{5,4,3,2,1,0:T(8,128)} %copy-done.4, f32[2,8,16,2,8,128]{5,4,3,2,1,0:T(8,128)} %copy-done.5, f32[16]{0:T(128)} %bias_ref.1, bf16[384,512]{1,0:T(8,128)(2,1)} %pad_maximum_fusion.3.phi_ref, ...), custom_call_target="tpu_custom_call" | custom-call | flops 6710886400 | bytes 67108864 | tf_op jit(solution)/shard_map/inverse_transform/pallas_call | solution.py:239
  (46 shorter events, 0.9 us)
Async XLA Ops:
  0.6 56.9 %copy-start = (f32[2,16,16,8,16]{4,3,2,1,0:T(8,128)S(1)}, f32[2,16,16,8,16]{4,3,2,1,0:T(8,128)}, u32[]{:S(2)}) copy-start(f32[2,16,16,8,16]{4,3,2,1,0:T(8,128)} %param.10) | copy-start | bytes 786436
  7.2 20.1 %copy-start.7 = (f32[16,16]{1,0:T(8,128)S(1)}, f32[16,16]{1,0:T(8,128)}, u32[]{:S(2)}) copy-start(f32[16,16]{1,0:T(8,128)} %param.11) | copy-start | bytes 3076
  26.8 4.6 %collective-permute-start = (f32[2,8,16,2,8,128]{5,4,3,2,1,0:T(8,128)}, f32[2,8,16,2,8,128]{5,4,3,2,1,0:T(8,128)}, u32[]{:S(2)}, u32[]{:S(2)}) collective-permute-start(f32[2,8,16,2,8,128]{5,4,3,2,1,0:T(8,128)} %get-tuple-element.63), channel_id=1, source_target_pairs={{0,1},{1,0},{2,3},{3,2},{4,5},{5,4},{6,7},{7,6},{8,9},{9,8},{10,11... | collective-permute-start | bytes 6291464 | tf_op jit(solution)/shard_map/ppermute | solution.py:262
  34.0 1.5 copy-start.2
  36.3 15.4 %collective-permute-start.1 = (f32[8,8,2,8,128]{4,3,2,1,0:T(8,128)}, f32[8,8,2,8,128]{4,3,2,1,0:T(8,128)}, u32[]{:S(2)}, u32[]{:S(2)}) collective-permute-start(f32[8,8,2,8,128]{4,3,2,1,0:T(8,128)} %slice_bitcast_fusion.2), channel_id=1, source_target_pairs={{0,2},{1,3},{2,0},{3,1},{4,6},{5,7},{6,4},{7,5},{8,10},{9,11},{10,... | collective-permute-start | bytes 1572872 | tf_op jit(solution)/shard_map/ppermute | solution.py:262
  39.2 14.0 %collective-permute-start.2 = (f32[2,4,8,2,8,128]{5,4,3,2,1,0:T(8,128)}, f32[2,4,8,2,8,128]{5,4,3,2,1,0:T(8,128)}, u32[]{:S(2)}, u32[]{:S(2)}) collective-permute-start(f32[2,4,8,2,8,128]{5,4,3,2,1,0:T(8,128)} %slice.76), channel_id=1, source_target_pairs={{0,4},{4,0},{8,12},{12,8},{16,20},{20,16},{24,28},{28,24},{1,5},{5... | collective-permute-start | bytes 1572872 | tf_op jit(solution)/shard_map/ppermute | solution.py:262
  46.4 6.8 %copy-start.3 = (f32[2,8,16,2,8,128]{5,4,3,2,1,0:T(8,128)S(1)}, f32[2,8,16,2,8,128]{5,4,3,2,1,0:T(8,128)}, u32[]{:S(2)}) copy-start(f32[2,8,16,2,8,128]{5,4,3,2,1,0:T(8,128)} %copy-done.2) | copy-start | bytes 6291460
  55.5 8.4 %collective-permute-start.3 = (f32[4,8,2,8,128]{4,3,2,1,0:T(8,128)S(1)}, f32[4,8,2,8,128]{4,3,2,1,0:T(8,128)S(1)}, u32[]{:S(2)}, u32[]{:S(2)}) collective-permute-start(f32[4,8,2,8,128]{4,3,2,1,0:T(8,128)S(1)} %slice.78), channel_id=1, source_target_pairs={{0,4},{4,0},{8,12},{12,8},{16,20},{20,16},{24,28},{28,24},{1,5},{5... | collective-permute-start | bytes 786440 | tf_op jit(solution)/shard_map/ppermute | solution.py:262
  57.0 6.9 %collective-permute-start.4 = (f32[4,8,2,8,128]{4,3,2,1,0:T(8,128)S(1)}, f32[4,8,2,8,128]{4,3,2,1,0:T(8,128)S(1)}, u32[]{:S(2)}, u32[]{:S(2)}) collective-permute-start(f32[4,8,2,8,128]{4,3,2,1,0:T(8,128)S(1)} %slice_bitcast_fusion.7), channel_id=1, source_target_pairs={{0,2},{1,3},{2,0},{3,1},{4,6},{5,7},{6,4},{7,5},{8,10},{9,11},{10,... | collective-permute-start | bytes 786440 | tf_op jit(solution)/shard_map/ppermute | solution.py:262
  64.1 7.1 %collective-permute-start.5 = (f32[2,16,2,8,128]{4,3,2,1,0:T(8,128)S(1)}, f32[2,16,2,8,128]{4,3,2,1,0:T(8,128)S(1)}, u32[]{:S(2)}, u32[]{:S(2)}) collective-permute-start(f32[2,16,2,8,128]{4,3,2,1,0:T(8,128)S(1)} %pad_maximum_fusion.4), channel_id=1, source_target_pairs={{0,8},{4,12},{8,0},{12,4},{16,24},{20,28},{24,16},{28,20},{1,9},{5... | collective-permute-start | bytes 786440 | tf_op jit(solution)/shard_map/ppermute | solution.py:262
  71.3 8.1 %collective-permute-start.6 = (f32[1,16,2,8,128]{4,3,2,1,0:T(8,128)S(1)}, f32[1,16,2,8,128]{4,3,2,1,0:T(8,128)S(1)}, u32[]{:S(2)}, u32[]{:S(2)}) collective-permute-start(f32[1,16,2,8,128]{4,3,2,1,0:T(8,128)S(1)} %slice.85), channel_id=1, source_target_pairs={{0,16},{4,20},{8,24},{12,28},{16,0},{20,4},{24,8},{28,12},{1,17},{... | collective-permute-start | bytes 393224 | tf_op jit(solution)/shard_map/ppermute | solution.py:262
  82.6 7.6 %copy-start.6 = (f32[16,2,8,128]{3,2,1,0:T(8,128)S(1)}, f32[16,2,8,128]{3,2,1,0:T(8,128)}, u32[]{:S(2)}) copy-start(f32[16,2,8,128]{3,2,1,0:T(8,128)} %mode_mix.1) | copy-start | bytes 393220
  82.6 7.6 %collective-permute-start.7 = (f32[1,16,2,8,128]{4,3,2,1,0:T(8,128)}, f32[1,16,2,8,128]{4,3,2,1,0:T(8,128)S(1)}, u32[]{:S(2)}, u32[]{:S(2)}) collective-permute-start(f32[1,16,2,8,128]{4,3,2,1,0:T(8,128)} %bitcast.42), channel_id=1, source_target_pairs={{0,16},{4,20},{8,24},{12,28},{16,0},{20,4},{24,8},{28,12},{1,17},{... | collective-permute-start | bytes 393224 | tf_op jit(solution)/shard_map/ppermute | solution.py:262
  90.2 6.4 %collective-permute-start.8 = (f32[2,16,2,8,128]{4,3,2,1,0:T(8,128)S(1)}, f32[2,16,2,8,128]{4,3,2,1,0:T(8,128)S(1)}, u32[]{:S(2)}, u32[]{:S(2)}) collective-permute-start(f32[2,16,2,8,128]{4,3,2,1,0:T(8,128)S(1)} %pad_maximum_fusion.5), channel_id=1, source_target_pairs={{0,8},{4,12},{8,0},{12,4},{16,24},{20,28},{24,16},{28,20},{1,9},{5... | collective-permute-start | bytes 786440 | tf_op jit(solution)/shard_map/ppermute | solution.py:262
  96.8 7.0 %collective-permute-start.10 = (f32[1,4,8,2,8,128]{5,4,3,2,1,0:T(8,128)S(1)}, f32[1,4,8,2,8,128]{5,4,3,2,1,0:T(8,128)S(1)}, u32[]{:S(2)}, u32[]{:S(2)}) collective-permute-start(f32[1,4,8,2,8,128]{5,4,3,2,1,0:T(8,128)S(1)} %get-tuple-element.122), channel_id=1, source_target_pairs={{0,2},{1,3},{2,0},{3,1},{4,6},{5,7},{6,4},{7,5},{8,10},{9,11},{10,... | collective-permute-start | bytes 786440 | tf_op jit(solution)/shard_map/ppermute | solution.py:262
  98.2 9.0 %collective-permute-start.9 = (f32[1,4,8,2,8,128]{5,4,3,2,1,0:T(8,128)S(1)}, f32[1,4,8,2,8,128]{5,4,3,2,1,0:T(8,128)S(1)}, u32[]{:S(2)}, u32[]{:S(2)}) collective-permute-start(f32[1,4,8,2,8,128]{5,4,3,2,1,0:T(8,128)S(1)} %get-tuple-element.123), channel_id=1, source_target_pairs={{0,4},{4,0},{8,12},{12,8},{16,20},{20,16},{24,28},{28,24},{1,5},{5... | collective-permute-start | bytes 786440 | tf_op jit(solution)/shard_map/ppermute | solution.py:262
  107.2 9.2 %collective-permute-start.12 = (f32[2,4,8,2,8,128]{5,4,3,2,1,0:T(8,128)S(1)}, f32[2,4,8,2,8,128]{5,4,3,2,1,0:T(8,128)S(1)}, u32[]{:S(2)}, u32[]{:S(2)}) collective-permute-start(f32[2,4,8,2,8,128]{5,4,3,2,1,0:T(8,128)S(1)} %pad_maximum_fusion.2), channel_id=1, source_target_pairs={{0,4},{4,0},{8,12},{12,8},{16,20},{20,16},{24,28},{28,24},{1,5},{5... | collective-permute-start | bytes 1572872 | tf_op jit(solution)/shard_map/ppermute | solution.py:262
  107.4 9.2 %collective-permute-start.11 = (f32[1,8,8,2,8,128]{5,4,3,2,1,0:T(8,128)S(1)}, f32[1,8,8,2,8,128]{5,4,3,2,1,0:T(8,128)S(1)}, u32[]{:S(2)}, u32[]{:S(2)}) collective-permute-start(f32[1,8,8,2,8,128]{5,4,3,2,1,0:T(8,128)S(1)} %pad_maximum_fusion.1), channel_id=1, source_target_pairs={{0,2},{1,3},{2,0},{3,1},{4,6},{5,7},{6,4},{7,5},{8,10},{9,11},{10,... | collective-permute-start | bytes 1572872 | tf_op jit(solution)/shard_map/ppermute | solution.py:262
  116.7 4.2 %copy-start.4 = (f32[2,8,16,2,8,128]{5,4,3,2,1,0:T(8,128)}, f32[2,8,16,2,8,128]{5,4,3,2,1,0:T(8,128)S(1)}, u32[]{:S(2)}) copy-start(f32[2,8,16,2,8,128]{5,4,3,2,1,0:T(8,128)S(1)} %maximum_maximum_fusion.own_ref) | copy-start | bytes 6291460
  116.8 4.2 %collective-permute-start.13 = (f32[2,8,16,2,8,128]{5,4,3,2,1,0:T(8,128)S(1)}, f32[2,8,16,2,8,128]{5,4,3,2,1,0:T(8,128)S(1)}, u32[]{:S(2)}, u32[]{:S(2)}) collective-permute-start(f32[2,8,16,2,8,128]{5,4,3,2,1,0:T(8,128)S(1)} %maximum_maximum_fusion.own_ref), channel_id=1, source_target_pairs={{0,1},{1,0},{2,3},{3,2},{4,5},{5,4},{6,7},{7,6},{8,9},{9,8},{10,11... | collective-permute-start | bytes 6291464 | tf_op jit(solution)/shard_map/ppermute | solution.py:262
  121.0 1.3 copy-start.5
  122.3 30.8 %copy-start.1 = (f32[2,16,16,8,16]{4,3,2,1,0:T(8,128)S(1)}, f32[2,16,16,8,16]{4,3,2,1,0:T(8,128)}, u32[]{:S(2)}) copy-start(f32[2,16,16,8,16]{4,3,2,1,0:T(8,128)} %param.10) | copy-start | bytes 786436

commit v3 on v2

v3 whole, which is shorter than its diff:
```python
import functools
import itertools
import math

import jax
import jax.numpy as jnp
from jax import lax
from jax.experimental import pallas as pl
from jax.experimental.pallas import tpu as pltpu
from jax.sharding import PartitionSpec as P

f32 = jnp.float32
bf16 = jnp.bfloat16
MIB = 1024 * 1024


def split(x):
    high = lax.reduce_precision(x, 8, 7)
    return high.astype(bf16), (x - high).astype(bf16)


def halves(x):
    high = x.astype(bf16)
    return high, (x - high.astype(f32)).astype(bf16)


def dot(a, b):
    return lax.dot_general(a, b, (((1,), (0,)), ((), ())), preferred_element_type=f32)


def angles(positions, modes, length):
    product = positions[:, None] * modes[None, :] % length
    angle = product.astype(f32) * (2.0 * math.pi / length)
    return jnp.cos(angle), jnp.sin(angle)


def exchange(items, width):
    items = list(items)
    count = len(items)
    lanes = items[0].shape[-1]
    lane = lax.broadcasted_iota(jnp.int32, items[0].shape, items[0].ndim - 1)
    step = 1
    while step < count:
        shift = width * step
        low = (lane // shift) % 2 == 0
        for i in range(count):
            if i & step:
                continue
            a, b = items[i], items[i | step]
            items[i] = jnp.where(low, a, pltpu.roll(b, shift, 1))
            items[i | step] = jnp.where(low, pltpu.roll(a, lanes - shift, 1), b)
        step *= 2
    return items


def wrap(x, n):
    return x & (n - 1) if n & (n - 1) == 0 else lax.rem(x, n)


def cosines(turns, n):
    return jnp.cos(wrap(turns, n).astype(f32) * (2.0 * math.pi / n))


def build_tables(z_modes, phi_modes, phi_ref, z_ref, n_gz, n_phi):
    phi_local, lanes = phi_ref.shape[0] // 2, phi_ref.shape[1] // 2
    rows, z_local = z_ref.shape[0] // 2, z_ref.shape[1]
    kp, kz = lanes // 2, rows // 2
    width, depth = kp // n_phi, kz // n_gz
    n = n_phi * phi_local
    me = lax.axis_index("phi")
    lane = lax.broadcasted_iota(jnp.int32, (8, lanes), 1)
    mode = jnp.zeros((8, lanes), jnp.int32)
    for i in range(kp):
        value = phi_modes[((i // width) ^ me) * width + i % width]
        mode = jnp.where((lane == i) | (lane == i + kp), value, mode)
    quarter = jnp.where(lane < kp, 0, n // 4)
    position = me * phi_local + lax.broadcasted_iota(jnp.int32, (phi_local, lanes), 0)
    high, low = halves(cosines(position * mode[:1] + quarter[:1], n))
    phi_ref[:phi_local, :lanes] = high
    phi_ref[:phi_local, lanes:] = low
    phi_ref[phi_local:, :lanes] = high
    phi_ref[phi_local:, lanes:] = jnp.zeros_like(low)

    n = n_gz * z_local
    me = lax.axis_index("gz")
    order = gz_order(n_gz)
    row = lax.broadcasted_iota(jnp.int32, (kz, z_local), 0)
    mode = jnp.zeros((kz, z_local), jnp.int32)
    for i in range(kz):
        value = z_modes[(order[i // depth] ^ me) * depth + i % depth]
        mode = jnp.where(row == i, value, mode)
    position = me * z_local + lax.broadcasted_iota(jnp.int32, (kz, z_local), 1)
    turns = position * mode
    for part, quarter in enumerate((0, 3 * n // 4)):
        high, low = halves(cosines(turns + quarter, n))
        z_ref[part * kz : (part + 1) * kz] = high
        z_ref[rows + part * kz : rows + (part + 1) * kz] = low


def forward_kernel(
    z_modes, phi_modes, x_ref, t_ref, ak_ref, as_ref, bk_ref, bs_ref, phi_ref, z_ref, *, n_gz, n_phi
):
    at, count = pl.program_id(0), pl.num_programs(0)

    @pl.when(at == 0)
    def _():
        build_tables(z_modes, phi_modes, phi_ref, z_ref, n_gz, n_phi)

    width = phi_ref.shape[1] // (4 * n_phi)
    for first, keep_ref, send_ref in ((True, ak_ref, as_ref), (False, bk_ref, bs_ref)):

        @pl.when((at < count // 2) == first)
        def _():
            transform(phi_ref, z_ref, x_ref, t_ref, keep_ref, send_ref, n_phi, width)


def transform(phi_ref, z_ref, x_ref, t_ref, keep_ref, send_ref, n_phi, width):
    block, cycles, z_local, phi_local = x_ref.shape
    modes2 = z_ref.shape[0] // 2
    modes = modes2 // 2
    lanes = phi_ref.shape[1] // 2
    shape = keep_ref.shape[1:-4] + keep_ref.shape[-2:]
    lane = lax.broadcasted_iota(jnp.int32, (modes, lanes), 1)
    sign = jnp.where(lane < lanes // 2, 1.0, -1.0).astype(f32)

    def along_phi(c, part):
        x = (x_ref, t_ref)[part][c].reshape(cycles * z_local, phi_local)
        high, low = halves(x)
        y = dot(jnp.concatenate([high, low], axis=1), phi_ref[...])
        high, low = halves(y[:, :lanes] + y[:, lanes:])
        return jnp.concatenate([high, low], axis=1)

    def along_z(y):
        return [dot(z_ref[...], y[r * z_local : (r + 1) * z_local]) for r in range(cycles)]

    def finish(c, products):
        items = []
        for m in products:
            m = m[:modes2, :lanes] + (m[:modes2, lanes:] + m[modes2:, :lanes])
            items.append(m[:modes] + sign * pltpu.roll(m[modes:], lanes // 2, 1))
        for group in range(len(items) // n_phi):
            part = exchange(items[group * n_phi : (group + 1) * n_phi], width)
            for slot, item in enumerate(part):
                out = keep_ref if slot % 2 == 0 else send_ref
                out[slot // 2, ..., c, group, :, :] = item.reshape(shape)

    steps = [(c, part) for c in range(block) for part in range(2)]
    ahead = along_phi(*steps[0])
    products = []
    for i, (c, part) in enumerate(steps):
        y = ahead
        if i + 1 < len(steps):
            ahead = along_phi(*steps[i + 1])
        products.append(along_z(y))
        if part == 0 and c:
            finish(c - 1, products[-3] + products[-2])
    finish(block - 1, products[-2] + products[-1])


def forward(field, tangent, z_modes, phi_modes, n_phi, n_gz):
    channels, cycles, z_local, phi_local = field.shape
    groups = 2 * cycles // n_phi
    kz, kp = z_modes.shape[0], phi_modes.shape[0]
    lanes = 2 * kp
    out = jax.ShapeDtypeStruct((n_phi // 2, n_gz, channels // 2, groups, kz // n_gz, lanes), f32)
    step = 4
    steps = channels // step
    block = pl.BlockSpec((step, cycles, z_local, phi_local), lambda c: (c, 0, 0, 0))
    shape = (n_phi // 2, n_gz, step, groups, kz // n_gz, lanes)
    a_block = pl.BlockSpec(shape, lambda c: (0, 0, jnp.minimum(c, steps // 2 - 1), 0, 0, 0))
    b_block = pl.BlockSpec(shape, lambda c: (0, 0, jnp.maximum(c - steps // 2, 0), 0, 0, 0))
    return pl.pallas_call(
        functools.partial(forward_kernel, n_gz=n_gz, n_phi=n_phi),
        grid=(steps,),
        in_specs=[pl.BlockSpec(memory_space=pltpu.SMEM)] * 2 + [block, block],
        out_specs=[a_block, a_block, b_block, b_block],
        out_shape=[out] * 4,
        scratch_shapes=[
            pltpu.VMEM((2 * phi_local, 2 * lanes), bf16),
            pltpu.VMEM((4 * kz, z_local), bf16),
        ],
        compiler_params=pltpu.CompilerParams(vmem_limit_bytes=36 * MIB),
        cost_estimate=pl.CostEstimate(
            flops=24 * field.size * lanes, bytes_accessed=8 * field.size, transcendentals=0
        ),
        name="forward_transform",
    )(z_modes, phi_modes, field, tangent)


def local_kernel(x_ref, t_ref, w_ref, bias_ref, xo_ref, to_ref):
    channels, _, rows, columns = x_ref.shape
    base = pl.multiple_of(pl.program_id(0) * rows, rows)
    tiles = [
        (ref, out, start) for ref, out in ((x_ref, xo_ref), (t_ref, to_ref)) for start in range(0, rows, 8)
    ]
    for at in range(0, len(tiles), 4):
        products = []
        for ref, _, start in tiles[at : at + 4]:
            high, low = halves(ref[:, 0, start : start + 8, :].reshape(channels * 8, columns))
            products.append(dot(w_ref[...], jnp.concatenate([high, low], axis=0)))
        for (_, out, start), m in zip(tiles[at : at + 4], products):
            m = (m[: channels * 8] + m[channels * 8 :]).reshape(channels, 8, columns)
            out[:, pl.ds(base + start, 8), :] = m + bias_ref[...] if out is xo_ref else m


def local_mix(field, tangent, weight, bias, cycle, part, parts):
    channels, _, z_local, phi_local = field.shape
    span = z_local // parts
    rows = min(64, span)
    steps = span // rows
    out = pltpu.VMEM((channels, span, phi_local), f32)
    block = pl.BlockSpec((channels, 1, rows, phi_local), lambda z: (0, cycle, part * steps + z, 0))
    out_block = pl.BlockSpec(memory_space=pltpu.VMEM)
    size = channels * span * phi_local
    return pl.pallas_call(
        local_kernel,
        grid=(steps,),
        in_specs=[
            block,
            block,
            pl.BlockSpec(weight.shape, lambda z: (0, 0)),
            pl.BlockSpec(bias.shape, lambda z: (0, 0, 0)),
        ],
        out_specs=[out_block, out_block],
        out_shape=[out, out],
        compiler_params=pltpu.CompilerParams(vmem_limit_bytes=16 * MIB),
        cost_estimate=pl.CostEstimate(flops=1024 * size, bytes_accessed=8 * size, transcendentals=0),
        name="local_mix",
    )(field, tangent, weight, bias)


def mix_kernel(s_ref, wr_ref, wi_ref, out_ref):
    channels = s_ref.shape[0]
    lanes = s_ref.shape[-1]
    total = jnp.zeros(out_ref.shape, f32)
    for c in range(channels):
        s = s_ref[c]
        turned = jnp.concatenate([s[..., lanes // 2 :], s[..., : lanes // 2]], axis=-1)
        total = total + s[None] * wr_ref[c][:, None] + turned[None] * wi_ref[c][:, None]
    out_ref[...] = total


def mix(spectrum, wr, wi):
    return pl.pallas_call(
        mix_kernel,
        out_shape=jax.ShapeDtypeStruct((wr.shape[1],) + spectrum.shape[1:], f32),
        compiler_params=pltpu.CompilerParams(vmem_limit_bytes=8 * MIB),
        name="mode_mix",
    )(spectrum, wr, wi)


def gelu_pair(x, t):
    a = math.sqrt(2.0 / math.pi)
    b = a * 0.044715
    square = x * x
    s = 0.5 + 0.5 * jnp.tanh(x * (a + b * square))
    out = x * s
    return out, t * (s + out * ((1.0 - s) * (2.0 * a + (6.0 * b) * square)))


def inverse_kernel(*refs, n_phi, width):
    own, other = refs[:4], refs[4:8]
    phi_ref, z_ref = refs[8:10]
    out_ref, out_t_ref = refs[-2:]
    refs = refs[10:-2]
    block, cycles, z_local, phi_local = out_ref.shape
    parts = len(refs) // (2 * cycles)
    span = z_local // parts
    groups, depth, lanes = own[0].shape[-3:]
    modes = z_ref.shape[1] // 6
    first = pl.program_id(0) < pl.num_programs(0) // 2
    at = pl.program_id(0) * block

    def slots(pieces, c, group):
        v, ab1, a2, b2 = pieces
        ab1 = ab1[:, c, group]
        low = [v[:, c, group], jnp.where(first, ab1, b2[0, :, c, group])]
        high = [
            jnp.where(first, a2[0, :, c, group], ab1),
            jnp.where(first, a2[1, :, c, group], b2[1, :, c, group]),
        ]
        return [jnp.concatenate(rows, axis=0).reshape(modes, lanes) for rows in (low, high)]

    for c in range(block):
        spectral = []
        for group in range(groups):
            pairs = zip(slots(own, c, group), slots(other, c, group))
            items = [item for pair in pairs for item in pair]
            high, low = halves(jnp.concatenate(exchange(items, width), axis=0))
            h = dot(jnp.concatenate([high, low, high], axis=1), phi_ref[...])
            for b in range(n_phi):
                part = h[b * modes : (b + 1) * modes]
                part = jnp.concatenate([part[:, :phi_local], part[:, phi_local:]], axis=0)
                high, low = halves(part)
                spectral.append(jnp.concatenate([high, high, low], axis=0))
        values = [dot(z_ref[...], part) for part in spectral]
        for r in range(cycles):
            for p in range(parts):
                rows = slice(p * span, (p + 1) * span)
                lx, lt = refs[2 * (r * parts + p) : 2 * (r * parts + p) + 2]
                x = values[r][rows] + lx[at + c]
                t = values[cycles + r][rows] + lt[at + c]
                out_ref[c, r, rows], out_t_ref[c, r, rows] = gelu_pair(x, t)


def inverse(own, other, phi_table, z_table, local, cycles, n_phi, width):
    channels, span, phi_local = local[0].shape
    z_local = span * len(local) // (2 * cycles)
    step = 2
    steps = channels // step
    zeros = lambda n: (0,) * n
    shape = (own[0].shape[0], step) + own[0].shape[2:]
    tail = zeros(len(shape) - 2)
    v_block = pl.BlockSpec(shape, lambda o: (0, o) + tail)
    a_block = pl.BlockSpec((2,) + shape, lambda o: (0, 0, jnp.minimum(o, steps // 2 - 1)) + tail)
    b_block = pl.BlockSpec((2,) + shape, lambda o: (0, 0, jnp.maximum(o - steps // 2, 0)) + tail)
    local_block = pl.BlockSpec(memory_space=pltpu.VMEM)
    local = [pltpu.with_memory_space_constraint(piece, pltpu.VMEM) for piece in local]
    out = jax.ShapeDtypeStruct((channels, cycles, z_local, phi_local), f32)
    out_block = pl.BlockSpec((step, cycles, z_local, phi_local), lambda o: (o, 0, 0, 0))
    size = channels * cycles * z_local * phi_local
    return pl.pallas_call(
        functools.partial(inverse_kernel, n_phi=n_phi, width=width),
        grid=(steps,),
        in_specs=[v_block, v_block, a_block, b_block] * 2
        + [
            pl.BlockSpec(phi_table.shape, lambda o: (0, 0)),
            pl.BlockSpec(z_table.shape, lambda o: (0, 0)),
        ]
        + [local_block] * len(local),
        out_specs=[out_block, out_block],
        out_shape=[out, out],
        compiler_params=pltpu.CompilerParams(vmem_limit_bytes=22 * MIB),
        cost_estimate=pl.CostEstimate(
            flops=1600 * size, bytes_accessed=16 * size, transcendentals=size
        ),
        name="inverse_transform",
    )(*own, *other, phi_table, z_table, *local)


def swap(x, axis, bit):
    count = lax.axis_size(axis)
    return lax.ppermute(x, axis, [(i, i ^ bit) for i in range(count)])


class Filler:
    def __init__(self, field, tangent, small, prepare, parts):
        self.inputs = (field, tangent)
        self.small = small
        self.prepare = prepare
        self.tables = None
        self.parts = parts
        self.todo = [(r, p) for r in range(field.shape[1]) for p in range(parts)]
        self.done = []

    def beside(self, sent, got, count=1):
        if self.tables is None:
            small, _ = lax.optimization_barrier((self.small, sent))
            self.tables = self.prepare(*small)
            got, self.tables = lax.optimization_barrier((got, self.tables))
            return got
        for _ in range(min(count, len(self.todo))):
            r, p = self.todo.pop(0)
            inputs, _ = lax.optimization_barrier((self.inputs, sent))
            piece = local_mix(*inputs, *self.tables[:2], r, p, self.parts)
            got, piece = lax.optimization_barrier((got, piece))
            self.done += piece
        return got


def add(terms, *index):
    return functools.reduce(jnp.add, [term[index] for term in terms])


def reduce_scatter(a, b, n_phi, n_gz, filler):
    low, high = slice(n_gz // 2), slice(n_gz // 2, None)
    a = [a[0], swap(a[1], "phi", 1)]
    b = [b[0], swap(b[1], "phi", 1)]
    sent = (add(a, 1), add(b, slice(None), high))
    got = (swap(sent[0], "phi", 2), swap(sent[1], "gz", 1))
    a_got, b_got = filler.beside(sent, got)
    a = [term[0] for term in a] + [a_got]
    b = [term[:, low] for term in b] + [b_got]
    sent = (add(a, high), add(b, 1))
    got = (swap(sent[0], "gz", 1), swap(sent[1], "phi", 2))
    a_got, b_got = filler.beside(sent, got)
    a = [term[low] for term in a] + [a_got]
    b = [term[0] for term in b] + [b_got]
    v = [jnp.concatenate([add(a), add(b)], axis=1)]
    for bits in gz_groups(n_gz):
        count = 1 << len(bits)
        size = v[0].shape[0] // count
        sent = [add(v, slice(i * size, (i + 1) * size)) for i in range(1, count)]
        got = [swap(part, "gz", group_bits(i, bits)) for i, part in enumerate(sent, 1)]
        v = [term[:size] for term in v] + list(filler.beside(sent, got, count // 2))
    return add(v, 0)


def all_gather(v, n_phi, n_gz, filler):
    v = v[None]
    for bits in reversed(gz_groups(n_gz)):
        count = 1 << len(bits)
        got = [swap(v, "gz", group_bits(i, bits)) for i in range(1, count)]
        got = filler.beside(v, got, count // 2)
        v = jnp.concatenate([v, *got], axis=0)
    half = v.shape[1] // 2
    a, b = v[:, :half], v[:, half:]
    got = (swap(a, "gz", 1), swap(b, "phi", 2), swap(v, "phi", 1))
    a1, b1, v_core = filler.beside((a, b), got)
    ab1 = jnp.concatenate([a1, b1], axis=1)
    a, b = jnp.stack([a, a1]), jnp.stack([b, b1])
    got = (swap(a, "phi", 2), swap(b, "gz", 1), swap(ab1, "phi", 1))
    a2, b2, ab1_core = filler.beside((a, b), got, len(filler.todo))
    return (v, ab1, a2, b2), (v_core, ab1_core, swap(a2, "phi", 1), swap(b2, "phi", 1))


def gz_groups(n_gz):
    bits = list(range(1, n_gz.bit_length() - 1))
    return [bits[i : i + 2] for i in range(0, len(bits), 2)]


def group_bits(i, bits):
    digits = [(i >> (len(bits) - 1 - j)) & 1 for j in range(len(bits))]
    return sum(digit << bit for digit, bit in zip(digits, bits))


def gz_order(n_gz):
    bits = n_gz.bit_length() - 1
    return [
        sum(digit << i for i, digit in enumerate(digits))
        for digits in itertools.product((0, 1), repeat=bits)
    ]


def tables(spectral_weight, local_weight, bias_term, z_modes, phi_modes, z_local, phi_local):
    n_gz = lax.axis_size("gz")
    n_phi = lax.axis_size("phi")
    kz, kp = z_modes.shape[0], phi_modes.shape[0]
    width = kp // n_phi
    z_total, phi_total = z_local * n_gz, phi_local * n_phi
    my_gz = lax.axis_index("gz")
    my_phi = lax.axis_index("phi")

    z_global = my_gz * z_local + jnp.arange(z_local, dtype=jnp.int32)
    phi_global = my_phi * phi_local + jnp.arange(phi_local, dtype=jnp.int32)
    z_kept = z_modes.reshape(n_gz, -1)[my_gz ^ jnp.array(gz_order(n_gz), jnp.int32)].reshape(-1)
    phi_kept = phi_modes.reshape(n_phi, -1)[my_phi ^ jnp.arange(n_phi, dtype=jnp.int32)].reshape(-1)
    zc, zs = angles(z_global, z_kept, z_total)
    pc, ps = angles(phi_global, phi_kept, phi_total)
    high, low = split(jnp.concatenate([zc, -zs], axis=1))
    z_back = jnp.concatenate([high, low, high], 1)
    high, low = split(
        jnp.concatenate(
            [jnp.concatenate([pc.T, ps.T], 1), jnp.concatenate([-ps.T, pc.T], 1)], 0
        )
    )
    phi_back = jnp.concatenate([high, high, low], 0)

    high, low = split(jnp.kron(local_weight.T, jnp.eye(8, dtype=f32)))
    local_table = jnp.concatenate(
        [jnp.concatenate([high, high], 1), jnp.concatenate([low, low], 1)], 0
    )
    wide_bias = jnp.broadcast_to(bias_term[:, None, None], (bias_term.shape[0], 8, phi_local))

    scale = (1.0 / math.sqrt(z_total * phi_total)) * (2.0 / math.sqrt(kz * kp))
    spread = jnp.tile(jnp.eye(width, dtype=f32), (1, 2 * n_phi)) * scale
    sign = jnp.where(jnp.arange(2 * kp) < kp, -1.0, 1.0).astype(f32)
    wide = jnp.dot(spectral_weight, spread, precision=lax.Precision.HIGHEST)
    return local_table, wide_bias, phi_back, z_back, wide[0], wide[1] * sign


def body(field, field_tangent, spectral_weight, local_weight, bias_term, z_modes, phi_modes):
    channels, cycles, z_local, phi_local = field.shape
    n_gz = lax.axis_size("gz")
    n_phi = lax.axis_size("phi")
    width = phi_modes.shape[0] // n_phi
    small = (spectral_weight, local_weight, bias_term, z_modes, phi_modes)
    prepare = functools.partial(tables, z_local=z_local, phi_local=phi_local)
    field = pltpu.with_memory_space_constraint(field, pltpu.HBM)
    field_tangent = pltpu.with_memory_space_constraint(field_tangent, pltpu.HBM)
    filler = Filler(field, field_tangent, small, prepare, 2)

    ak, asent, bk, bsent = forward(field, field_tangent, z_modes, phi_modes, n_phi, n_gz)
    spectrum = reduce_scatter((ak, asent), (bk, bsent), n_phi, n_gz, filler)
    _, _, phi_back, z_back, wr, wi = filler.tables
    mixed = mix(spectrum, wr, wi)
    own, other = all_gather(mixed, n_phi, n_gz, filler)
    return inverse(own, other, phi_back, z_back, filler.done, cycles, n_phi, width)


def solution(mesh):
    return jax.shard_map(
        body,
        mesh=mesh,
        in_specs=(
            P(None, None, "gz", "phi"),
            P(None, None, "gz", "phi"),
            P(None, None, None, "gz", "phi"),
            P(),
            P(),
            P(),
            P(),
        ),
        out_specs=(P(None, None, "gz", "phi"), P(None, None, "gz", "phi")),
        check_vma=False,
    )
```

time: 154 us -> 139 us (0.903)
  Pallas kernels: 88.5 us -> 70.9 us
  starting transfers between devices: 14.7 us -> 21.9 us
  local copies, waits for them, and re-layouts: 9.02 us -> 6.88 us
    pallas_call x8, Pallas kernels: 35.6 us -> 24.4 us  [local_mix(): pl.pallas_call(local_kernel, grid=(steps,), in_specs=[block, block, pl.Bl...]
    ppermute x14 -> x20, starting transfers between devices: 14.7 us -> 21.9 us  [swap(): return lax.ppermute(x, axis, [(i, i ^ bit) for i in range(count)])]
    pallas_call x1, Pallas kernels: 30.7 us -> 25.2 us  [inverse(): pl.pallas_call(functools.partial(inverse_kernel, n_phi=n_phi, width=width...]
    add x7 -> x8, other arithmetic: 4.89 us -> 7.48 us  [the longest x6 7.47 us: add(): return functools.reduce(jnp.add, [term[index] for term in terms])]
    pallas_call x1, Pallas kernels: 2.59 us -> 0.35 us  [mix(): pl.pallas_call(mix_kernel, out_shape=jax.ShapeDtypeStruct((wr.shape[1],)...]
    concatenate x11 -> x5, other arithmetic: 3.42 us -> 1.58 us  [the longest x1 0.79 us: tables(): phi_back = jnp.concatenate([high, high, low], 0)]
    squeeze x3 -> x1, local copies, waits for them, and re-layouts: 1.94 us -> 0.09 us  [tables(): return (local_table, wide_bias, phi_back, z_back, wide[0], wide[1] * sign)]
    unnamed x16 -> x39, local copies, waits for them, and re-layouts: 1.88 us -> 3.34 us
  transfers between devices with their start and end apart: 14 -> 20, of which waited for: 11 -> 12; matrix products, arithmetic and copies ran while one was open for 5% -> 10% of each run, Pallas kernels for 23% -> 18%
where the time goes in v3:
time: 139 us
  Pallas kernels  70.9 us (51%)
  waiting for transfers between devices  24.8 us (18%)
  starting transfers between devices  21.9 us (16%)
  other arithmetic  11.5 us (8%)
  local copies, waits for them, and re-layouts  6.88 us (5%)
  matrix products  1.77 us (1%)
    pallas_call x1, Pallas kernels, inverse(): pl.pallas_call(functools.partial(inverse_kernel, n_phi=n_phi, width=width...  25.2 us
    ppermute x20, waiting for transfers between devices, swap(): return lax.ppermute(x, axis, [(i, i ^ bit) for i in range(count)])  24.8 us
    pallas_call x8, Pallas kernels, local_mix(): pl.pallas_call(local_kernel, grid=(steps,), in_specs=[block, block, pl.Bl...  24.4 us
    ppermute x20, starting transfers between devices, swap(): return lax.ppermute(x, axis, [(i, i ^ bit) for i in range(count)])  21.9 us
    pallas_call x1, Pallas kernels, forward(): pl.pallas_call(functools.partial(forward_kernel, n_gz=n_gz, n_phi=n_phi),...  20.9 us
    add x6, other arithmetic, add(): return functools.reduce(jnp.add, [term[index] for term in terms])  7.47 us
    unnamed x39, local copies, waits for them, and re-layouts  3.34 us
  transfers between devices with their start and end apart: 20, of which 12 were waited for; matrix products, arithmetic and copies ran while one was open for 10% of the time, Pallas kernels for 18%

profile of v3, /device:TPU:0, one launch (start us, length us, event | category | flops | bytes accessed | tf_op | source)
XLA Modules:
  0.0 138.9 jit_solution(4220976554741369811)
XLA Ops:
  0.7 0.8 copy-done.4
  1.5 0.7 copy-done.6
  2.1 20.9 %forward_transform.1 = (f32[2,8,8,2,8,128]{5,4,3,2,1,0:T(8,128)S(1)}, f32[2,8,8,2,8,128]{5,4,3,2,1,0:T(8,128)}, f32[2,8,8,2,8,128]{5,4,3,2,1,0:T(8,128)S(1)}, f32[2,8,8,2,8,128]{5,4,3,2,1,0:T(8,128)}) custom-call(s32[64]{0:T(128)S(1)} %copy-done.6, s32[64]{0:T(128)S(1)} %copy-done.4, f32[16,4,256,256]{3,2,1,0:T(8,128)} %x_ref.9, f32[16,4,256,256]{3,2,1,0:T(8,128)} %t_ref.9), custom_call_target="tpu_custom_call" | custom-call | flops 12884901888 | bytes 33554432 | tf_op jit(solution)/shard_map/forward_transform/pallas_call | solution.py:172
  23.0 1.0 copy-done.2
  23.9 0.5 collective-permute-start
  24.5 0.1 reshape.102
  24.7 2.3 %collective-permute-done = f32[2,8,8,2,8,128]{5,4,3,2,1,0:T(8,128)} collective-permute-done((f32[2,8,8,2,8,128]{5,4,3,2,1,0:T(8,128)}, f32[2,8,8,2,8,128]{5,4,3,2,1,0:T(8,128)}, u32[]{:S(2)}, u32[]{:S(2)}) %collective-permute-start) | collective-permute-done | bytes 1048608 | tf_op jit(solution)/shard_map/ppermute | solution.py:343
  27.0 1.9 %fusion.1 = f32[8,8,2,8,128]{4,3,2,1,0:T(8,128)} fusion(f32[2,8,8,2,8,128]{5,4,3,2,1,0:T(8,128)} %collective-permute-done, f32[2,8,8,2,8,128]{5,4,3,2,1,0:T(8,128)S(1)} %get-tuple-element.84), kind=kLoop, calls=%fused_computation.13 | loop fusion | flops 131072 | bytes 1572864 | tf_op jit(solution)/shard_map/add | solution.py:372
  28.9 2.9 %collective-permute-start.1 = (f32[8,8,2,8,128]{4,3,2,1,0:T(8,128)}, f32[8,8,2,8,128]{4,3,2,1,0:T(8,128)}, u32[]{:S(2)}, u32[]{:S(2)}) collective-permute-start(f32[8,8,2,8,128]{4,3,2,1,0:T(8,128)} %fusion.1), channel_id=1, source_target_pairs={{0,2},{1,3},{2,0},{3,1},{4,6},{5,7},{6,4},{7,5},{8,10},{9,11},{10,... | collective-permute-start | bytes 1572872 | tf_op jit(solution)/shard_map/ppermute | solution.py:343
  31.8 2.1 %slice_add_fusion = f32[2,4,8,2,8,128]{5,4,3,2,1,0:T(8,128)} fusion(f32[2,8,8,2,8,128]{5,4,3,2,1,0:T(8,128)} %collective-permute-done.2, f32[2,8,8,2,8,128]{5,4,3,2,1,0:T(8,128)} %copy-done.2), kind=kLoop, calls=%fused_computation.11 | loop fusion | flops 131072 | bytes 1572864 | tf_op jit(solution)/shard_map/add | solution.py:372
  33.9 1.5 %collective-permute-start.3 = (f32[2,4,8,2,8,128]{5,4,3,2,1,0:T(8,128)}, f32[2,4,8,2,8,128]{5,4,3,2,1,0:T(8,128)}, u32[]{:S(2)}, u32[]{:S(2)}) collective-permute-start(f32[2,4,8,2,8,128]{5,4,3,2,1,0:T(8,128)} %slice_add_fusion), channel_id=1, source_target_pairs={{0,4},{4,0},{8,12},{12,8},{16,20},{20,16},{24,28},{28,24},{1,5},{5... | collective-permute-start | bytes 1572872 | tf_op jit(solution)/shard_map/ppermute | solution.py:343
  35.4 0.1 reshape.83
  35.5 0.6 gather_fusion
  36.0 0.1 mul.100
  36.2 0.6 gather_fusion.1
  36.7 0.1 mul.107
  36.9 1.1 broadcast_multiply_fusion
  38.0 1.6 %mul.97 = f32[128,128]{1,0:T(8,128)S(1)} reshape(f32[16,8,16,8]{3,2,1,0:T(8,128)} %broadcast_multiply_fusion) | data formatting | bytes 131072 | tf_op jit(solution)/shard_map/jit(kron)/mul | solution.py:459
  39.7 0.3 fusion.29
  40.1 0.8 pad_maximum_fusion.3.refs_8_
  40.8 0.6 fusion.28
  41.4 0.1 fusion.13
  41.6 0.7 pad_maximum_fusion.4.refs_9_
  42.3 1.8 %fusion.32 = f32[2,16,16,8,128]{4,3,2,1,0:T(8,128)S(1)} fusion(f32[2,16,16,8,16]{4,3,2,1,0:T(8,128)S(1)} %copy-done, f32[16,128,1,1,1]{1,0,2,3,4:T(8,128)S(1)} %reshape.102), kind=kOutput, calls=%fused_computation.75 | convolution fusion | flops 100663296 | bytes 2367488 | tf_op jit(solution)/shard_map/dot_general | solution.py:468
  44.1 0.1 slice_bitcast_fusion.1.wr_ref
  44.2 0.1 fusion.wi_ref
  44.3 3.5 %collective-permute-done.3 = f32[2,4,8,2,8,128]{5,4,3,2,1,0:T(8,128)} collective-permute-done((f32[2,4,8,2,8,128]{5,4,3,2,1,0:T(8,128)}, f32[2,4,8,2,8,128]{5,4,3,2,1,0:T(8,128)}, u32[]{:S(2)}, u32[]{:S(2)}) %collective-permute-start.3) | collective-permute-done | bytes 524320 | tf_op jit(solution)/shard_map/ppermute | solution.py:343
  47.9 0.1 broadcast_in_dim.28.bias_ref
  48.0 1.1 fusion.7
  49.0 0.4 collective-permute-start.5
  49.4 1.1 fusion.9
  50.5 1.8 %collective-permute-start.4 = (f32[4,8,2,8,128]{4,3,2,1,0:T(8,128)S(1)}, f32[4,8,2,8,128]{4,3,2,1,0:T(8,128)S(1)}, u32[]{:S(2)}, u32[]{:S(2)}) collective-permute-start(f32[4,8,2,8,128]{4,3,2,1,0:T(8,128)S(1)} %fusion.9), channel_id=1, source_target_pairs={{0,4},{4,0},{8,12},{12,8},{16,20},{20,16},{24,28},{28,24},{1,5},{5... | collective-permute-start | bytes 786440 | tf_op jit(solution)/shard_map/ppermute | solution.py:343
  52.3 3.0 %local_mix.8 = (f32[16,128,256]{2,1,0:T(8,128)S(1)}, f32[16,128,256]{2,1,0:T(8,128)S(1)}) custom-call(f32[16,4,256,256]{3,2,1,0:T(8,128)} %x_ref.9, f32[16,4,256,256]{3,2,1,0:T(8,128)} %t_ref.9, bf16[256,256]{1,0:T(8,128)(2,1)S(1)} %maximum_maximum_fusion.1.w_ref, f32[16,8,256]{2,1,0:T(8,128)S(1)} %broadcast_in_dim.28.bias_ref), custom_call_target="tpu_custom_call" | custom-call | flops 536870912 | bytes 4194304 | tf_op jit(solution)/shard_map/local_mix/pallas_call | solution.py:215
  55.4 0.9 collective-permute-done.5
  56.3 1.5 %collective-permute-done.4 = f32[4,8,2,8,128]{4,3,2,1,0:T(8,128)S(1)} collective-permute-done((f32[4,8,2,8,128]{4,3,2,1,0:T(8,128)S(1)}, f32[4,8,2,8,128]{4,3,2,1,0:T(8,128)S(1)}, u32[]{:S(2)}, u32[]{:S(2)}) %collective-permute-start.4) | collective-permute-done | bytes 262176 | tf_op jit(solution)/shard_map/ppermute | solution.py:343
  57.8 1.3 fusion.5
  59.2 3.6 %collective-permute-start.8 = (f32[1,16,2,8,128]{4,3,2,1,0:T(8,128)S(1)}, f32[1,16,2,8,128]{4,3,2,1,0:T(8,128)S(1)}, u32[]{:S(2)}, u32[]{:S(2)}) collective-permute-start(f32[1,16,2,8,128]{4,3,2,1,0:T(8,128)S(1)} %get-tuple-element.170), channel_id=1, source_target_pairs={{0,24},{4,28},{8,16},{12,20},{16,8},{20,12},{24,0},{28,4},{1,25},{... | collective-permute-start | bytes 393224 | tf_op jit(solution)/shard_map/ppermute | solution.py:343
  62.7 0.9 collective-permute-start.7
  63.6 3.0 %local_mix.10 = (f32[16,128,256]{2,1,0:T(8,128)S(1)}, f32[16,128,256]{2,1,0:T(8,128)S(1)}) custom-call(f32[16,4,256,256]{3,2,1,0:T(8,128)} %x_ref.9, f32[16,4,256,256]{3,2,1,0:T(8,128)} %t_ref.9, bf16[256,256]{1,0:T(8,128)(2,1)S(1)} %maximum_maximum_fusion.1.w_ref, f32[16,8,256]{2,1,0:T(8,128)S(1)} %broadcast_in_dim.28.bias_ref), custom_call_target="tpu_custom_call" | custom-call | flops 536870912 | bytes 4194304 | tf_op jit(solution)/shard_map/local_mix/pallas_call | solution.py:215
  66.7 3.1 %local_mix.9 = (f32[16,128,256]{2,1,0:T(8,128)S(1)}, f32[16,128,256]{2,1,0:T(8,128)S(1)}) custom-call(f32[16,4,256,256]{3,2,1,0:T(8,128)} %x_ref.9, f32[16,4,256,256]{3,2,1,0:T(8,128)} %t_ref.9, bf16[256,256]{1,0:T(8,128)(2,1)S(1)} %maximum_maximum_fusion.1.w_ref, f32[16,8,256]{2,1,0:T(8,128)S(1)} %broadcast_in_dim.28.bias_ref), custom_call_target="tpu_custom_call" | custom-call | flops 536870912 | bytes 4194304 | tf_op jit(solution)/shard_map/local_mix/pallas_call | solution.py:215
  69.8 2.3 %collective-permute-done.6 = f32[1,16,2,8,128]{4,3,2,1,0:T(8,128)S(1)} collective-permute-done((f32[1,16,2,8,128]{4,3,2,1,0:T(8,128)S(1)}, f32[1,16,2,8,128]{4,3,2,1,0:T(8,128)S(1)}, u32[]{:S(2)}, u32[]{:S(2)}) %collective-permute-start.6) | collective-permute-done | bytes 131104 | tf_op jit(solution)/shard_map/ppermute | solution.py:343
  72.1 0.4 mode_mix.1
  72.5 2.4 %collective-permute-start.11 = (f32[1,16,2,8,128]{4,3,2,1,0:T(8,128)S(1)}, f32[1,16,2,8,128]{4,3,2,1,0:T(8,128)S(1)}, u32[]{:S(2)}, u32[]{:S(2)}) collective-permute-start(f32[1,16,2,8,128]{4,3,2,1,0:T(8,128)S(1)} %bitcast.42), channel_id=1, source_target_pairs={{0,24},{4,28},{8,16},{12,20},{16,8},{20,12},{24,0},{28,4},{1,25},{... | collective-permute-start | bytes 393224 | tf_op jit(solution)/shard_map/ppermute | solution.py:343
  74.9 2.1 %collective-permute-start.9 = (f32[1,16,2,8,128]{4,3,2,1,0:T(8,128)S(1)}, f32[1,16,2,8,128]{4,3,2,1,0:T(8,128)S(1)}, u32[]{:S(2)}, u32[]{:S(2)}) collective-permute-start(f32[1,16,2,8,128]{4,3,2,1,0:T(8,128)S(1)} %bitcast.44), channel_id=1, source_target_pairs={{0,16},{4,20},{8,24},{12,28},{16,0},{20,4},{24,8},{28,12},{1,17},{... | collective-permute-start | bytes 393224 | tf_op jit(solution)/shard_map/ppermute | solution.py:343
  76.9 3.0 %local_mix.12 = (f32[16,128,256]{2,1,0:T(8,128)S(1)}, f32[16,128,256]{2,1,0:T(8,128)S(1)}) custom-call(f32[16,4,256,256]{3,2,1,0:T(8,128)} %x_ref.9, f32[16,4,256,256]{3,2,1,0:T(8,128)} %t_ref.9, bf16[256,256]{1,0:T(8,128)(2,1)S(1)} %maximum_maximum_fusion.1.w_ref, f32[16,8,256]{2,1,0:T(8,128)S(1)} %broadcast_in_dim.28.bias_ref), custom_call_target="tpu_custom_call" | custom-call | flops 536870912 | bytes 4194304 | tf_op jit(solution)/shard_map/local_mix/pallas_call | solution.py:215
  80.0 3.1 %local_mix.11 = (f32[16,128,256]{2,1,0:T(8,128)S(1)}, f32[16,128,256]{2,1,0:T(8,128)S(1)}) custom-call(f32[16,4,256,256]{3,2,1,0:T(8,128)} %x_ref.9, f32[16,4,256,256]{3,2,1,0:T(8,128)} %t_ref.9, bf16[256,256]{1,0:T(8,128)(2,1)S(1)} %maximum_maximum_fusion.1.w_ref, f32[16,8,256]{2,1,0:T(8,128)S(1)} %broadcast_in_dim.28.bias_ref), custom_call_target="tpu_custom_call" | custom-call | flops 536870912 | bytes 4194304 | tf_op jit(solution)/shard_map/local_mix/pallas_call | solution.py:215
  83.1 1.8 %collective-permute-done.9 = f32[1,16,2,8,128]{4,3,2,1,0:T(8,128)S(1)} collective-permute-done((f32[1,16,2,8,128]{4,3,2,1,0:T(8,128)S(1)}, f32[1,16,2,8,128]{4,3,2,1,0:T(8,128)S(1)}, u32[]{:S(2)}, u32[]{:S(2)}) %collective-permute-start.9) | collective-permute-done | bytes 131104 | tf_op jit(solution)/shard_map/ppermute | solution.py:343
  85.0 0.1 slice_bitcast_fusion.2
  85.1 1.5 %collective-permute-start.13 = (f32[4,8,2,8,128]{4,3,2,1,0:T(8,128)S(1)}, f32[4,8,2,8,128]{4,3,2,1,0:T(8,128)S(1)}, u32[]{:S(2)}, u32[]{:S(2)}) collective-permute-start(f32[4,8,2,8,128]{4,3,2,1,0:T(8,128)S(1)} %get-tuple-element.168), channel_id=1, source_target_pairs={{0,2},{1,3},{2,0},{3,1},{4,6},{5,7},{6,4},{7,5},{8,10},{9,11},{10,... | collective-permute-start | bytes 786440 | tf_op jit(solution)/shard_map/ppermute | solution.py:343
  86.7 1.5 %collective-permute-start.12 = (f32[4,8,2,8,128]{4,3,2,1,0:T(8,128)S(1)}, f32[4,8,2,8,128]{4,3,2,1,0:T(8,128)S(1)}, u32[]{:S(2)}, u32[]{:S(2)}) collective-permute-start(f32[4,8,2,8,128]{4,3,2,1,0:T(8,128)S(1)} %get-tuple-element.169), channel_id=1, source_target_pairs={{0,4},{4,0},{8,12},{12,8},{16,20},{20,16},{24,28},{28,24},{1,5},{5... | collective-permute-start | bytes 786440 | tf_op jit(solution)/shard_map/ppermute | solution.py:343
  88.2 3.0 %local_mix.13 = (f32[16,128,256]{2,1,0:T(8,128)S(1)}, f32[16,128,256]{2,1,0:T(8,128)S(1)}) custom-call(f32[16,4,256,256]{3,2,1,0:T(8,128)} %x_ref.9, f32[16,4,256,256]{3,2,1,0:T(8,128)} %t_ref.9, bf16[256,256]{1,0:T(8,128)(2,1)S(1)} %maximum_maximum_fusion.1.w_ref, f32[16,8,256]{2,1,0:T(8,128)S(1)} %broadcast_in_dim.28.bias_ref), custom_call_target="tpu_custom_call" | custom-call | flops 536870912 | bytes 4194304 | tf_op jit(solution)/shard_map/local_mix/pallas_call | solution.py:215
  91.3 2.6 %collective-permute-done.13 = f32[4,8,2,8,128]{4,3,2,1,0:T(8,128)S(1)} collective-permute-done((f32[4,8,2,8,128]{4,3,2,1,0:T(8,128)S(1)}, f32[4,8,2,8,128]{4,3,2,1,0:T(8,128)S(1)}, u32[]{:S(2)}, u32[]{:S(2)}) %collective-permute-start.13) | collective-permute-done | bytes 262176 | tf_op jit(solution)/shard_map/ppermute | solution.py:343
  93.9 1.2 collective-permute-done.12
  95.3 0.6 collective-permute-start.15
  95.9 1.6 %collective-permute-start.16 = (f32[2,4,8,2,8,128]{5,4,3,2,1,0:T(8,128)S(1)}, f32[2,4,8,2,8,128]{5,4,3,2,1,0:T(8,128)S(1)}, u32[]{:S(2)}, u32[]{:S(2)}) collective-permute-start(f32[2,4,8,2,8,128]{5,4,3,2,1,0:T(8,128)S(1)} %pad_maximum_fusion.2), channel_id=1, source_target_pairs={{0,4},{4,0},{8,12},{12,8},{16,20},{20,16},{24,28},{28,24},{1,5},{5... | collective-permute-start | bytes 1572872 | tf_op jit(solution)/shard_map/ppermute | solution.py:343
  97.5 3.0 %local_mix.15 = (f32[16,128,256]{2,1,0:T(8,128)S(1)}, f32[16,128,256]{2,1,0:T(8,128)S(1)}) custom-call(f32[16,4,256,256]{3,2,1,0:T(8,128)} %x_ref.9, f32[16,4,256,256]{3,2,1,0:T(8,128)} %t_ref.9, bf16[256,256]{1,0:T(8,128)(2,1)S(1)} %maximum_maximum_fusion.1.w_ref, f32[16,8,256]{2,1,0:T(8,128)S(1)} %broadcast_in_dim.28.bias_ref), custom_call_target="tpu_custom_call" | custom-call | flops 536870912 | bytes 4194304 | tf_op jit(solution)/shard_map/local_mix/pallas_call | solution.py:215
  100.6 3.1 %local_mix.14 = (f32[16,128,256]{2,1,0:T(8,128)S(1)}, f32[16,128,256]{2,1,0:T(8,128)S(1)}) custom-call(f32[16,4,256,256]{3,2,1,0:T(8,128)} %x_ref.9, f32[16,4,256,256]{3,2,1,0:T(8,128)} %t_ref.9, bf16[256,256]{1,0:T(8,128)(2,1)S(1)} %maximum_maximum_fusion.1.w_ref, f32[16,8,256]{2,1,0:T(8,128)S(1)} %broadcast_in_dim.28.bias_ref), custom_call_target="tpu_custom_call" | custom-call | flops 536870912 | bytes 4194304 | tf_op jit(solution)/shard_map/local_mix/pallas_call | solution.py:215
  103.7 6.0 %collective-permute-done.15.refs_2_ = f32[2,4,8,2,8,128]{5,4,3,2,1,0:T(8,128)S(1)} collective-permute-done((f32[2,4,8,2,8,128]{5,4,3,2,1,0:T(8,128)S(1)}, f32[2,4,8,2,8,128]{5,4,3,2,1,0:T(8,128)S(1)}, u32[]{:S(2)}, u32[]{:S(2)}) %collective-permute-start.15) | collective-permute-done | bytes 524320 | tf_op jit(solution)/shard_map/ppermute | solution.py:343
  109.7 0.4 collective-permute-done.16.refs_3_
  110.0 0.5 collective-permute-start.19
  110.6 1.4 %collective-permute-done.18.refs_6_ = f32[2,4,8,2,8,128]{5,4,3,2,1,0:T(8,128)S(1)} collective-permute-done((f32[2,4,8,2,8,128]{5,4,3,2,1,0:T(8,128)S(1)}, f32[2,4,8,2,8,128]{5,4,3,2,1,0:T(8,128)S(1)}, u32[]{:S(2)}, u32[]{:S(2)}) %collective-permute-start.18) | collective-permute-done | bytes 524320 | tf_op jit(solution)/shard_map/ppermute | solution.py:343
  112.0 0.7 collective-permute-done.19.refs_7_
  112.7 0.8 copy-done.15
  113.6 25.2 %inverse_transform.1 = (f32[16,4,256,256]{3,2,1,0:T(8,128)}, f32[16,4,256,256]{3,2,1,0:T(8,128)}) custom-call(f32[4,16,2,8,128]{4,3,2,1,0:T(8,128)} %copy-done.8, f32[4,16,2,8,128]{4,3,2,1,0:T(8,128)} %copy-done.9, f32[2,4,8,2,8,128]{5,4,3,2,1,0:T(8,128)} %copy-done.12, f32[2,4,8,2,8,128]{5,4,3,2,1,0:T(8,128)} %copy-done.13, ...), custom_call_target="tpu_custom_call" | custom-call | flops 6710886400 | bytes 67108864 | tf_op jit(solution)/shard_map/inverse_transform/pallas_call | solution.py:322
  (70 shorter events, 0.8 us)
Async XLA Ops:
  0.6 41.7 %copy-start = (f32[2,16,16,8,16]{4,3,2,1,0:T(8,128)S(1)}, f32[2,16,16,8,16]{4,3,2,1,0:T(8,128)}, u32[]{:S(2)}) copy-start(f32[2,16,16,8,16]{4,3,2,1,0:T(8,128)} %param.10) | copy-start | bytes 786436
  0.6 0.8 copy-start.4
  1.5 0.7 copy-start.6
  2.1 22.5 %copy-start.18 = (s32[8]{0:T(128)S(1)}, s32[8]{0:T(128)}, u32[]{:S(2)}) copy-start(s32[8]{0:T(128)} %constant.59.clone) | copy-start | bytes 100
  23.0 1.0 copy-start.2
  23.9 11.4 %copy-start.5 = (s32[64]{0:T(128)S(1)}, s32[64]{0:T(128)}, u32[]{:S(2)}) copy-start(s32[64]{0:T(128)} %phi_modes.1) | copy-start | bytes 772
  23.9 12.2 %copy-start.7 = (s32[64]{0:T(128)S(1)}, s32[64]{0:T(128)}, u32[]{:S(2)}) copy-start(s32[64]{0:T(128)} %z_modes.1) | copy-start | bytes 772
  23.9 12.9 %copy-start.16 = (f32[16,16]{1,0:T(8,128)S(1)}, f32[16,16]{1,0:T(8,128)}, u32[]{:S(2)}) copy-start(f32[16,16]{1,0:T(8,128)} %param.11) | copy-start | bytes 3076
  23.9 3.1 %collective-permute-start = (f32[2,8,8,2,8,128]{5,4,3,2,1,0:T(8,128)}, f32[2,8,8,2,8,128]{5,4,3,2,1,0:T(8,128)}, u32[]{:S(2)}, u32[]{:S(2)}) collective-permute-start(f32[2,8,8,2,8,128]{5,4,3,2,1,0:T(8,128)} %get-tuple-element.85), channel_id=1, source_target_pairs={{0,1},{1,0},{2,3},{3,2},{4,5},{5,4},{6,7},{7,6},{8,9},{9,8},{10,11... | collective-permute-start | bytes 3145736 | tf_op jit(solution)/shard_map/ppermute | solution.py:343
  24.4 7.4 %collective-permute-start.2 = (f32[2,8,8,2,8,128]{5,4,3,2,1,0:T(8,128)}, f32[2,8,8,2,8,128]{5,4,3,2,1,0:T(8,128)}, u32[]{:S(2)}, u32[]{:S(2)}) collective-permute-start(f32[2,8,8,2,8,128]{5,4,3,2,1,0:T(8,128)} %get-tuple-element.87), channel_id=1, source_target_pairs={{0,1},{1,0},{2,3},{3,2},{4,5},{5,4},{6,7},{7,6},{8,9},{9,8},{10,11... | collective-permute-start | bytes 3145736 | tf_op jit(solution)/shard_map/ppermute | solution.py:343
  28.9 15.4 %collective-permute-start.1 = (f32[8,8,2,8,128]{4,3,2,1,0:T(8,128)}, f32[8,8,2,8,128]{4,3,2,1,0:T(8,128)}, u32[]{:S(2)}, u32[]{:S(2)}) collective-permute-start(f32[8,8,2,8,128]{4,3,2,1,0:T(8,128)} %fusion.1), channel_id=1, source_target_pairs={{0,2},{1,3},{2,0},{3,1},{4,6},{5,7},{6,4},{7,5},{8,10},{9,11},{10,... | collective-permute-start | bytes 1572872 | tf_op jit(solution)/shard_map/ppermute | solution.py:343
  33.9 14.0 %collective-permute-start.3 = (f32[2,4,8,2,8,128]{5,4,3,2,1,0:T(8,128)}, f32[2,4,8,2,8,128]{5,4,3,2,1,0:T(8,128)}, u32[]{:S(2)}, u32[]{:S(2)}) collective-permute-start(f32[2,4,8,2,8,128]{5,4,3,2,1,0:T(8,128)} %slice_add_fusion), channel_id=1, source_target_pairs={{0,4},{4,0},{8,12},{12,8},{16,20},{20,16},{24,28},{28,24},{1,5},{5... | collective-permute-start | bytes 1572872 | tf_op jit(solution)/shard_map/ppermute | solution.py:343
  44.1 3.8 %copy-start.17 = (f32[16]{0:T(128)S(1)}, f32[16]{0:T(128)}, u32[]{:S(2)}) copy-start(f32[16]{0:T(128)} %param.12) | copy-start | bytes 196
  44.1 3.9 %copy-start.3 = (f32[2,8,8,2,8,128]{5,4,3,2,1,0:T(8,128)S(1)}, f32[2,8,8,2,8,128]{5,4,3,2,1,0:T(8,128)}, u32[]{:S(2)}) copy-start(f32[2,8,8,2,8,128]{5,4,3,2,1,0:T(8,128)} %copy-done.2) | copy-start | bytes 3145732
  49.0 7.3 %collective-permute-start.5 = (f32[4,8,2,8,128]{4,3,2,1,0:T(8,128)S(1)}, f32[4,8,2,8,128]{4,3,2,1,0:T(8,128)S(1)}, u32[]{:S(2)}, u32[]{:S(2)}) collective-permute-start(f32[4,8,2,8,128]{4,3,2,1,0:T(8,128)S(1)} %fusion.7), channel_id=1, source_target_pairs={{0,2},{1,3},{2,0},{3,1},{4,6},{5,7},{6,4},{7,5},{8,10},{9,11},{10,... | collective-permute-start | bytes 786440 | tf_op jit(solution)/shard_map/ppermute | solution.py:343
  50.5 7.3 %collective-permute-start.4 = (f32[4,8,2,8,128]{4,3,2,1,0:T(8,128)S(1)}, f32[4,8,2,8,128]{4,3,2,1,0:T(8,128)S(1)}, u32[]{:S(2)}, u32[]{:S(2)}) collective-permute-start(f32[4,8,2,8,128]{4,3,2,1,0:T(8,128)S(1)} %fusion.9), channel_id=1, source_target_pairs={{0,4},{4,0},{8,12},{12,8},{16,20},{20,16},{24,28},{28,24},{1,5},{5... | collective-permute-start | bytes 786440 | tf_op jit(solution)/shard_map/ppermute | solution.py:343
  59.2 10.6 %collective-permute-start.8 = (f32[1,16,2,8,128]{4,3,2,1,0:T(8,128)S(1)}, f32[1,16,2,8,128]{4,3,2,1,0:T(8,128)S(1)}, u32[]{:S(2)}, u32[]{:S(2)}) collective-permute-start(f32[1,16,2,8,128]{4,3,2,1,0:T(8,128)S(1)} %get-tuple-element.170), channel_id=1, source_target_pairs={{0,24},{4,28},{8,16},{12,20},{16,8},{20,12},{24,0},{28,4},{1,25},{... | collective-permute-start | bytes 393224 | tf_op jit(solution)/shard_map/ppermute | solution.py:343
  62.7 9.3 %collective-permute-start.6 = (f32[1,16,2,8,128]{4,3,2,1,0:T(8,128)S(1)}, f32[1,16,2,8,128]{4,3,2,1,0:T(8,128)S(1)}, u32[]{:S(2)}, u32[]{:S(2)}) collective-permute-start(f32[1,16,2,8,128]{4,3,2,1,0:T(8,128)S(1)} %get-tuple-element.171), channel_id=1, source_target_pairs={{0,16},{4,20},{8,24},{12,28},{16,0},{20,4},{24,8},{28,12},{1,17},{... | collective-permute-start | bytes 393224 | tf_op jit(solution)/shard_map/ppermute | solution.py:343
  62.7 9.3 %collective-permute-start.7 = (f32[1,16,2,8,128]{4,3,2,1,0:T(8,128)S(1)}, f32[1,16,2,8,128]{4,3,2,1,0:T(8,128)S(1)}, u32[]{:S(2)}, u32[]{:S(2)}) collective-permute-start(f32[1,16,2,8,128]{4,3,2,1,0:T(8,128)S(1)} %get-tuple-element.172), channel_id=1, source_target_pairs={{0,8},{4,12},{8,0},{12,4},{16,24},{20,28},{24,16},{28,20},{1,9},{5... | collective-permute-start | bytes 393224 | tf_op jit(solution)/shard_map/ppermute | solution.py:343
  72.5 10.6 %collective-permute-start.11 = (f32[1,16,2,8,128]{4,3,2,1,0:T(8,128)S(1)}, f32[1,16,2,8,128]{4,3,2,1,0:T(8,128)S(1)}, u32[]{:S(2)}, u32[]{:S(2)}) collective-permute-start(f32[1,16,2,8,128]{4,3,2,1,0:T(8,128)S(1)} %bitcast.42), channel_id=1, source_target_pairs={{0,24},{4,28},{8,16},{12,20},{16,8},{20,12},{24,0},{28,4},{1,25},{... | collective-permute-start | bytes 393224 | tf_op jit(solution)/shard_map/ppermute | solution.py:343
  74.9 8.2 %collective-permute-start.10 = (f32[1,16,2,8,128]{4,3,2,1,0:T(8,128)S(1)}, f32[1,16,2,8,128]{4,3,2,1,0:T(8,128)S(1)}, u32[]{:S(2)}, u32[]{:S(2)}) collective-permute-start(f32[1,16,2,8,128]{4,3,2,1,0:T(8,128)S(1)} %bitcast.43), channel_id=1, source_target_pairs={{0,8},{4,12},{8,0},{12,4},{16,24},{20,28},{24,16},{28,20},{1,9},{5... | collective-permute-start | bytes 393224 | tf_op jit(solution)/shard_map/ppermute | solution.py:343
  74.9 10.0 %collective-permute-start.9 = (f32[1,16,2,8,128]{4,3,2,1,0:T(8,128)S(1)}, f32[1,16,2,8,128]{4,3,2,1,0:T(8,128)S(1)}, u32[]{:S(2)}, u32[]{:S(2)}) collective-permute-start(f32[1,16,2,8,128]{4,3,2,1,0:T(8,128)S(1)} %bitcast.44), channel_id=1, source_target_pairs={{0,16},{4,20},{8,24},{12,28},{16,0},{20,4},{24,8},{28,12},{1,17},{... | collective-permute-start | bytes 393224 | tf_op jit(solution)/shard_map/ppermute | solution.py:343
  84.9 6.3 %copy-start.8 = (f32[4,16,2,8,128]{4,3,2,1,0:T(8,128)}, f32[4,16,2,8,128]{4,3,2,1,0:T(8,128)S(1)}, u32[]{:S(2)}) copy-start(f32[4,16,2,8,128]{4,3,2,1,0:T(8,128)S(1)} %pad_maximum_fusion.refs_0_) | copy-start | bytes 1572868
  84.9 10.2 %collective-permute-start.14 = (f32[4,16,2,8,128]{4,3,2,1,0:T(8,128)S(1)}, f32[4,16,2,8,128]{4,3,2,1,0:T(8,128)S(1)}, u32[]{:S(2)}, u32[]{:S(2)}) collective-permute-start(f32[4,16,2,8,128]{4,3,2,1,0:T(8,128)S(1)} %pad_maximum_fusion.refs_0_), channel_id=1, source_target_pairs={{0,1},{1,0},{2,3},{3,2},{4,5},{5,4},{6,7},{7,6},{8,9},{9,8},{10,11... | collective-permute-start | bytes 1572872 | tf_op jit(solution)/shard_map/ppermute | solution.py:343
  85.1 8.8 %collective-permute-start.13 = (f32[4,8,2,8,128]{4,3,2,1,0:T(8,128)S(1)}, f32[4,8,2,8,128]{4,3,2,1,0:T(8,128)S(1)}, u32[]{:S(2)}, u32[]{:S(2)}) collective-permute-start(f32[4,8,2,8,128]{4,3,2,1,0:T(8,128)S(1)} %get-tuple-element.168), channel_id=1, source_target_pairs={{0,2},{1,3},{2,0},{3,1},{4,6},{5,7},{6,4},{7,5},{8,10},{9,11},{10,... | collective-permute-start | bytes 786440 | tf_op jit(solution)/shard_map/ppermute | solution.py:343
  86.7 8.4 %collective-permute-start.12 = (f32[4,8,2,8,128]{4,3,2,1,0:T(8,128)S(1)}, f32[4,8,2,8,128]{4,3,2,1,0:T(8,128)S(1)}, u32[]{:S(2)}, u32[]{:S(2)}) collective-permute-start(f32[4,8,2,8,128]{4,3,2,1,0:T(8,128)S(1)} %get-tuple-element.169), channel_id=1, source_target_pairs={{0,4},{4,0},{8,12},{12,8},{16,20},{20,16},{24,28},{28,24},{1,5},{5... | collective-permute-start | bytes 786440 | tf_op jit(solution)/shard_map/ppermute | solution.py:343
  95.1 5.5 %copy-start.10 = (f32[4,16,2,8,128]{4,3,2,1,0:T(8,128)}, f32[4,16,2,8,128]{4,3,2,1,0:T(8,128)S(1)}, u32[]{:S(2)}) copy-start(f32[4,16,2,8,128]{4,3,2,1,0:T(8,128)S(1)} %collective-permute-done.14.refs_4_) | copy-start | bytes 1572868
  95.1 5.4 %copy-start.9 = (f32[4,16,2,8,128]{4,3,2,1,0:T(8,128)}, f32[4,16,2,8,128]{4,3,2,1,0:T(8,128)S(1)}, u32[]{:S(2)}) copy-start(f32[4,16,2,8,128]{4,3,2,1,0:T(8,128)S(1)} %constant_dynamic-update-slice_fusion.refs_1_) | copy-start | bytes 1572868
  95.2 8.5 %collective-permute-start.17 = (f32[4,16,2,8,128]{4,3,2,1,0:T(8,128)S(1)}, f32[4,16,2,8,128]{4,3,2,1,0:T(8,128)S(1)}, u32[]{:S(2)}, u32[]{:S(2)}) collective-permute-start(f32[4,16,2,8,128]{4,3,2,1,0:T(8,128)S(1)} %constant_dynamic-update-slice_fusion.refs_1_), channel_id=1, source_target_pairs={{0,1},{1,0},{2,3},{3,2},{4,5},{5,4},{6,7},{7,6},{8,9},{9,8},{10,11... | collective-permute-start | bytes 1572872 | tf_op jit(solution)/shard_map/ppermute | solution.py:343
  95.3 14.4 %collective-permute-start.15 = (f32[2,4,8,2,8,128]{5,4,3,2,1,0:T(8,128)S(1)}, f32[2,4,8,2,8,128]{5,4,3,2,1,0:T(8,128)S(1)}, u32[]{:S(2)}, u32[]{:S(2)}) collective-permute-start(f32[2,4,8,2,8,128]{5,4,3,2,1,0:T(8,128)S(1)} %pad_maximum_fusion.1), channel_id=1, source_target_pairs={{0,2},{1,3},{2,0},{3,1},{4,6},{5,7},{6,4},{7,5},{8,10},{9,11},{10,... | collective-permute-start | bytes 1572872 | tf_op jit(solution)/shard_map/ppermute | solution.py:343
  95.9 14.1 %collective-permute-start.16 = (f32[2,4,8,2,8,128]{5,4,3,2,1,0:T(8,128)S(1)}, f32[2,4,8,2,8,128]{5,4,3,2,1,0:T(8,128)S(1)}, u32[]{:S(2)}, u32[]{:S(2)}) collective-permute-start(f32[2,4,8,2,8,128]{5,4,3,2,1,0:T(8,128)S(1)} %pad_maximum_fusion.2), channel_id=1, source_target_pairs={{0,4},{4,0},{8,12},{12,8},{16,20},{20,16},{24,28},{28,24},{1,5},{5... | collective-permute-start | bytes 1572872 | tf_op jit(solution)/shard_map/ppermute | solution.py:343
  103.7 9.0 %copy-start.11 = (f32[4,16,2,8,128]{4,3,2,1,0:T(8,128)}, f32[4,16,2,8,128]{4,3,2,1,0:T(8,128)S(1)}, u32[]{:S(2)}) copy-start(f32[4,16,2,8,128]{4,3,2,1,0:T(8,128)S(1)} %collective-permute-done.17.refs_5_) | copy-start | bytes 1572868
  109.7 3.0 %copy-start.12 = (f32[2,4,8,2,8,128]{5,4,3,2,1,0:T(8,128)}, f32[2,4,8,2,8,128]{5,4,3,2,1,0:T(8,128)S(1)}, u32[]{:S(2)}) copy-start(f32[2,4,8,2,8,128]{5,4,3,2,1,0:T(8,128)S(1)} %collective-permute-done.15.refs_2_) | copy-start | bytes 1572868
  110.0 2.7 %copy-start.13 = (f32[2,4,8,2,8,128]{5,4,3,2,1,0:T(8,128)}, f32[2,4,8,2,8,128]{5,4,3,2,1,0:T(8,128)S(1)}, u32[]{:S(2)}) copy-start(f32[2,4,8,2,8,128]{5,4,3,2,1,0:T(8,128)S(1)} %collective-permute-done.16.refs_3_) | copy-start | bytes 1572868
  110.0 1.9 %collective-permute-start.18 = (f32[2,4,8,2,8,128]{5,4,3,2,1,0:T(8,128)S(1)}, f32[2,4,8,2,8,128]{5,4,3,2,1,0:T(8,128)S(1)}, u32[]{:S(2)}, u32[]{:S(2)}) collective-permute-start(f32[2,4,8,2,8,128]{5,4,3,2,1,0:T(8,128)S(1)} %collective-permute-done.15.refs_2_), channel_id=1, source_target_pairs={{0,1},{1,0},{2,3},{3,2},{4,5},{5,4},{6,7},{7,6},{8,9},{9,8},{10,11... | collective-permute-start | bytes 1572872 | tf_op jit(solution)/shard_map/ppermute | solution.py:343
  110.0 2.7 %collective-permute-start.19 = (f32[2,4,8,2,8,128]{5,4,3,2,1,0:T(8,128)S(1)}, f32[2,4,8,2,8,128]{5,4,3,2,1,0:T(8,128)S(1)}, u32[]{:S(2)}, u32[]{:S(2)}) collective-permute-start(f32[2,4,8,2,8,128]{5,4,3,2,1,0:T(8,128)S(1)} %collective-permute-done.16.refs_3_), channel_id=1, source_target_pairs={{0,1},{1,0},{2,3},{3,2},{4,5},{5,4},{6,7},{7,6},{8,9},{9,8},{10,11... | collective-permute-start | bytes 1572872 | tf_op jit(solution)/shard_map/ppermute | solution.py:343
  112.0 0.8 copy-start.14
  112.7 0.8 copy-start.15
  113.5 25.2 %copy-start.1 = (f32[2,16,16,8,16]{4,3,2,1,0:T(8,128)S(1)}, f32[2,16,16,8,16]{4,3,2,1,0:T(8,128)}, u32[]{:S(2)}) copy-start(f32[2,16,16,8,16]{4,3,2,1,0:T(8,128)} %param.10) | copy-start | bytes 786436

commit v4 on v3

--- a/solution.py
+++ b/solution.py
@@ -14,11 +14,6 @@
 MIB = 1024 * 1024
 
 
-def split(x):
-    high = lax.reduce_precision(x, 8, 7)
-    return high.astype(bf16), (x - high).astype(bf16)
-
-
 def halves(x):
     high = x.astype(bf16)
     return high, (x - high.astype(f32)).astype(bf16)
@@ -26,12 +21,6 @@
 
 def dot(a, b):
     return lax.dot_general(a, b, (((1,), (0,)), ((), ())), preferred_element_type=f32)
-
-
-def angles(positions, modes, length):
-    product = positions[:, None] * modes[None, :] % length
-    angle = product.astype(f32) * (2.0 * math.pi / length)
-    return jnp.cos(angle), jnp.sin(angle)
 
 
 def exchange(items, width):
@@ -61,38 +50,52 @@
     return jnp.cos(wrap(turns, n).astype(f32) * (2.0 * math.pi / n))
 
 
+def modes_by_lane(modes, slots, count, lanes):
+    width = count // len(slots)
+    lane = lax.rem(lax.broadcasted_iota(jnp.int32, (8, lanes), 1), count)
+    mode = jnp.zeros((8, lanes), jnp.int32)
+    for i in range(count):
+        mode = jnp.where(lane == i, modes[slots[i // width] * width + i % width], mode)
+    return mode[:1]
+
+
+def modes_by_row(modes, slots, count, lanes):
+    width = count // len(slots)
+    row = lax.broadcasted_iota(jnp.int32, (count, lanes), 0)
+    mode = jnp.zeros((count, lanes), jnp.int32)
+    for i in range(count):
+        mode = jnp.where(row == i, modes[slots[i // width] * width + i % width], mode)
+    return mode
+
+
+def phi_slots(n_phi):
+    return [slot ^ lax.axis_index("phi") for slot in range(n_phi)]
+
+
+def gz_slots(n_gz):
+    return [slot ^ lax.axis_index("gz") for slot in gz_order(n_gz)]
+
+
 def build_tables(z_modes, phi_modes, phi_ref, z_ref, n_gz, n_phi):
     phi_local, lanes = phi_ref.shape[0] // 2, phi_ref.shape[1] // 2
     rows, z_local = z_ref.shape[0] // 2, z_ref.shape[1]
     kp, kz = lanes // 2, rows // 2
-    width, depth = kp // n_phi, kz // n_gz
     n = n_phi * phi_local
-    me = lax.axis_index("phi")
-    lane = lax.broadcasted_iota(jnp.int32, (8, lanes), 1)
-    mode = jnp.zeros((8, lanes), jnp.int32)
-    for i in range(kp):
-        value = phi_modes[((i // width) ^ me) * width + i % width]
-        mode = jnp.where((lane == i) | (lane == i + kp), value, mode)
+    mode = modes_by_lane(phi_modes, phi_slots(n_phi), kp, lanes)
+    lane = lax.broadcasted_iota(jnp.int32, (1, lanes), 1)
     quarter = jnp.where(lane < kp, 0, n // 4)
-    position = me * phi_local + lax.broadcasted_iota(jnp.int32, (phi_local, lanes), 0)
-    high, low = halves(cosines(position * mode[:1] + quarter[:1], n))
+    position = lax.axis_index("phi") * phi_local + lax.broadcasted_iota(jnp.int32, (phi_local, lanes), 0)
+    high, low = halves(cosines(position * mode + quarter, n))
     phi_ref[:phi_local, :lanes] = high
     phi_ref[:phi_local, lanes:] = low
     phi_ref[phi_local:, :lanes] = high
     phi_ref[phi_local:, lanes:] = jnp.zeros_like(low)
 
     n = n_gz * z_local
-    me = lax.axis_index("gz")
-    order = gz_order(n_gz)
-    row = lax.broadcasted_iota(jnp.int32, (kz, z_local), 0)
-    mode = jnp.zeros((kz, z_local), jnp.int32)
-    for i in range(kz):
-        value = z_modes[(order[i // depth] ^ me) * depth + i % depth]
-        mode = jnp.where(row == i, value, mode)
-    position = me * z_local + lax.broadcasted_iota(jnp.int32, (kz, z_local), 1)
-    turns = position * mode
+    mode = modes_by_row(z_modes, gz_slots(n_gz), kz, z_local)
+    position = lax.axis_index("gz") * z_local + lax.broadcasted_iota(jnp.int32, (kz, z_local), 1)
     for part, quarter in enumerate((0, 3 * n // 4)):
-        high, low = halves(cosines(turns + quarter, n))
+        high, low = halves(cosines(position * mode + quarter, n))
         z_ref[part * kz : (part + 1) * kz] = high
         z_ref[rows + part * kz : rows + (part + 1) * kz] = low
 
@@ -111,10 +114,11 @@
 
         @pl.when((at < count // 2) == first)
         def _():
-            transform(phi_ref, z_ref, x_ref, t_ref, keep_ref, send_ref, n_phi, width)
-
-
-def transform(phi_ref, z_ref, x_ref, t_ref, keep_ref, send_ref, n_phi, width):
+            base = (at if first else at - count // 2) * x_ref.shape[0]
+            transform(phi_ref, z_ref, x_ref, t_ref, keep_ref, send_ref, base, n_phi, width)
+
+
+def transform(phi_ref, z_ref, x_ref, t_ref, keep_ref, send_ref, base, n_phi, width):
     block, cycles, z_local, phi_local = x_ref.shape
     modes2 = z_ref.shape[0] // 2
     modes = modes2 // 2
@@ -142,7 +146,7 @@
             part = exchange(items[group * n_phi : (group + 1) * n_phi], width)
             for slot, item in enumerate(part):
                 out = keep_ref if slot % 2 == 0 else send_ref
-                out[slot // 2, ..., c, group, :, :] = item.reshape(shape)
+                out[slot // 2, :, base + c, group, :, :] = item.reshape(shape)
 
     steps = [(c, part) for c in range(block) for part in range(2)]
     ahead = along_phi(*steps[0])
@@ -162,24 +166,20 @@
     groups = 2 * cycles // n_phi
     kz, kp = z_modes.shape[0], phi_modes.shape[0]
     lanes = 2 * kp
-    out = jax.ShapeDtypeStruct((n_phi // 2, n_gz, channels // 2, groups, kz // n_gz, lanes), f32)
+    out = pltpu.VMEM((n_phi // 2, n_gz, channels // 2, groups, kz // n_gz, lanes), f32)
     step = 4
-    steps = channels // step
     block = pl.BlockSpec((step, cycles, z_local, phi_local), lambda c: (c, 0, 0, 0))
-    shape = (n_phi // 2, n_gz, step, groups, kz // n_gz, lanes)
-    a_block = pl.BlockSpec(shape, lambda c: (0, 0, jnp.minimum(c, steps // 2 - 1), 0, 0, 0))
-    b_block = pl.BlockSpec(shape, lambda c: (0, 0, jnp.maximum(c - steps // 2, 0), 0, 0, 0))
     return pl.pallas_call(
         functools.partial(forward_kernel, n_gz=n_gz, n_phi=n_phi),
-        grid=(steps,),
+        grid=(channels // step,),
         in_specs=[pl.BlockSpec(memory_space=pltpu.SMEM)] * 2 + [block, block],
-        out_specs=[a_block, a_block, b_block, b_block],
+        out_specs=[pl.BlockSpec(memory_space=pltpu.VMEM)] * 4,
         out_shape=[out] * 4,
         scratch_shapes=[
             pltpu.VMEM((2 * phi_local, 2 * lanes), bf16),
             pltpu.VMEM((4 * kz, z_local), bf16),
         ],
-        compiler_params=pltpu.CompilerParams(vmem_limit_bytes=36 * MIB),
+        compiler_params=pltpu.CompilerParams(vmem_limit_bytes=40 * MIB),
         cost_estimate=pl.CostEstimate(
             flops=24 * field.size * lanes, bytes_accessed=8 * field.size, transcendentals=0
         ),
@@ -330,7 +330,7 @@
         + [local_block] * len(local),
         out_specs=[out_block, out_block],
         out_shape=[out, out],
-        compiler_params=pltpu.CompilerParams(vmem_limit_bytes=22 * MIB),
+        compiler_params=pltpu.CompilerParams(vmem_limit_bytes=18 * MIB),
         cost_estimate=pl.CostEstimate(
             flops=1600 * size, bytes_accessed=16 * size, transcendentals=size
         ),
@@ -368,32 +368,75 @@
         return got
 
 
-def add(terms, *index):
-    return functools.reduce(jnp.add, [term[index] for term in terms])
+def sums_kernel(*refs, outputs):
+    refs, outs = refs[: -len(outputs)], refs[-len(outputs) :]
+    for out, parts in zip(outs, outputs):
+        total = [functools.reduce(jnp.add, [refs[at][index] for at, index in part]) for part in parts]
+        out[...] = total[0] if len(total) == 1 else jnp.concatenate(total, axis=1)
+
+
+def sums(*outputs):
+    arrays = []
+    plan = []
+    shapes = []
+    for parts in outputs:
+        entry = []
+        for part in parts:
+            terms = []
+            for array, index in part:
+                known = [i for i, other in enumerate(arrays) if other is array]
+                if not known:
+                    known = [len(arrays)]
+                    arrays.append(array)
+                terms.append((known[0], index))
+            entry.append(terms)
+        plan.append(entry)
+        shape = list(jax.eval_shape(lambda x: x[parts[0][0][1]], parts[0][0][0]).shape)
+        if len(parts) > 1:
+            shape[1] *= len(parts)
+        shapes.append(pltpu.VMEM(tuple(shape), f32))
+    return pl.pallas_call(
+        functools.partial(sums_kernel, outputs=plan),
+        in_specs=[pl.BlockSpec(memory_space=pltpu.VMEM)] * len(arrays),
+        out_specs=[pl.BlockSpec(memory_space=pltpu.VMEM)] * len(shapes),
+        out_shape=shapes,
+        compiler_params=pltpu.CompilerParams(vmem_limit_bytes=8 * MIB),
+        name="add_terms",
+    )(*[pltpu.with_memory_space_constraint(array, pltpu.VMEM) for array in arrays])
 
 
 def reduce_scatter(a, b, n_phi, n_gz, filler):
-    low, high = slice(n_gz // 2), slice(n_gz // 2, None)
+    every, low, high = slice(None), slice(n_gz // 2), slice(n_gz // 2, None)
     a = [a[0], swap(a[1], "phi", 1)]
     b = [b[0], swap(b[1], "phi", 1)]
-    sent = (add(a, 1), add(b, slice(None), high))
-    got = (swap(sent[0], "phi", 2), swap(sent[1], "gz", 1))
-    a_got, b_got = filler.beside(sent, got)
-    a = [term[0] for term in a] + [a_got]
-    b = [term[:, low] for term in b] + [b_got]
-    sent = (add(a, high), add(b, 1))
-    got = (swap(sent[0], "gz", 1), swap(sent[1], "phi", 2))
-    a_got, b_got = filler.beside(sent, got)
-    a = [term[low] for term in a] + [a_got]
-    b = [term[0] for term in b] + [b_got]
-    v = [jnp.concatenate([add(a), add(b)], axis=1)]
+    (a_sent,) = sums([[(term, (1,)) for term in a]])
+    (b_sent,) = sums([[(term, (every, high)) for term in b]])
+    got = (swap(a_sent, "phi", 2), swap(b_sent, "gz", 1))
+    a_got, b_got = filler.beside((a_sent, b_sent), got)
+    a_sent, b_sent = sums(
+        [[(term, (0, high)) for term in a] + [(a_got, (high,))]],
+        [[(term, (1, low)) for term in b] + [(b_got, (1,))]],
+    )
+    got = (swap(a_sent, "gz", 1), swap(b_sent, "phi", 2))
+    a_new, b_new = filler.beside((a_sent, b_sent), got)
+
+    def rest(i, size):
+        rows = slice(i * size, (i + 1) * size)
+        return [
+            [(term, (0, rows)) for term in a] + [(a_got, (rows,)), (a_new, (rows,))],
+            [(term, (0, rows)) for term in b] + [(b_got, (0, rows)), (b_new, (rows,))],
+        ]
+
+    left = n_gz // 2
     for bits in gz_groups(n_gz):
         count = 1 << len(bits)
-        size = v[0].shape[0] // count
-        sent = [add(v, slice(i * size, (i + 1) * size)) for i in range(1, count)]
+        size = left // count
+        v, *sent = sums(*[rest(i, size) for i in range(count)])
         got = [swap(part, "gz", group_bits(i, bits)) for i, part in enumerate(sent, 1)]
-        v = [term[:size] for term in v] + list(filler.beside(sent, got, count // 2))
-    return add(v, 0)
+        terms = [v, *filler.beside(sent, got, count // 2)]
+        rest = lambda i, size: [[(term, (slice(i * size, (i + 1) * size),)) for term in terms]]
+        left = size
+    return functools.reduce(jnp.add, terms)[0]
 
 
 def all_gather(v, n_phi, n_gz, filler):
@@ -432,41 +475,94 @@
     ]
 
 
+def tables_kernel(
+    z_modes, phi_modes, bias, weight_ref, modes_ref, local_ref, bias_ref, phi_ref, z_ref, wr_ref, wi_ref,
+    *, n_gz, n_phi, scale
+):
+    channels = weight_ref.shape[0]
+    rows = 8 * channels
+    row = lax.broadcasted_iota(jnp.int32, (rows, channels), 0)
+    copy = (row // 8 == lax.broadcasted_iota(jnp.int32, (rows, channels), 1)).astype(bf16)
+    row = lax.broadcasted_iota(jnp.int32, (rows, rows), 0)
+    column = lax.broadcasted_iota(jnp.int32, (rows, rows), 1)
+    same = lax.rem(row, 8) == lax.rem(column, 8)
+    last = (((1,), (1,)), ((), ()))
+    for part, w in enumerate(halves(weight_ref[...])):
+        wide = lax.dot_general(copy, w, last, preferred_element_type=f32).astype(bf16)
+        wide = lax.dot_general(wide, copy, last, preferred_element_type=f32)
+        wide = jnp.where(same, wide, 0.0).astype(bf16)
+        local_ref[part * rows : (part + 1) * rows, :rows] = wide
+        local_ref[part * rows : (part + 1) * rows, rows:] = wide
+    for o in range(channels):
+        bias_ref[o] = jnp.full(bias_ref.shape[1:], bias[o], f32)
+
+    lanes = phi_ref.shape[0] // 3
+    phi_local = phi_ref.shape[1] // 2
+    kp = lanes // 2
+    n = n_phi * phi_local
+    mode = modes_by_row(phi_modes, phi_slots(n_phi), kp, phi_local)
+    position = lax.axis_index("phi") * phi_local + lax.broadcasted_iota(jnp.int32, (kp, phi_local), 1)
+    turns = position * mode
+    cosine = halves(cosines(turns, n))
+    sine = halves(cosines(turns + 3 * n // 4, n))
+    minus = halves(cosines(turns + n // 4, n))
+    for i, part in enumerate((0, 0, 1)):
+        at = i * lanes
+        phi_ref[at : at + kp, :phi_local] = cosine[part]
+        phi_ref[at : at + kp, phi_local:] = sine[part]
+        phi_ref[at + kp : at + lanes, :phi_local] = minus[part]
+        phi_ref[at + kp : at + lanes, phi_local:] = cosine[part]
+
+    z_local, both = z_ref.shape[0], z_ref.shape[1] // 3
+    kz = both // 2
+    n = n_gz * z_local
+    mode = modes_by_lane(z_modes, gz_slots(n_gz), kz, both)
+    quarter = jnp.where(lax.broadcasted_iota(jnp.int32, (1, both), 1) < kz, 0, n // 4)
+    position = lax.axis_index("gz") * z_local + lax.broadcasted_iota(jnp.int32, (z_local, both), 0)
+    high, low = halves(cosines(position * mode + quarter, n))
+    for i, part in enumerate((high, low, high)):
+        z_ref[:, i * both : (i + 1) * both] = part
+
+    width = kp // n_phi
+    lane = lax.broadcasted_iota(jnp.int32, (width, lanes), 1)
+    copy = (lax.rem(lane, width) == lax.broadcasted_iota(jnp.int32, (width, lanes), 0)).astype(bf16)
+    sign = jnp.where(lax.broadcasted_iota(jnp.int32, (1, lanes), 1) < kp, -scale, scale).astype(f32)
+    for part, (out, factor) in enumerate(((wr_ref, scale), (wi_ref, sign))):
+        left = modes_ref[part]
+        total = jnp.zeros(out.shape, f32)
+        for _ in range(3):
+            term = left.astype(bf16)
+            left = left - term.astype(f32)
+            total = total + dot(term, copy)
+        out[...] = total * factor
+
+
 def tables(spectral_weight, local_weight, bias_term, z_modes, phi_modes, z_local, phi_local):
     n_gz = lax.axis_size("gz")
     n_phi = lax.axis_size("phi")
     kz, kp = z_modes.shape[0], phi_modes.shape[0]
-    width = kp // n_phi
-    z_total, phi_total = z_local * n_gz, phi_local * n_phi
-    my_gz = lax.axis_index("gz")
-    my_phi = lax.axis_index("phi")
-
-    z_global = my_gz * z_local + jnp.arange(z_local, dtype=jnp.int32)
-    phi_global = my_phi * phi_local + jnp.arange(phi_local, dtype=jnp.int32)
-    z_kept = z_modes.reshape(n_gz, -1)[my_gz ^ jnp.array(gz_order(n_gz), jnp.int32)].reshape(-1)
-    phi_kept = phi_modes.reshape(n_phi, -1)[my_phi ^ jnp.arange(n_phi, dtype=jnp.int32)].reshape(-1)
-    zc, zs = angles(z_global, z_kept, z_total)
-    pc, ps = angles(phi_global, phi_kept, phi_total)
-    high, low = split(jnp.concatenate([zc, -zs], axis=1))
-    z_back = jnp.concatenate([high, low, high], 1)
-    high, low = split(
-        jnp.concatenate(
-            [jnp.concatenate([pc.T, ps.T], 1), jnp.concatenate([-ps.T, pc.T], 1)], 0
-        )
-    )
-    phi_back = jnp.concatenate([high, high, low], 0)
-
-    high, low = split(jnp.kron(local_weight.T, jnp.eye(8, dtype=f32)))
-    local_table = jnp.concatenate(
-        [jnp.concatenate([high, high], 1), jnp.concatenate([low, low], 1)], 0
-    )
-    wide_bias = jnp.broadcast_to(bias_term[:, None, None], (bias_term.shape[0], 8, phi_local))
-
-    scale = (1.0 / math.sqrt(z_total * phi_total)) * (2.0 / math.sqrt(kz * kp))
-    spread = jnp.tile(jnp.eye(width, dtype=f32), (1, 2 * n_phi)) * scale
-    sign = jnp.where(jnp.arange(2 * kp) < kp, -1.0, 1.0).astype(f32)
-    wide = jnp.dot(spectral_weight, spread, precision=lax.Precision.HIGHEST)
-    return local_table, wide_bias, phi_back, z_back, wide[0], wide[1] * sign
+    channels = local_weight.shape[0]
+    depth, width = spectral_weight.shape[-2:]
+    rows = channels * channels * depth
+    scale = (1.0 / math.sqrt(z_local * n_gz * phi_local * n_phi)) * (2.0 / math.sqrt(kz * kp))
+    vmem, smem = pl.BlockSpec(memory_space=pltpu.VMEM), pl.BlockSpec(memory_space=pltpu.SMEM)
+    *result, wr, wi = pl.pallas_call(
+        functools.partial(tables_kernel, n_gz=n_gz, n_phi=n_phi, scale=scale),
+        in_specs=[smem, smem, smem, vmem, vmem],
+        out_specs=[vmem] * 6,
+        out_shape=[
+            jax.ShapeDtypeStruct((16 * channels, 16 * channels), bf16),
+            jax.ShapeDtypeStruct((channels, 8, phi_local), f32),
+            jax.ShapeDtypeStruct((6 * kp, 2 * phi_local), bf16),
+            jax.ShapeDtypeStruct((z_local, 6 * kz), bf16),
+            jax.ShapeDtypeStruct((rows, 2 * kp), f32),
+            jax.ShapeDtypeStruct((rows, 2 * kp), f32),
+        ],
+        compiler_params=pltpu.CompilerParams(vmem_limit_bytes=16 * MIB),
+        name="small_tables",
+    )(z_modes, phi_modes, bias_term, local_weight, spectral_weight.reshape(2, rows, width))
+    shape = (channels, channels, depth, 2 * kp)
+    return *result, wr.reshape(shape), wi.reshape(shape)
 
 
 def body(field, field_tangent, spectral_weight, local_weight, bias_term, z_modes, phi_modes):

time: 139 us -> 130 us (0.935)
  other arithmetic: 11.5 us -> 0.14 us
  waiting for transfers between devices: 24.8 us -> 31.5 us
  local copies, waits for them, and re-layouts: 6.88 us -> 2.31 us
  Pallas kernels: 70.9 us -> 73.5 us
  matrix products: 1.77 us -> 0 us
    add x8 -> x0, other arithmetic: 7.48 us -> none  [the longest x6 7.47 us: add(): return functools.reduce(jnp.add, [term[index] for term in terms])]
    ppermute x20, waiting for transfers between devices: 24.8 us -> 31.5 us  [swap(): return lax.ppermute(x, axis, [(i, i ^ bit) for i in range(count)])]
    pallas_call x0 -> x5, Pallas kernels: none -> 3.11 us  [the longest x1 2.75 us: tables(): pl.pallas_call(functools.partial(tables_kernel, n_gz=n_gz, n_phi=n_phi, s...]
    mul x4 -> x0, local copies, waits for them, and re-layouts: 1.9 us -> none  [the longest x1 1.65 us: tables(): high, low = split(jnp.kron(local_weight.T, jnp.eye(8, dtype=f32)))]
    dot_general x1 -> x0, matrix products: 1.77 us -> none  [tables(): wide = jnp.dot(spectral_weight, spread, precision=lax.Precision.HIGHEST)]
    concatenate x4 -> x0, other arithmetic: 1.54 us -> none  [the longest x1 0.79 us: tables(): phi_back = jnp.concatenate([high, high, low], 0)]
    unnamed x39 -> x15, local copies, waits for them, and re-layouts: 3.34 us -> 2.19 us
  transfers between devices with their start and end apart: 20 -> 20, of which waited for: 12 -> 13; matrix products, arithmetic and copies ran while one was open for 10% -> 0% of each run, Pallas kernels for 18% -> 22%
where the time goes in v4:
time: 130 us
  Pallas kernels  73.5 us (57%)
  waiting for transfers between devices  31.5 us (24%)
  starting transfers between devices  21.5 us (17%)
  local copies, waits for them, and re-layouts  2.31 us (2%)
    ppermute x20, waiting for transfers between devices, swap(): return lax.ppermute(x, axis, [(i, i ^ bit) for i in range(count)])  31.5 us
    pallas_call x8, Pallas kernels, local_mix(): pl.pallas_call(local_kernel, grid=(steps,), in_specs=[block, block, pl.Bl...  25.3 us
    pallas_call x1, Pallas kernels, inverse(): pl.pallas_call(functools.partial(inverse_kernel, n_phi=n_phi, width=width...  25 us
    ppermute x20, starting transfers between devices, swap(): return lax.ppermute(x, axis, [(i, i ^ bit) for i in range(count)])  21.5 us
    pallas_call x1, Pallas kernels, forward(): pl.pallas_call(functools.partial(forward_kernel, n_gz=n_gz, n_phi=n_phi),...  19.6 us
    pallas_call x1, Pallas kernels, tables(): pl.pallas_call(functools.partial(tables_kernel, n_gz=n_gz, n_phi=n_phi, s...  2.75 us
  transfers between devices with their start and end apart: 20, of which 13 were waited for; matrix products, arithmetic and copies ran while one was open for 0% of the time, Pallas kernels for 22%

profile of v4, /device:TPU:0, one launch (start us, length us, event | category | flops | bytes accessed | tf_op | source)
XLA Modules:
  0.0 129.8 jit_solution(4582885180754593008)
XLA Ops:
  0.6 0.0 copy-start.2
  0.6 0.6 copy-done.2
  1.3 0.7 copy-done.3
  1.9 19.6 %forward_transform.1 = (f32[2,8,8,2,8,128]{5,4,3,2,1,0:T(8,128)S(1)}, f32[2,8,8,2,8,128]{5,4,3,2,1,0:T(8,128)S(1)}, f32[2,8,8,2,8,128]{5,4,3,2,1,0:T(8,128)S(1)}, f32[2,8,8,2,8,128]{5,4,3,2,1,0:T(8,128)S(1)}) custom-call(s32[64]{0:T(128)S(1)} %copy-done.2, s32[64]{0:T(128)S(1)} %copy-done.3, f32[16,4,256,256]{3,2,1,0:T(8,128)} %x_ref.9, ...), custom_call_target="tpu_custom_call" | custom-call | flops 12884901888 | bytes 33554432 | tf_op jit(solution)/shard_map/forward_transform/pallas_call | solution.py:172
  21.6 0.5 collective-permute-start
  22.1 0.1 collective-permute-start.2
  22.2 2.2 %collective-permute-done.refs_1_ = f32[2,8,8,2,8,128]{5,4,3,2,1,0:T(8,128)S(1)} collective-permute-done((f32[2,8,8,2,8,128]{5,4,3,2,1,0:T(8,128)S(1)}, f32[2,8,8,2,8,128]{5,4,3,2,1,0:T(8,128)S(1)}, u32[]{:S(2)}, u32[]{:S(2)}) %collective-permute-start) | collective-permute-done | bytes 1048608 | tf_op jit(solution)/shard_map/ppermute | solution.py:343
  24.4 0.1 add_terms.4
  24.5 2.9 %collective-permute-start.1 = (f32[8,8,2,8,128]{4,3,2,1,0:T(8,128)S(1)}, f32[8,8,2,8,128]{4,3,2,1,0:T(8,128)S(1)}, u32[]{:S(2)}, u32[]{:S(2)}) collective-permute-start(f32[8,8,2,8,128]{4,3,2,1,0:T(8,128)S(1)} %add_terms.4), channel_id=1, source_target_pairs={{0,2},{1,3},{2,0},{3,1},{4,6},{5,7},{6,4},{7,5},{8,10},{9,11},{10,... | collective-permute-start | bytes 1572872 | tf_op jit(solution)/shard_map/ppermute | solution.py:343
  27.4 0.0 collective-permute-done.2.refs_1_.refs_4_.refs_5_
  27.4 0.1 add_terms.5
  27.4 1.6 %collective-permute-start.3 = (f32[2,4,8,2,8,128]{5,4,3,2,1,0:T(8,128)S(1)}, f32[2,4,8,2,8,128]{5,4,3,2,1,0:T(8,128)S(1)}, u32[]{:S(2)}, u32[]{:S(2)}) collective-permute-start(f32[2,4,8,2,8,128]{5,4,3,2,1,0:T(8,128)S(1)} %add_terms.5), channel_id=1, source_target_pairs={{0,4},{4,0},{8,12},{12,8},{16,20},{20,16},{24,28},{28,24},{1,5},{5... | collective-permute-start | bytes 1572872 | tf_op jit(solution)/shard_map/ppermute | solution.py:343
  29.0 0.0 copy-done
  29.0 0.0 copy-done.1
  29.0 2.7 %small_tables.1 = (bf16[256,256]{1,0:T(8,128)(2,1)S(1)}, f32[16,8,256]{2,1,0:T(8,128)S(1)}, bf16[384,512]{1,0:T(8,128)(2,1)S(1)}, bf16[256,384]{1,0:T(8,128)(2,1...) custom-call(s32[64]{0:T(128)S(1)} %copy-done.2, s32[64]{0:T(128)S(1)} %copy-done.3, f32[16]{0:T(128)S(1)} %copy-done.4, ...), custom_call_target="tpu_custom_call" | custom-call | tf_op jit(solution)/shard_map/small_tables/pallas_call | solution.py:549
  31.8 7.8 %collective-permute-done.1.refs_2_ = f32[8,8,2,8,128]{4,3,2,1,0:T(8,128)S(1)} collective-permute-done((f32[8,8,2,8,128]{4,3,2,1,0:T(8,128)S(1)}, f32[8,8,2,8,128]{4,3,2,1,0:T(8,128)S(1)}, u32[]{:S(2)}, u32[]{:S(2)}) %collective-permute-start.1) | collective-permute-done | bytes 524320 | tf_op jit(solution)/shard_map/ppermute | solution.py:343
  39.6 1.6 %collective-permute-done.3.refs_5_.refs_6_ = f32[2,4,8,2,8,128]{5,4,3,2,1,0:T(8,128)S(1)} collective-permute-done((f32[2,4,8,2,8,128]{5,4,3,2,1,0:T(8,128)S(1)}, f32[2,4,8,2,8,128]{5,4,3,2,1,0:T(8,128)S(1)}, u32[]{:S(2)}, u32[]{:S(2)}) %collective-permute-start.3) | collective-permute-done | bytes 524320 | tf_op jit(solution)/shard_map/ppermute | solution.py:343
  41.2 0.1 add_terms.6
  41.3 1.7 %collective-permute-start.4 = (f32[4,8,2,8,128]{4,3,2,1,0:T(8,128)S(1)}, f32[4,8,2,8,128]{4,3,2,1,0:T(8,128)S(1)}, u32[]{:S(2)}, u32[]{:S(2)}) collective-permute-start(f32[4,8,2,8,128]{4,3,2,1,0:T(8,128)S(1)} %get-tuple-element.113), channel_id=1, source_target_pairs={{0,4},{4,0},{8,12},{12,8},{16,20},{20,16},{24,28},{28,24},{1,5},{5... | collective-permute-start | bytes 786440 | tf_op jit(solution)/shard_map/ppermute | solution.py:343
  43.0 1.5 %collective-permute-start.5 = (f32[4,8,2,8,128]{4,3,2,1,0:T(8,128)S(1)}, f32[4,8,2,8,128]{4,3,2,1,0:T(8,128)S(1)}, u32[]{:S(2)}, u32[]{:S(2)}) collective-permute-start(f32[4,8,2,8,128]{4,3,2,1,0:T(8,128)S(1)} %get-tuple-element.114), channel_id=1, source_target_pairs={{0,2},{1,3},{2,0},{3,1},{4,6},{5,7},{6,4},{7,5},{8,10},{9,11},{10,... | collective-permute-start | bytes 786440 | tf_op jit(solution)/shard_map/ppermute | solution.py:343
  44.5 3.3 %local_mix.8 = (f32[16,128,256]{2,1,0:T(8,128)S(1)}, f32[16,128,256]{2,1,0:T(8,128)S(1)}) custom-call(f32[16,4,256,256]{3,2,1,0:T(8,128)} %x_ref.9, f32[16,4,256,256]{3,2,1,0:T(8,128)} %t_ref.9, bf16[256,256]{1,0:T(8,128)(2,1)S(1)} %get-tuple-element.117.w_ref, f32[16,8,256]{2,1,0:T(8,128)S(1)} %get-tuple-element.118.bias_ref), custom_call_target="tpu_custom_call" | custom-call | flops 536870912 | bytes 4194304 | tf_op jit(solution)/shard_map/local_mix/pallas_call | solution.py:215
  47.8 0.8 collective-permute-done.4.refs_3_
  48.6 1.5 %collective-permute-done.5.refs_7_ = f32[4,8,2,8,128]{4,3,2,1,0:T(8,128)S(1)} collective-permute-done((f32[4,8,2,8,128]{4,3,2,1,0:T(8,128)S(1)}, f32[4,8,2,8,128]{4,3,2,1,0:T(8,128)S(1)}, u32[]{:S(2)}, u32[]{:S(2)}) %collective-permute-start.5) | collective-permute-done | bytes 262176 | tf_op jit(solution)/shard_map/ppermute | solution.py:343
  50.1 0.2 add_terms.7
  50.3 2.7 %collective-permute-start.6 = (f32[1,16,2,8,128]{4,3,2,1,0:T(8,128)S(1)}, f32[1,16,2,8,128]{4,3,2,1,0:T(8,128)S(1)}, u32[]{:S(2)}, u32[]{:S(2)}) collective-permute-start(f32[1,16,2,8,128]{4,3,2,1,0:T(8,128)S(1)} %get-tuple-element.124), channel_id=1, source_target_pairs={{0,16},{4,20},{8,24},{12,28},{16,0},{20,4},{24,8},{28,12},{1,17},{... | collective-permute-start | bytes 393224 | tf_op jit(solution)/shard_map/ppermute | solution.py:343
  53.0 1.5 %collective-permute-start.7 = (f32[1,16,2,8,128]{4,3,2,1,0:T(8,128)S(1)}, f32[1,16,2,8,128]{4,3,2,1,0:T(8,128)S(1)}, u32[]{:S(2)}, u32[]{:S(2)}) collective-permute-start(f32[1,16,2,8,128]{4,3,2,1,0:T(8,128)S(1)} %get-tuple-element.125), channel_id=1, source_target_pairs={{0,8},{4,12},{8,0},{12,4},{16,24},{20,28},{24,16},{28,20},{1,9},{5... | collective-permute-start | bytes 393224 | tf_op jit(solution)/shard_map/ppermute | solution.py:343
  54.5 0.3 collective-permute-start.8
  54.7 3.1 %local_mix.10 = (f32[16,128,256]{2,1,0:T(8,128)S(1)}, f32[16,128,256]{2,1,0:T(8,128)S(1)}) custom-call(f32[16,4,256,256]{3,2,1,0:T(8,128)} %x_ref.9, f32[16,4,256,256]{3,2,1,0:T(8,128)} %t_ref.9, bf16[256,256]{1,0:T(8,128)(2,1)S(1)} %get-tuple-element.117.w_ref, f32[16,8,256]{2,1,0:T(8,128)S(1)} %get-tuple-element.118.bias_ref), custom_call_target="tpu_custom_call" | custom-call | flops 536870912 | bytes 4194304 | tf_op jit(solution)/shard_map/local_mix/pallas_call | solution.py:215
  57.9 3.2 %local_mix.9 = (f32[16,128,256]{2,1,0:T(8,128)S(1)}, f32[16,128,256]{2,1,0:T(8,128)S(1)}) custom-call(f32[16,4,256,256]{3,2,1,0:T(8,128)} %x_ref.9, f32[16,4,256,256]{3,2,1,0:T(8,128)} %t_ref.9, bf16[256,256]{1,0:T(8,128)(2,1)S(1)} %get-tuple-element.117.w_ref, f32[16,8,256]{2,1,0:T(8,128)S(1)} %get-tuple-element.118.bias_ref), custom_call_target="tpu_custom_call" | custom-call | flops 536870912 | bytes 4194304 | tf_op jit(solution)/shard_map/local_mix/pallas_call | solution.py:215
  61.0 0.6 collective-permute-done.6
  61.6 0.0 collective-permute-done.7
  61.6 0.0 collective-permute-done.8
  61.7 0.4 mode_mix.1
  62.1 3.6 %collective-permute-start.11 = (f32[1,16,2,8,128]{4,3,2,1,0:T(8,128)S(1)}, f32[1,16,2,8,128]{4,3,2,1,0:T(8,128)S(1)}, u32[]{:S(2)}, u32[]{:S(2)}) collective-permute-start(f32[1,16,2,8,128]{4,3,2,1,0:T(8,128)S(1)} %bitcast.15), channel_id=1, source_target_pairs={{0,24},{4,28},{8,16},{12,20},{16,8},{20,12},{24,0},{28,4},{1,25},{... | collective-permute-start | bytes 393224 | tf_op jit(solution)/shard_map/ppermute | solution.py:343
  65.6 1.1 collective-permute-start.10
  66.7 0.0 collective-permute-start.9
  66.7 3.1 %local_mix.12 = (f32[16,128,256]{2,1,0:T(8,128)S(1)}, f32[16,128,256]{2,1,0:T(8,128)S(1)}) custom-call(f32[16,4,256,256]{3,2,1,0:T(8,128)} %x_ref.9, f32[16,4,256,256]{3,2,1,0:T(8,128)} %t_ref.9, bf16[256,256]{1,0:T(8,128)(2,1)S(1)} %get-tuple-element.117.w_ref, f32[16,8,256]{2,1,0:T(8,128)S(1)} %get-tuple-element.118.bias_ref), custom_call_target="tpu_custom_call" | custom-call | flops 536870912 | bytes 4194304 | tf_op jit(solution)/shard_map/local_mix/pallas_call | solution.py:215
  69.8 3.2 %local_mix.11 = (f32[16,128,256]{2,1,0:T(8,128)S(1)}, f32[16,128,256]{2,1,0:T(8,128)S(1)}) custom-call(f32[16,4,256,256]{3,2,1,0:T(8,128)} %x_ref.9, f32[16,4,256,256]{3,2,1,0:T(8,128)} %t_ref.9, bf16[256,256]{1,0:T(8,128)(2,1)S(1)} %get-tuple-element.117.w_ref, f32[16,8,256]{2,1,0:T(8,128)S(1)} %get-tuple-element.118.bias_ref), custom_call_target="tpu_custom_call" | custom-call | flops 536870912 | bytes 4194304 | tf_op jit(solution)/shard_map/local_mix/pallas_call | solution.py:215
  73.0 0.0 collective-permute-done.11
  73.0 0.0 collective-permute-done.10
  73.0 3.0 %collective-permute-done.9 = f32[1,16,2,8,128]{4,3,2,1,0:T(8,128)S(1)} collective-permute-done((f32[1,16,2,8,128]{4,3,2,1,0:T(8,128)S(1)}, f32[1,16,2,8,128]{4,3,2,1,0:T(8,128)S(1)}, u32[]{:S(2)}, u32[]{:S(2)}) %collective-permute-start.9) | collective-permute-done | bytes 131104 | tf_op jit(solution)/shard_map/ppermute | solution.py:343
  76.1 0.1 collective-permute-start.14
  76.1 0.1 slice_bitcast_fusion
  76.2 1.8 %collective-permute-start.13 = (f32[4,8,2,8,128]{4,3,2,1,0:T(8,128)S(1)}, f32[4,8,2,8,128]{4,3,2,1,0:T(8,128)S(1)}, u32[]{:S(2)}, u32[]{:S(2)}) collective-permute-start(f32[4,8,2,8,128]{4,3,2,1,0:T(8,128)S(1)} %get-tuple-element.192), channel_id=1, source_target_pairs={{0,2},{1,3},{2,0},{3,1},{4,6},{5,7},{6,4},{7,5},{8,10},{9,11},{10,... | collective-permute-start | bytes 786440 | tf_op jit(solution)/shard_map/ppermute | solution.py:343
  78.1 0.6 collective-permute-start.12
  78.6 3.1 %local_mix.13 = (f32[16,128,256]{2,1,0:T(8,128)S(1)}, f32[16,128,256]{2,1,0:T(8,128)S(1)}) custom-call(f32[16,4,256,256]{3,2,1,0:T(8,128)} %x_ref.9, f32[16,4,256,256]{3,2,1,0:T(8,128)} %t_ref.9, bf16[256,256]{1,0:T(8,128)(2,1)S(1)} %get-tuple-element.117.w_ref, f32[16,8,256]{2,1,0:T(8,128)S(1)} %get-tuple-element.118.bias_ref), custom_call_target="tpu_custom_call" | custom-call | flops 536870912 | bytes 4194304 | tf_op jit(solution)/shard_map/local_mix/pallas_call | solution.py:215
  81.8 3.3 %collective-permute-done.13 = f32[4,8,2,8,128]{4,3,2,1,0:T(8,128)S(1)} collective-permute-done((f32[4,8,2,8,128]{4,3,2,1,0:T(8,128)S(1)}, f32[4,8,2,8,128]{4,3,2,1,0:T(8,128)S(1)}, u32[]{:S(2)}, u32[]{:S(2)}) %collective-permute-start.13) | collective-permute-done | bytes 262176 | tf_op jit(solution)/shard_map/ppermute | solution.py:343
  85.0 1.5 %collective-permute-done.12 = f32[4,8,2,8,128]{4,3,2,1,0:T(8,128)S(1)} collective-permute-done((f32[4,8,2,8,128]{4,3,2,1,0:T(8,128)S(1)}, f32[4,8,2,8,128]{4,3,2,1,0:T(8,128)S(1)}, u32[]{:S(2)}, u32[]{:S(2)}) %collective-permute-start.12) | collective-permute-done | bytes 262176 | tf_op jit(solution)/shard_map/ppermute | solution.py:343
  86.5 0.0 collective-permute-done.14.refs_4_
  86.6 0.1 collective-permute-start.17
  86.7 0.4 collective-permute-start.15
  87.1 0.6 collective-permute-start.16
  87.8 3.1 %local_mix.15 = (f32[16,128,256]{2,1,0:T(8,128)S(1)}, f32[16,128,256]{2,1,0:T(8,128)S(1)}) custom-call(f32[16,4,256,256]{3,2,1,0:T(8,128)} %x_ref.9, f32[16,4,256,256]{3,2,1,0:T(8,128)} %t_ref.9, bf16[256,256]{1,0:T(8,128)(2,1)S(1)} %get-tuple-element.117.w_ref, f32[16,8,256]{2,1,0:T(8,128)S(1)} %get-tuple-element.118.bias_ref), custom_call_target="tpu_custom_call" | custom-call | flops 536870912 | bytes 4194304 | tf_op jit(solution)/shard_map/local_mix/pallas_call | solution.py:215
  90.9 3.2 %local_mix.14 = (f32[16,128,256]{2,1,0:T(8,128)S(1)}, f32[16,128,256]{2,1,0:T(8,128)S(1)}) custom-call(f32[16,4,256,256]{3,2,1,0:T(8,128)} %x_ref.9, f32[16,4,256,256]{3,2,1,0:T(8,128)} %t_ref.9, bf16[256,256]{1,0:T(8,128)(2,1)S(1)} %get-tuple-element.117.w_ref, f32[16,8,256]{2,1,0:T(8,128)S(1)} %get-tuple-element.118.bias_ref), custom_call_target="tpu_custom_call" | custom-call | flops 536870912 | bytes 4194304 | tf_op jit(solution)/shard_map/local_mix/pallas_call | solution.py:215
  94.1 0.0 collective-permute-done.17.refs_5_
  94.1 7.0 %collective-permute-done.15.refs_2_ = f32[2,4,8,2,8,128]{5,4,3,2,1,0:T(8,128)S(1)} collective-permute-done((f32[2,4,8,2,8,128]{5,4,3,2,1,0:T(8,128)S(1)}, f32[2,4,8,2,8,128]{5,4,3,2,1,0:T(8,128)S(1)}, u32[]{:S(2)}, u32[]{:S(2)}) %collective-permute-start.15) | collective-permute-done | bytes 524320 | tf_op jit(solution)/shard_map/ppermute | solution.py:343
  101.1 0.2 collective-permute-done.16.refs_3_
  101.2 0.0 collective-permute-start.18
  101.2 0.5 collective-permute-start.19
  101.8 1.4 %collective-permute-done.18.refs_6_ = f32[2,4,8,2,8,128]{5,4,3,2,1,0:T(8,128)S(1)} collective-permute-done((f32[2,4,8,2,8,128]{5,4,3,2,1,0:T(8,128)S(1)}, f32[2,4,8,2,8,128]{5,4,3,2,1,0:T(8,128)S(1)}, u32[]{:S(2)}, u32[]{:S(2)}) %collective-permute-start.18) | collective-permute-done | bytes 524320 | tf_op jit(solution)/shard_map/ppermute | solution.py:343
  103.2 0.7 collective-permute-done.19.refs_7_
  103.9 0.0 copy-done.5
  103.9 0.8 copy-done.6
  104.8 25.0 %inverse_transform.1 = (f32[16,4,256,256]{3,2,1,0:T(8,128)}, f32[16,4,256,256]{3,2,1,0:T(8,128)}) custom-call(f32[4,16,2,8,128]{4,3,2,1,0:T(8,128)S(1)} %pad_maximum_fusion.refs_0_, f32[4,16,2,8,128]{4,3,2,1,0:T(8,128)S(1)} %constant_dynamic-update-slice_fusion.refs_1_, f32[2,4,8,2,8,128]{5,4,3,2,1,0:T(8,128)S(1)} %collective-permute-done.15.refs_2_, ...), custom_call_target="tpu_custom_call" | custom-call | flops 6710886400 | bytes 67108864 | tf_op jit(solution)/shard_map/inverse_transform/pallas_call | solution.py:322
  (13 shorter events, 0.2 us)
Async XLA Ops:
  0.6 0.7 copy-start.2
  1.3 0.7 copy-start.3
  21.6 2.8 %collective-permute-start = (f32[2,8,8,2,8,128]{5,4,3,2,1,0:T(8,128)S(1)}, f32[2,8,8,2,8,128]{5,4,3,2,1,0:T(8,128)S(1)}, u32[]{:S(2)}, u32[]{:S(2)}) collective-permute-start(f32[2,8,8,2,8,128]{5,4,3,2,1,0:T(8,128)S(1)} %get-tuple-element.97), channel_id=1, source_target_pairs={{0,1},{1,0},{2,3},{3,2},{4,5},{5,4},{6,7},{7,6},{8,9},{9,8},{10,11... | collective-permute-start | bytes 3145736 | tf_op jit(solution)/shard_map/ppermute | solution.py:343
  22.1 5.3 %collective-permute-start.2 = (f32[2,8,8,2,8,128]{5,4,3,2,1,0:T(8,128)S(1)}, f32[2,8,8,2,8,128]{5,4,3,2,1,0:T(8,128)S(1)}, u32[]{:S(2)}, u32[]{:S(2)}) collective-permute-start(f32[2,8,8,2,8,128]{5,4,3,2,1,0:T(8,128)S(1)} %get-tuple-element.99), channel_id=1, source_target_pairs={{0,1},{1,0},{2,3},{3,2},{4,5},{5,4},{6,7},{7,6},{8,9},{9,8},{10,11... | collective-permute-start | bytes 3145736 | tf_op jit(solution)/shard_map/ppermute | solution.py:343
  24.4 4.6 %copy-start = (f32[2,16,16,8,16]{4,3,2,1,0:T(8,128)S(1)}, f32[2,16,16,8,16]{4,3,2,1,0:T(8,128)}, u32[]{:S(2)}) copy-start(f32[2,16,16,8,16]{4,3,2,1,0:T(8,128)} %param.9) | copy-start | bytes 786436
  24.4 4.6 %copy-start.1 = (f32[16,16]{1,0:T(8,128)S(1)}, f32[16,16]{1,0:T(8,128)}, u32[]{:S(2)}) copy-start(f32[16,16]{1,0:T(8,128)} %weight_ref) | copy-start | bytes 3076
  24.4 4.7 %copy-start.4 = (f32[16]{0:T(128)S(1)}, f32[16]{0:T(128)}, u32[]{:S(2)}) copy-start(f32[16]{0:T(128)} %bias) | copy-start | bytes 196
  24.5 15.2 %collective-permute-start.1 = (f32[8,8,2,8,128]{4,3,2,1,0:T(8,128)S(1)}, f32[8,8,2,8,128]{4,3,2,1,0:T(8,128)S(1)}, u32[]{:S(2)}, u32[]{:S(2)}) collective-permute-start(f32[8,8,2,8,128]{4,3,2,1,0:T(8,128)S(1)} %add_terms.4), channel_id=1, source_target_pairs={{0,2},{1,3},{2,0},{3,1},{4,6},{5,7},{6,4},{7,5},{8,10},{9,11},{10,... | collective-permute-start | bytes 1572872 | tf_op jit(solution)/shard_map/ppermute | solution.py:343
  27.4 13.8 %collective-permute-start.3 = (f32[2,4,8,2,8,128]{5,4,3,2,1,0:T(8,128)S(1)}, f32[2,4,8,2,8,128]{5,4,3,2,1,0:T(8,128)S(1)}, u32[]{:S(2)}, u32[]{:S(2)}) collective-permute-start(f32[2,4,8,2,8,128]{5,4,3,2,1,0:T(8,128)S(1)} %add_terms.5), channel_id=1, source_target_pairs={{0,4},{4,0},{8,12},{12,8},{16,20},{20,16},{24,28},{28,24},{1,5},{5... | collective-permute-start | bytes 1572872 | tf_op jit(solution)/shard_map/ppermute | solution.py:343
  41.3 7.4 %collective-permute-start.4 = (f32[4,8,2,8,128]{4,3,2,1,0:T(8,128)S(1)}, f32[4,8,2,8,128]{4,3,2,1,0:T(8,128)S(1)}, u32[]{:S(2)}, u32[]{:S(2)}) collective-permute-start(f32[4,8,2,8,128]{4,3,2,1,0:T(8,128)S(1)} %get-tuple-element.113), channel_id=1, source_target_pairs={{0,4},{4,0},{8,12},{12,8},{16,20},{20,16},{24,28},{28,24},{1,5},{5... | collective-permute-start | bytes 786440 | tf_op jit(solution)/shard_map/ppermute | solution.py:343
  43.0 7.1 %collective-permute-start.5 = (f32[4,8,2,8,128]{4,3,2,1,0:T(8,128)S(1)}, f32[4,8,2,8,128]{4,3,2,1,0:T(8,128)S(1)}, u32[]{:S(2)}, u32[]{:S(2)}) collective-permute-start(f32[4,8,2,8,128]{4,3,2,1,0:T(8,128)S(1)} %get-tuple-element.114), channel_id=1, source_target_pairs={{0,2},{1,3},{2,0},{3,1},{4,6},{5,7},{6,4},{7,5},{8,10},{9,11},{10,... | collective-permute-start | bytes 786440 | tf_op jit(solution)/shard_map/ppermute | solution.py:343
  50.3 11.4 %collective-permute-start.6 = (f32[1,16,2,8,128]{4,3,2,1,0:T(8,128)S(1)}, f32[1,16,2,8,128]{4,3,2,1,0:T(8,128)S(1)}, u32[]{:S(2)}, u32[]{:S(2)}) collective-permute-start(f32[1,16,2,8,128]{4,3,2,1,0:T(8,128)S(1)} %get-tuple-element.124), channel_id=1, source_target_pairs={{0,16},{4,20},{8,24},{12,28},{16,0},{20,4},{24,8},{28,12},{1,17},{... | collective-permute-start | bytes 393224 | tf_op jit(solution)/shard_map/ppermute | solution.py:343
  53.0 8.7 %collective-permute-start.7 = (f32[1,16,2,8,128]{4,3,2,1,0:T(8,128)S(1)}, f32[1,16,2,8,128]{4,3,2,1,0:T(8,128)S(1)}, u32[]{:S(2)}, u32[]{:S(2)}) collective-permute-start(f32[1,16,2,8,128]{4,3,2,1,0:T(8,128)S(1)} %get-tuple-element.125), channel_id=1, source_target_pairs={{0,8},{4,12},{8,0},{12,4},{16,24},{20,28},{24,16},{28,20},{1,9},{5... | collective-permute-start | bytes 393224 | tf_op jit(solution)/shard_map/ppermute | solution.py:343
  54.5 7.2 %collective-permute-start.8 = (f32[1,16,2,8,128]{4,3,2,1,0:T(8,128)S(1)}, f32[1,16,2,8,128]{4,3,2,1,0:T(8,128)S(1)}, u32[]{:S(2)}, u32[]{:S(2)}) collective-permute-start(f32[1,16,2,8,128]{4,3,2,1,0:T(8,128)S(1)} %get-tuple-element.126), channel_id=1, source_target_pairs={{0,24},{4,28},{8,16},{12,20},{16,8},{20,12},{24,0},{28,4},{1,25},{... | collective-permute-start | bytes 393224 | tf_op jit(solution)/shard_map/ppermute | solution.py:343
  62.1 10.9 %collective-permute-start.11 = (f32[1,16,2,8,128]{4,3,2,1,0:T(8,128)S(1)}, f32[1,16,2,8,128]{4,3,2,1,0:T(8,128)S(1)}, u32[]{:S(2)}, u32[]{:S(2)}) collective-permute-start(f32[1,16,2,8,128]{4,3,2,1,0:T(8,128)S(1)} %bitcast.15), channel_id=1, source_target_pairs={{0,24},{4,28},{8,16},{12,20},{16,8},{20,12},{24,0},{28,4},{1,25},{... | collective-permute-start | bytes 393224 | tf_op jit(solution)/shard_map/ppermute | solution.py:343
  65.6 7.4 %collective-permute-start.10 = (f32[1,16,2,8,128]{4,3,2,1,0:T(8,128)S(1)}, f32[1,16,2,8,128]{4,3,2,1,0:T(8,128)S(1)}, u32[]{:S(2)}, u32[]{:S(2)}) collective-permute-start(f32[1,16,2,8,128]{4,3,2,1,0:T(8,128)S(1)} %bitcast.16), channel_id=1, source_target_pairs={{0,8},{4,12},{8,0},{12,4},{16,24},{20,28},{24,16},{28,20},{1,9},{5... | collective-permute-start | bytes 393224 | tf_op jit(solution)/shard_map/ppermute | solution.py:343
  66.7 9.3 %collective-permute-start.9 = (f32[1,16,2,8,128]{4,3,2,1,0:T(8,128)S(1)}, f32[1,16,2,8,128]{4,3,2,1,0:T(8,128)S(1)}, u32[]{:S(2)}, u32[]{:S(2)}) collective-permute-start(f32[1,16,2,8,128]{4,3,2,1,0:T(8,128)S(1)} %bitcast.17), channel_id=1, source_target_pairs={{0,16},{4,20},{8,24},{12,28},{16,0},{20,4},{24,8},{28,12},{1,17},{... | collective-permute-start | bytes 393224 | tf_op jit(solution)/shard_map/ppermute | solution.py:343
  76.1 10.4 %collective-permute-start.14 = (f32[4,16,2,8,128]{4,3,2,1,0:T(8,128)S(1)}, f32[4,16,2,8,128]{4,3,2,1,0:T(8,128)S(1)}, u32[]{:S(2)}, u32[]{:S(2)}) collective-permute-start(f32[4,16,2,8,128]{4,3,2,1,0:T(8,128)S(1)} %pad_maximum_fusion.refs_0_), channel_id=1, source_target_pairs={{0,1},{1,0},{2,3},{3,2},{4,5},{5,4},{6,7},{7,6},{8,9},{9,8},{10,11... | collective-permute-start | bytes 1572872 | tf_op jit(solution)/shard_map/ppermute | solution.py:343
  76.2 8.8 %collective-permute-start.13 = (f32[4,8,2,8,128]{4,3,2,1,0:T(8,128)S(1)}, f32[4,8,2,8,128]{4,3,2,1,0:T(8,128)S(1)}, u32[]{:S(2)}, u32[]{:S(2)}) collective-permute-start(f32[4,8,2,8,128]{4,3,2,1,0:T(8,128)S(1)} %get-tuple-element.192), channel_id=1, source_target_pairs={{0,2},{1,3},{2,0},{3,1},{4,6},{5,7},{6,4},{7,5},{8,10},{9,11},{10,... | collective-permute-start | bytes 786440 | tf_op jit(solution)/shard_map/ppermute | solution.py:343
  78.1 8.4 %collective-permute-start.12 = (f32[4,8,2,8,128]{4,3,2,1,0:T(8,128)S(1)}, f32[4,8,2,8,128]{4,3,2,1,0:T(8,128)S(1)}, u32[]{:S(2)}, u32[]{:S(2)}) collective-permute-start(f32[4,8,2,8,128]{4,3,2,1,0:T(8,128)S(1)} %get-tuple-element.193), channel_id=1, source_target_pairs={{0,4},{4,0},{8,12},{12,8},{16,20},{20,16},{24,28},{28,24},{1,5},{5... | collective-permute-start | bytes 786440 | tf_op jit(solution)/shard_map/ppermute | solution.py:343
  86.6 7.5 %collective-permute-start.17 = (f32[4,16,2,8,128]{4,3,2,1,0:T(8,128)S(1)}, f32[4,16,2,8,128]{4,3,2,1,0:T(8,128)S(1)}, u32[]{:S(2)}, u32[]{:S(2)}) collective-permute-start(f32[4,16,2,8,128]{4,3,2,1,0:T(8,128)S(1)} %constant_dynamic-update-slice_fusion.refs_1_), channel_id=1, source_target_pairs={{0,1},{1,0},{2,3},{3,2},{4,5},{5,4},{6,7},{7,6},{8,9},{9,8},{10,11... | collective-permute-start | bytes 1572872 | tf_op jit(solution)/shard_map/ppermute | solution.py:343
  86.7 14.4 %collective-permute-start.15 = (f32[2,4,8,2,8,128]{5,4,3,2,1,0:T(8,128)S(1)}, f32[2,4,8,2,8,128]{5,4,3,2,1,0:T(8,128)S(1)}, u32[]{:S(2)}, u32[]{:S(2)}) collective-permute-start(f32[2,4,8,2,8,128]{5,4,3,2,1,0:T(8,128)S(1)} %pad_maximum_fusion.1), channel_id=1, source_target_pairs={{0,2},{1,3},{2,0},{3,1},{4,6},{5,7},{6,4},{7,5},{8,10},{9,11},{10,... | collective-permute-start | bytes 1572872 | tf_op jit(solution)/shard_map/ppermute | solution.py:343
  87.1 14.1 %collective-permute-start.16 = (f32[2,4,8,2,8,128]{5,4,3,2,1,0:T(8,128)S(1)}, f32[2,4,8,2,8,128]{5,4,3,2,1,0:T(8,128)S(1)}, u32[]{:S(2)}, u32[]{:S(2)}) collective-permute-start(f32[2,4,8,2,8,128]{5,4,3,2,1,0:T(8,128)S(1)} %pad_maximum_fusion.2), channel_id=1, source_target_pairs={{0,4},{4,0},{8,12},{12,8},{16,20},{20,16},{24,28},{28,24},{1,5},{5... | collective-permute-start | bytes 1572872 | tf_op jit(solution)/shard_map/ppermute | solution.py:343
  101.2 1.9 %collective-permute-start.18 = (f32[2,4,8,2,8,128]{5,4,3,2,1,0:T(8,128)S(1)}, f32[2,4,8,2,8,128]{5,4,3,2,1,0:T(8,128)S(1)}, u32[]{:S(2)}, u32[]{:S(2)}) collective-permute-start(f32[2,4,8,2,8,128]{5,4,3,2,1,0:T(8,128)S(1)} %collective-permute-done.15.refs_2_), channel_id=1, source_target_pairs={{0,1},{1,0},{2,3},{3,2},{4,5},{5,4},{6,7},{7,6},{8,9},{9,8},{10,11... | collective-permute-start | bytes 1572872 | tf_op jit(solution)/shard_map/ppermute | solution.py:343
  101.2 2.7 %collective-permute-start.19 = (f32[2,4,8,2,8,128]{5,4,3,2,1,0:T(8,128)S(1)}, f32[2,4,8,2,8,128]{5,4,3,2,1,0:T(8,128)S(1)}, u32[]{:S(2)}, u32[]{:S(2)}) collective-permute-start(f32[2,4,8,2,8,128]{5,4,3,2,1,0:T(8,128)S(1)} %collective-permute-done.16.refs_3_), channel_id=1, source_target_pairs={{0,1},{1,0},{2,3},{3,2},{4,5},{5,4},{6,7},{7,6},{8,9},{9,8},{10,11... | collective-permute-start | bytes 1572872 | tf_op jit(solution)/shard_map/ppermute | solution.py:343
  103.2 0.8 copy-start.5
  103.9 0.8 copy-start.6

commit v5 on v4

--- a/solution.py
+++ b/solution.py
@@ -78,8 +78,8 @@
 
 def build_tables(z_modes, phi_modes, phi_ref, z_ref, n_gz, n_phi):
     phi_local, lanes = phi_ref.shape[0] // 2, phi_ref.shape[1] // 2
-    rows, z_local = z_ref.shape[0] // 2, z_ref.shape[1]
-    kp, kz = lanes // 2, rows // 2
+    z_local = z_ref.shape[1] // 3
+    kp, kz = lanes // 2, z_ref.shape[0] // 2
     n = n_phi * phi_local
     mode = modes_by_lane(phi_modes, phi_slots(n_phi), kp, lanes)
     lane = lax.broadcasted_iota(jnp.int32, (1, lanes), 1)
@@ -96,8 +96,8 @@
     position = lax.axis_index("gz") * z_local + lax.broadcasted_iota(jnp.int32, (kz, z_local), 1)
     for part, quarter in enumerate((0, 3 * n // 4)):
         high, low = halves(cosines(position * mode + quarter, n))
-        z_ref[part * kz : (part + 1) * kz] = high
-        z_ref[rows + part * kz : rows + (part + 1) * kz] = low
+        for i, term in enumerate((high, low, high)):
+            z_ref[part * kz : (part + 1) * kz, i * z_local : (i + 1) * z_local] = term
 
 
 def forward_kernel(
@@ -120,8 +120,7 @@
 
 def transform(phi_ref, z_ref, x_ref, t_ref, keep_ref, send_ref, base, n_phi, width):
     block, cycles, z_local, phi_local = x_ref.shape
-    modes2 = z_ref.shape[0] // 2
-    modes = modes2 // 2
+    modes = z_ref.shape[0] // 2
     lanes = phi_ref.shape[1] // 2
     shape = keep_ref.shape[1:-4] + keep_ref.shape[-2:]
     lane = lax.broadcasted_iota(jnp.int32, (modes, lanes), 1)
@@ -131,16 +130,19 @@
         x = (x_ref, t_ref)[part][c].reshape(cycles * z_local, phi_local)
         high, low = halves(x)
         y = dot(jnp.concatenate([high, low], axis=1), phi_ref[...])
-        high, low = halves(y[:, :lanes] + y[:, lanes:])
-        return jnp.concatenate([high, low], axis=1)
+        high, low = (
+            jnp.concatenate([term[r * z_local : (r + 1) * z_local] for r in range(cycles)], axis=1)
+            for term in halves(y[:, :lanes] + y[:, lanes:])
+        )
+        return jnp.concatenate([high, high, low], axis=0)
 
     def along_z(y):
-        return [dot(z_ref[...], y[r * z_local : (r + 1) * z_local]) for r in range(cycles)]
+        m = dot(z_ref[...], y)
+        return [m[:, r * lanes : (r + 1) * lanes] for r in range(cycles)]
 
     def finish(c, products):
         items = []
         for m in products:
-            m = m[:modes2, :lanes] + (m[:modes2, lanes:] + m[modes2:, :lanes])
             items.append(m[:modes] + sign * pltpu.roll(m[modes:], lanes // 2, 1))
         for group in range(len(items) // n_phi):
             part = exchange(items[group * n_phi : (group + 1) * n_phi], width)
@@ -177,9 +179,9 @@
         out_shape=[out] * 4,
         scratch_shapes=[
             pltpu.VMEM((2 * phi_local, 2 * lanes), bf16),
-            pltpu.VMEM((4 * kz, z_local), bf16),
+            pltpu.VMEM((2 * kz, 3 * z_local), bf16),
         ],
-        compiler_params=pltpu.CompilerParams(vmem_limit_bytes=40 * MIB),
+        compiler_params=pltpu.CompilerParams(vmem_limit_bytes=54 * MIB),
         cost_estimate=pl.CostEstimate(
             flops=24 * field.size * lanes, bytes_accessed=8 * field.size, transcendentals=0
         ),
@@ -273,11 +275,13 @@
 
     def slots(pieces, c, group):
         v, ab1, a2, b2 = pieces
-        ab1 = ab1[:, c, group]
-        low = [v[:, c, group], jnp.where(first, ab1, b2[0, :, c, group])]
+        half = a2.shape[2]
+        a_at, b_at = jnp.minimum(at + c, half - 1), jnp.maximum(at + c - half, 0)
+        ab1 = ab1[:, at + c, group]
+        low = [v[:, at + c, group], jnp.where(first, ab1, b2[0, :, b_at, group])]
         high = [
-            jnp.where(first, a2[0, :, c, group], ab1),
-            jnp.where(first, a2[1, :, c, group], b2[1, :, c, group]),
+            jnp.where(first, a2[0, :, a_at, group], ab1),
+            jnp.where(first, a2[1, :, a_at, group], b2[1, :, b_at, group]),
         ]
         return [jnp.concatenate(rows, axis=0).reshape(modes, lanes) for rows in (low, high)]
 
@@ -308,26 +312,23 @@
     z_local = span * len(local) // (2 * cycles)
     step = 2
     steps = channels // step
-    zeros = lambda n: (0,) * n
-    shape = (own[0].shape[0], step) + own[0].shape[2:]
-    tail = zeros(len(shape) - 2)
-    v_block = pl.BlockSpec(shape, lambda o: (0, o) + tail)
-    a_block = pl.BlockSpec((2,) + shape, lambda o: (0, 0, jnp.minimum(o, steps // 2 - 1)) + tail)
-    b_block = pl.BlockSpec((2,) + shape, lambda o: (0, 0, jnp.maximum(o - steps // 2, 0)) + tail)
-    local_block = pl.BlockSpec(memory_space=pltpu.VMEM)
-    local = [pltpu.with_memory_space_constraint(piece, pltpu.VMEM) for piece in local]
+    held = pl.BlockSpec(memory_space=pltpu.VMEM)
+    own, other, local = (
+        [pltpu.with_memory_space_constraint(piece, pltpu.VMEM) for piece in pieces]
+        for pieces in (own, other, local)
+    )
     out = jax.ShapeDtypeStruct((channels, cycles, z_local, phi_local), f32)
     out_block = pl.BlockSpec((step, cycles, z_local, phi_local), lambda o: (o, 0, 0, 0))
     size = channels * cycles * z_local * phi_local
     return pl.pallas_call(
         functools.partial(inverse_kernel, n_phi=n_phi, width=width),
         grid=(steps,),
-        in_specs=[v_block, v_block, a_block, b_block] * 2
+        in_specs=[held] * 8
         + [
             pl.BlockSpec(phi_table.shape, lambda o: (0, 0)),
             pl.BlockSpec(z_table.shape, lambda o: (0, 0)),
         ]
-        + [local_block] * len(local),
+        + [held] * len(local),
         out_specs=[out_block, out_block],
         out_shape=[out, out],
         compiler_params=pltpu.CompilerParams(vmem_limit_bytes=18 * MIB),

time: 130 us -> 127 us (0.977)
  local copies, waits for them, and re-layouts: 2.31 us -> 0.14 us
    unnamed x15, local copies, waits for them, and re-layouts: 2.19 us -> 0.04 us
where the time goes in v5:
time: 127 us
  Pallas kernels  72.4 us (57%)
  waiting for transfers between devices  31.7 us (25%)
  starting transfers between devices  21.5 us (17%)
    ppermute x20, waiting for transfers between devices, swap(): return lax.ppermute(x, axis, [(i, i ^ bit) for i in range(count)])  31.7 us
    pallas_call x8, Pallas kernels, local_mix(): pl.pallas_call(local_kernel, grid=(steps,), in_specs=[block, block, pl.Bl...  25.1 us
    pallas_call x1, Pallas kernels, inverse(): pl.pallas_call(functools.partial(inverse_kernel, n_phi=n_phi, width=width...  24.5 us
    ppermute x20, starting transfers between devices, swap(): return lax.ppermute(x, axis, [(i, i ^ bit) for i in range(count)])  21.5 us
    pallas_call x1, Pallas kernels, forward(): pl.pallas_call(functools.partial(forward_kernel, n_gz=n_gz, n_phi=n_phi),...  19.2 us
    pallas_call x1, Pallas kernels, tables(): pl.pallas_call(functools.partial(tables_kernel, n_gz=n_gz, n_phi=n_phi, s...  2.75 us
  transfers between devices with their start and end apart: 20, of which 13 were waited for; matrix products, arithmetic and copies ran while one was open for 0% of the time, Pallas kernels for 22%

profile of v5, /device:TPU:0, one launch (start us, length us, event | category | flops | bytes accessed | tf_op | source)
XLA Modules:
  0.0 126.7 jit_solution(3538904476185823276)
XLA Ops:
  0.6 19.2 %forward_transform.1 = (f32[2,8,8,2,8,128]{5,4,3,2,1,0:T(8,128)S(1)}, f32[2,8,8,2,8,128]{5,4,3,2,1,0:T(8,128)S(1)}, f32[2,8,8,2,8,128]{5,4,3,2,1,0:T(8,128)S(1)}, f32[2,8,8,2,8,128]{5,4,3,2,1,0:T(8,128)S(1)}) custom-call(s32[64]{0:T(128)} %z_modes.2, s32[64]{0:T(128)} %phi_modes.2, f32[16,4,256,256]{3,2,1,0:T(8,128)} %x_ref.9, f32[16,4,256,256]{3,2,1,0:T(8,128)} %t_ref.9), custom_call_target="tpu_custom_call" | custom-call | flops 12884901888 | bytes 33554432 | tf_op jit(solution)/shard_map/forward_transform/pallas_call | solution.py:174
  19.8 0.5 collective-permute-start
  20.3 0.1 collective-permute-start.2
  20.4 2.2 %collective-permute-done.refs_1_ = f32[2,8,8,2,8,128]{5,4,3,2,1,0:T(8,128)S(1)} collective-permute-done((f32[2,8,8,2,8,128]{5,4,3,2,1,0:T(8,128)S(1)}, f32[2,8,8,2,8,128]{5,4,3,2,1,0:T(8,128)S(1)}, u32[]{:S(2)}, u32[]{:S(2)}) %collective-permute-start) | collective-permute-done | bytes 1048608 | tf_op jit(solution)/shard_map/ppermute | solution.py:344
  22.7 0.1 add_terms.4
  22.7 2.9 %collective-permute-start.1 = (f32[8,8,2,8,128]{4,3,2,1,0:T(8,128)S(1)}, f32[8,8,2,8,128]{4,3,2,1,0:T(8,128)S(1)}, u32[]{:S(2)}, u32[]{:S(2)}) collective-permute-start(f32[8,8,2,8,128]{4,3,2,1,0:T(8,128)S(1)} %add_terms.4), channel_id=1, source_target_pairs={{0,2},{1,3},{2,0},{3,1},{4,6},{5,7},{6,4},{7,5},{8,10},{9,11},{10,... | collective-permute-start | bytes 1572872 | tf_op jit(solution)/shard_map/ppermute | solution.py:344
  25.6 0.0 collective-permute-done.2.refs_1_.refs_4_.refs_5_
  25.7 0.1 add_terms.5
  25.7 1.6 %collective-permute-start.3 = (f32[2,4,8,2,8,128]{5,4,3,2,1,0:T(8,128)S(1)}, f32[2,4,8,2,8,128]{5,4,3,2,1,0:T(8,128)S(1)}, u32[]{:S(2)}, u32[]{:S(2)}) collective-permute-start(f32[2,4,8,2,8,128]{5,4,3,2,1,0:T(8,128)S(1)} %add_terms.5), channel_id=1, source_target_pairs={{0,4},{4,0},{8,12},{12,8},{16,20},{20,16},{24,28},{28,24},{1,5},{5... | collective-permute-start | bytes 1572872 | tf_op jit(solution)/shard_map/ppermute | solution.py:344
  27.3 0.0 copy-done
  27.3 0.0 copy-done.3
  27.3 0.0 copy-done.4
  27.3 0.0 copy-done.5
  27.3 0.0 copy-done.6
  27.3 2.8 %small_tables.1 = (bf16[256,256]{1,0:T(8,128)(2,1)S(1)}, f32[16,8,256]{2,1,0:T(8,128)S(1)}, bf16[384,512]{1,0:T(8,128)(2,1)S(1)}, bf16[256,384]{1,0:T(8,128)(2,1...) custom-call(s32[64]{0:T(128)S(1)} %copy-done.4, s32[64]{0:T(128)S(1)} %copy-done.5, f32[16]{0:T(128)S(1)} %copy-done.6, ...), custom_call_target="tpu_custom_call" | custom-call | tf_op jit(solution)/shard_map/small_tables/pallas_call | solution.py:550
  30.1 0.0 copy-start.1
  30.1 0.0 copy-start.2
  30.1 7.8 %collective-permute-done.1.refs_2_ = f32[8,8,2,8,128]{4,3,2,1,0:T(8,128)S(1)} collective-permute-done((f32[8,8,2,8,128]{4,3,2,1,0:T(8,128)S(1)}, f32[8,8,2,8,128]{4,3,2,1,0:T(8,128)S(1)}, u32[]{:S(2)}, u32[]{:S(2)}) %collective-permute-start.1) | collective-permute-done | bytes 524320 | tf_op jit(solution)/shard_map/ppermute | solution.py:344
  37.9 1.6 %collective-permute-done.3.refs_5_.refs_6_ = f32[2,4,8,2,8,128]{5,4,3,2,1,0:T(8,128)S(1)} collective-permute-done((f32[2,4,8,2,8,128]{5,4,3,2,1,0:T(8,128)S(1)}, f32[2,4,8,2,8,128]{5,4,3,2,1,0:T(8,128)S(1)}, u32[]{:S(2)}, u32[]{:S(2)}) %collective-permute-start.3) | collective-permute-done | bytes 524320 | tf_op jit(solution)/shard_map/ppermute | solution.py:344
  39.5 0.1 add_terms.6
  39.6 1.7 %collective-permute-start.4 = (f32[4,8,2,8,128]{4,3,2,1,0:T(8,128)S(1)}, f32[4,8,2,8,128]{4,3,2,1,0:T(8,128)S(1)}, u32[]{:S(2)}, u32[]{:S(2)}) collective-permute-start(f32[4,8,2,8,128]{4,3,2,1,0:T(8,128)S(1)} %get-tuple-element.113), channel_id=1, source_target_pairs={{0,4},{4,0},{8,12},{12,8},{16,20},{20,16},{24,28},{28,24},{1,5},{5... | collective-permute-start | bytes 786440 | tf_op jit(solution)/shard_map/ppermute | solution.py:344
  41.3 1.5 %collective-permute-start.5 = (f32[4,8,2,8,128]{4,3,2,1,0:T(8,128)S(1)}, f32[4,8,2,8,128]{4,3,2,1,0:T(8,128)S(1)}, u32[]{:S(2)}, u32[]{:S(2)}) collective-permute-start(f32[4,8,2,8,128]{4,3,2,1,0:T(8,128)S(1)} %get-tuple-element.114), channel_id=1, source_target_pairs={{0,2},{1,3},{2,0},{3,1},{4,6},{5,7},{6,4},{7,5},{8,10},{9,11},{10,... | collective-permute-start | bytes 786440 | tf_op jit(solution)/shard_map/ppermute | solution.py:344
  42.8 3.1 %local_mix.8 = (f32[16,128,256]{2,1,0:T(8,128)S(1)}, f32[16,128,256]{2,1,0:T(8,128)S(1)}) custom-call(f32[16,4,256,256]{3,2,1,0:T(8,128)} %x_ref.9, f32[16,4,256,256]{3,2,1,0:T(8,128)} %t_ref.9, bf16[256,256]{1,0:T(8,128)(2,1)S(1)} %get-tuple-element.117.w_ref, f32[16,8,256]{2,1,0:T(8,128)S(1)} %get-tuple-element.118.bias_ref), custom_call_target="tpu_custom_call" | custom-call | flops 536870912 | bytes 4194304 | tf_op jit(solution)/shard_map/local_mix/pallas_call | solution.py:217
  46.0 1.0 collective-permute-done.4.refs_3_
  46.9 1.5 %collective-permute-done.5.refs_7_ = f32[4,8,2,8,128]{4,3,2,1,0:T(8,128)S(1)} collective-permute-done((f32[4,8,2,8,128]{4,3,2,1,0:T(8,128)S(1)}, f32[4,8,2,8,128]{4,3,2,1,0:T(8,128)S(1)}, u32[]{:S(2)}, u32[]{:S(2)}) %collective-permute-start.5) | collective-permute-done | bytes 262176 | tf_op jit(solution)/shard_map/ppermute | solution.py:344
  48.4 0.2 add_terms.7
  48.6 2.6 %collective-permute-start.6 = (f32[1,16,2,8,128]{4,3,2,1,0:T(8,128)S(1)}, f32[1,16,2,8,128]{4,3,2,1,0:T(8,128)S(1)}, u32[]{:S(2)}, u32[]{:S(2)}) collective-permute-start(f32[1,16,2,8,128]{4,3,2,1,0:T(8,128)S(1)} %get-tuple-element.124), channel_id=1, source_target_pairs={{0,16},{4,20},{8,24},{12,28},{16,0},{20,4},{24,8},{28,12},{1,17},{... | collective-permute-start | bytes 393224 | tf_op jit(solution)/shard_map/ppermute | solution.py:344
  51.2 1.6 %collective-permute-start.7 = (f32[1,16,2,8,128]{4,3,2,1,0:T(8,128)S(1)}, f32[1,16,2,8,128]{4,3,2,1,0:T(8,128)S(1)}, u32[]{:S(2)}, u32[]{:S(2)}) collective-permute-start(f32[1,16,2,8,128]{4,3,2,1,0:T(8,128)S(1)} %get-tuple-element.125), channel_id=1, source_target_pairs={{0,8},{4,12},{8,0},{12,4},{16,24},{20,28},{24,16},{28,20},{1,9},{5... | collective-permute-start | bytes 393224 | tf_op jit(solution)/shard_map/ppermute | solution.py:344
  52.8 0.2 collective-permute-start.8
  53.0 3.1 %local_mix.10 = (f32[16,128,256]{2,1,0:T(8,128)S(1)}, f32[16,128,256]{2,1,0:T(8,128)S(1)}) custom-call(f32[16,4,256,256]{3,2,1,0:T(8,128)} %x_ref.9, f32[16,4,256,256]{3,2,1,0:T(8,128)} %t_ref.9, bf16[256,256]{1,0:T(8,128)(2,1)S(1)} %get-tuple-element.117.w_ref, f32[16,8,256]{2,1,0:T(8,128)S(1)} %get-tuple-element.118.bias_ref), custom_call_target="tpu_custom_call" | custom-call | flops 536870912 | bytes 4194304 | tf_op jit(solution)/shard_map/local_mix/pallas_call | solution.py:217
  56.2 3.2 %local_mix.9 = (f32[16,128,256]{2,1,0:T(8,128)S(1)}, f32[16,128,256]{2,1,0:T(8,128)S(1)}) custom-call(f32[16,4,256,256]{3,2,1,0:T(8,128)} %x_ref.9, f32[16,4,256,256]{3,2,1,0:T(8,128)} %t_ref.9, bf16[256,256]{1,0:T(8,128)(2,1)S(1)} %get-tuple-element.117.w_ref, f32[16,8,256]{2,1,0:T(8,128)S(1)} %get-tuple-element.118.bias_ref), custom_call_target="tpu_custom_call" | custom-call | flops 536870912 | bytes 4194304 | tf_op jit(solution)/shard_map/local_mix/pallas_call | solution.py:217
  59.3 0.6 collective-permute-done.6
  59.9 0.0 collective-permute-done.7
  59.9 0.0 collective-permute-done.8
  59.9 0.4 mode_mix.1
  60.3 3.5 %collective-permute-start.11 = (f32[1,16,2,8,128]{4,3,2,1,0:T(8,128)S(1)}, f32[1,16,2,8,128]{4,3,2,1,0:T(8,128)S(1)}, u32[]{:S(2)}, u32[]{:S(2)}) collective-permute-start(f32[1,16,2,8,128]{4,3,2,1,0:T(8,128)S(1)} %bitcast.15), channel_id=1, source_target_pairs={{0,24},{4,28},{8,16},{12,20},{16,8},{20,12},{24,0},{28,4},{1,25},{... | collective-permute-start | bytes 393224 | tf_op jit(solution)/shard_map/ppermute | solution.py:344
  63.8 1.1 collective-permute-start.10
  64.9 0.0 collective-permute-start.9
  64.9 3.1 %local_mix.12 = (f32[16,128,256]{2,1,0:T(8,128)S(1)}, f32[16,128,256]{2,1,0:T(8,128)S(1)}) custom-call(f32[16,4,256,256]{3,2,1,0:T(8,128)} %x_ref.9, f32[16,4,256,256]{3,2,1,0:T(8,128)} %t_ref.9, bf16[256,256]{1,0:T(8,128)(2,1)S(1)} %get-tuple-element.117.w_ref, f32[16,8,256]{2,1,0:T(8,128)S(1)} %get-tuple-element.118.bias_ref), custom_call_target="tpu_custom_call" | custom-call | flops 536870912 | bytes 4194304 | tf_op jit(solution)/shard_map/local_mix/pallas_call | solution.py:217
  68.0 3.2 %local_mix.11 = (f32[16,128,256]{2,1,0:T(8,128)S(1)}, f32[16,128,256]{2,1,0:T(8,128)S(1)}) custom-call(f32[16,4,256,256]{3,2,1,0:T(8,128)} %x_ref.9, f32[16,4,256,256]{3,2,1,0:T(8,128)} %t_ref.9, bf16[256,256]{1,0:T(8,128)(2,1)S(1)} %get-tuple-element.117.w_ref, f32[16,8,256]{2,1,0:T(8,128)S(1)} %get-tuple-element.118.bias_ref), custom_call_target="tpu_custom_call" | custom-call | flops 536870912 | bytes 4194304 | tf_op jit(solution)/shard_map/local_mix/pallas_call | solution.py:217
  71.2 0.0 collective-permute-done.11
  71.2 0.0 collective-permute-done.10
  71.2 3.0 %collective-permute-done.9 = f32[1,16,2,8,128]{4,3,2,1,0:T(8,128)S(1)} collective-permute-done((f32[1,16,2,8,128]{4,3,2,1,0:T(8,128)S(1)}, f32[1,16,2,8,128]{4,3,2,1,0:T(8,128)S(1)}, u32[]{:S(2)}, u32[]{:S(2)}) %collective-permute-start.9) | collective-permute-done | bytes 131104 | tf_op jit(solution)/shard_map/ppermute | solution.py:344
  74.3 0.1 collective-permute-start.14
  74.4 0.1 slice_bitcast_fusion
  74.4 1.9 %collective-permute-start.13 = (f32[4,8,2,8,128]{4,3,2,1,0:T(8,128)S(1)}, f32[4,8,2,8,128]{4,3,2,1,0:T(8,128)S(1)}, u32[]{:S(2)}, u32[]{:S(2)}) collective-permute-start(f32[4,8,2,8,128]{4,3,2,1,0:T(8,128)S(1)} %get-tuple-element.192), channel_id=1, source_target_pairs={{0,2},{1,3},{2,0},{3,1},{4,6},{5,7},{6,4},{7,5},{8,10},{9,11},{10,... | collective-permute-start | bytes 786440 | tf_op jit(solution)/shard_map/ppermute | solution.py:344
  76.3 0.6 collective-permute-start.12
  76.9 3.1 %local_mix.13 = (f32[16,128,256]{2,1,0:T(8,128)S(1)}, f32[16,128,256]{2,1,0:T(8,128)S(1)}) custom-call(f32[16,4,256,256]{3,2,1,0:T(8,128)} %x_ref.9, f32[16,4,256,256]{3,2,1,0:T(8,128)} %t_ref.9, bf16[256,256]{1,0:T(8,128)(2,1)S(1)} %get-tuple-element.117.w_ref, f32[16,8,256]{2,1,0:T(8,128)S(1)} %get-tuple-element.118.bias_ref), custom_call_target="tpu_custom_call" | custom-call | flops 536870912 | bytes 4194304 | tf_op jit(solution)/shard_map/local_mix/pallas_call | solution.py:217
  80.0 3.3 %collective-permute-done.13 = f32[4,8,2,8,128]{4,3,2,1,0:T(8,128)S(1)} collective-permute-done((f32[4,8,2,8,128]{4,3,2,1,0:T(8,128)S(1)}, f32[4,8,2,8,128]{4,3,2,1,0:T(8,128)S(1)}, u32[]{:S(2)}, u32[]{:S(2)}) %collective-permute-start.13) | collective-permute-done | bytes 262176 | tf_op jit(solution)/shard_map/ppermute | solution.py:344
  83.3 1.5 %collective-permute-done.12 = f32[4,8,2,8,128]{4,3,2,1,0:T(8,128)S(1)} collective-permute-done((f32[4,8,2,8,128]{4,3,2,1,0:T(8,128)S(1)}, f32[4,8,2,8,128]{4,3,2,1,0:T(8,128)S(1)}, u32[]{:S(2)}, u32[]{:S(2)}) %collective-permute-start.12) | collective-permute-done | bytes 262176 | tf_op jit(solution)/shard_map/ppermute | solution.py:344
  84.8 0.0 collective-permute-done.14.refs_4_
  84.8 0.1 collective-permute-start.17
  84.9 0.4 collective-permute-start.15
  85.4 0.6 collective-permute-start.16
  86.0 3.1 %local_mix.15 = (f32[16,128,256]{2,1,0:T(8,128)S(1)}, f32[16,128,256]{2,1,0:T(8,128)S(1)}) custom-call(f32[16,4,256,256]{3,2,1,0:T(8,128)} %x_ref.9, f32[16,4,256,256]{3,2,1,0:T(8,128)} %t_ref.9, bf16[256,256]{1,0:T(8,128)(2,1)S(1)} %get-tuple-element.117.w_ref, f32[16,8,256]{2,1,0:T(8,128)S(1)} %get-tuple-element.118.bias_ref), custom_call_target="tpu_custom_call" | custom-call | flops 536870912 | bytes 4194304 | tf_op jit(solution)/shard_map/local_mix/pallas_call | solution.py:217
  89.2 3.2 %local_mix.14 = (f32[16,128,256]{2,1,0:T(8,128)S(1)}, f32[16,128,256]{2,1,0:T(8,128)S(1)}) custom-call(f32[16,4,256,256]{3,2,1,0:T(8,128)} %x_ref.9, f32[16,4,256,256]{3,2,1,0:T(8,128)} %t_ref.9, bf16[256,256]{1,0:T(8,128)(2,1)S(1)} %get-tuple-element.117.w_ref, f32[16,8,256]{2,1,0:T(8,128)S(1)} %get-tuple-element.118.bias_ref), custom_call_target="tpu_custom_call" | custom-call | flops 536870912 | bytes 4194304 | tf_op jit(solution)/shard_map/local_mix/pallas_call | solution.py:217
  92.3 0.0 collective-permute-done.17.refs_5_
  92.3 7.0 %collective-permute-done.15.refs_2_ = f32[2,4,8,2,8,128]{5,4,3,2,1,0:T(8,128)S(1)} collective-permute-done((f32[2,4,8,2,8,128]{5,4,3,2,1,0:T(8,128)S(1)}, f32[2,4,8,2,8,128]{5,4,3,2,1,0:T(8,128)S(1)}, u32[]{:S(2)}, u32[]{:S(2)}) %collective-permute-start.15) | collective-permute-done | bytes 524320 | tf_op jit(solution)/shard_map/ppermute | solution.py:344
  99.3 0.2 collective-permute-done.16.refs_3_
  99.5 0.0 collective-permute-start.18
  99.5 0.5 collective-permute-start.19
  100.0 1.4 %collective-permute-done.18.refs_6_ = f32[2,4,8,2,8,128]{5,4,3,2,1,0:T(8,128)S(1)} collective-permute-done((f32[2,4,8,2,8,128]{5,4,3,2,1,0:T(8,128)S(1)}, f32[2,4,8,2,8,128]{5,4,3,2,1,0:T(8,128)S(1)}, u32[]{:S(2)}, u32[]{:S(2)}) %collective-permute-start.18) | collective-permute-done | bytes 524320 | tf_op jit(solution)/shard_map/ppermute | solution.py:344
  101.4 0.7 collective-permute-done.19.refs_7_
  102.2 24.5 %inverse_transform.1 = (f32[16,4,256,256]{3,2,1,0:T(8,128)}, f32[16,4,256,256]{3,2,1,0:T(8,128)}) custom-call(f32[4,16,2,8,128]{4,3,2,1,0:T(8,128)S(1)} %pad_maximum_fusion.refs_0_, f32[4,16,2,8,128]{4,3,2,1,0:T(8,128)S(1)} %constant_dynamic-update-slice_fusion.refs_1_, f32[2,4,8,2,8,128]{5,4,3,2,1,0:T(8,128)S(1)} %collective-permute-done.15.refs_2_, ...), custom_call_target="tpu_custom_call" | custom-call | flops 6710886400 | bytes 67108864 | tf_op jit(solution)/shard_map/inverse_transform/pallas_call | solution.py:323
  (13 shorter events, 0.2 us)
Async XLA Ops:
  19.8 2.8 %collective-permute-start = (f32[2,8,8,2,8,128]{5,4,3,2,1,0:T(8,128)S(1)}, f32[2,8,8,2,8,128]{5,4,3,2,1,0:T(8,128)S(1)}, u32[]{:S(2)}, u32[]{:S(2)}) collective-permute-start(f32[2,8,8,2,8,128]{5,4,3,2,1,0:T(8,128)S(1)} %get-tuple-element.97), channel_id=1, source_target_pairs={{0,1},{1,0},{2,3},{3,2},{4,5},{5,4},{6,7},{7,6},{8,9},{9,8},{10,11... | collective-permute-start | bytes 3145736 | tf_op jit(solution)/shard_map/ppermute | solution.py:344
  20.3 5.3 %collective-permute-start.2 = (f32[2,8,8,2,8,128]{5,4,3,2,1,0:T(8,128)S(1)}, f32[2,8,8,2,8,128]{5,4,3,2,1,0:T(8,128)S(1)}, u32[]{:S(2)}, u32[]{:S(2)}) collective-permute-start(f32[2,8,8,2,8,128]{5,4,3,2,1,0:T(8,128)S(1)} %get-tuple-element.99), channel_id=1, source_target_pairs={{0,1},{1,0},{2,3},{3,2},{4,5},{5,4},{6,7},{7,6},{8,9},{9,8},{10,11... | collective-permute-start | bytes 3145736 | tf_op jit(solution)/shard_map/ppermute | solution.py:344
  22.6 4.7 %copy-start = (f32[2,16,16,8,16]{4,3,2,1,0:T(8,128)S(1)}, f32[2,16,16,8,16]{4,3,2,1,0:T(8,128)}, u32[]{:S(2)}) copy-start(f32[2,16,16,8,16]{4,3,2,1,0:T(8,128)} %param.9) | copy-start | bytes 786436
  22.6 4.7 %copy-start.3 = (f32[16,16]{1,0:T(8,128)S(1)}, f32[16,16]{1,0:T(8,128)}, u32[]{:S(2)}) copy-start(f32[16,16]{1,0:T(8,128)} %weight_ref) | copy-start | bytes 3076
  22.6 4.7 %copy-start.4 = (s32[64]{0:T(128)S(1)}, s32[64]{0:T(128)}, u32[]{:S(2)}) copy-start(s32[64]{0:T(128)} %z_modes.2) | copy-start | bytes 772
  22.6 4.7 %copy-start.5 = (s32[64]{0:T(128)S(1)}, s32[64]{0:T(128)}, u32[]{:S(2)}) copy-start(s32[64]{0:T(128)} %phi_modes.2) | copy-start | bytes 772
  22.6 4.7 %copy-start.6 = (f32[16]{0:T(128)S(1)}, f32[16]{0:T(128)}, u32[]{:S(2)}) copy-start(f32[16]{0:T(128)} %bias) | copy-start | bytes 196
  22.7 15.2 %collective-permute-start.1 = (f32[8,8,2,8,128]{4,3,2,1,0:T(8,128)S(1)}, f32[8,8,2,8,128]{4,3,2,1,0:T(8,128)S(1)}, u32[]{:S(2)}, u32[]{:S(2)}) collective-permute-start(f32[8,8,2,8,128]{4,3,2,1,0:T(8,128)S(1)} %add_terms.4), channel_id=1, source_target_pairs={{0,2},{1,3},{2,0},{3,1},{4,6},{5,7},{6,4},{7,5},{8,10},{9,11},{10,... | collective-permute-start | bytes 1572872 | tf_op jit(solution)/shard_map/ppermute | solution.py:344
  25.7 13.7 %collective-permute-start.3 = (f32[2,4,8,2,8,128]{5,4,3,2,1,0:T(8,128)S(1)}, f32[2,4,8,2,8,128]{5,4,3,2,1,0:T(8,128)S(1)}, u32[]{:S(2)}, u32[]{:S(2)}) collective-permute-start(f32[2,4,8,2,8,128]{5,4,3,2,1,0:T(8,128)S(1)} %add_terms.5), channel_id=1, source_target_pairs={{0,4},{4,0},{8,12},{12,8},{16,20},{20,16},{24,28},{28,24},{1,5},{5... | collective-permute-start | bytes 1572872 | tf_op jit(solution)/shard_map/ppermute | solution.py:344
  30.1 9.5 %copy-start.1 = (bf16[384,512]{1,0:T(8,128)(2,1)}, bf16[384,512]{1,0:T(8,128)(2,1)S(1)}, u32[]{:S(2)}) copy-start(bf16[384,512]{1,0:T(8,128)(2,1)S(1)} %get-tuple-element.172.refs_8_) | copy-start | bytes 1179652
  30.1 9.5 %copy-start.2 = (bf16[256,384]{1,0:T(8,128)(2,1)}, bf16[256,384]{1,0:T(8,128)(2,1)S(1)}, u32[]{:S(2)}) copy-start(bf16[256,384]{1,0:T(8,128)(2,1)S(1)} %get-tuple-element.173.refs_9_) | copy-start | bytes 589828
  39.6 7.3 %collective-permute-start.4 = (f32[4,8,2,8,128]{4,3,2,1,0:T(8,128)S(1)}, f32[4,8,2,8,128]{4,3,2,1,0:T(8,128)S(1)}, u32[]{:S(2)}, u32[]{:S(2)}) collective-permute-start(f32[4,8,2,8,128]{4,3,2,1,0:T(8,128)S(1)} %get-tuple-element.113), channel_id=1, source_target_pairs={{0,4},{4,0},{8,12},{12,8},{16,20},{20,16},{24,28},{28,24},{1,5},{5... | collective-permute-start | bytes 786440 | tf_op jit(solution)/shard_map/ppermute | solution.py:344
  41.3 7.1 %collective-permute-start.5 = (f32[4,8,2,8,128]{4,3,2,1,0:T(8,128)S(1)}, f32[4,8,2,8,128]{4,3,2,1,0:T(8,128)S(1)}, u32[]{:S(2)}, u32[]{:S(2)}) collective-permute-start(f32[4,8,2,8,128]{4,3,2,1,0:T(8,128)S(1)} %get-tuple-element.114), channel_id=1, source_target_pairs={{0,2},{1,3},{2,0},{3,1},{4,6},{5,7},{6,4},{7,5},{8,10},{9,11},{10,... | collective-permute-start | bytes 786440 | tf_op jit(solution)/shard_map/ppermute | solution.py:344
  48.6 11.3 %collective-permute-start.6 = (f32[1,16,2,8,128]{4,3,2,1,0:T(8,128)S(1)}, f32[1,16,2,8,128]{4,3,2,1,0:T(8,128)S(1)}, u32[]{:S(2)}, u32[]{:S(2)}) collective-permute-start(f32[1,16,2,8,128]{4,3,2,1,0:T(8,128)S(1)} %get-tuple-element.124), channel_id=1, source_target_pairs={{0,16},{4,20},{8,24},{12,28},{16,0},{20,4},{24,8},{28,12},{1,17},{... | collective-permute-start | bytes 393224 | tf_op jit(solution)/shard_map/ppermute | solution.py:344
  51.2 8.7 %collective-permute-start.7 = (f32[1,16,2,8,128]{4,3,2,1,0:T(8,128)S(1)}, f32[1,16,2,8,128]{4,3,2,1,0:T(8,128)S(1)}, u32[]{:S(2)}, u32[]{:S(2)}) collective-permute-start(f32[1,16,2,8,128]{4,3,2,1,0:T(8,128)S(1)} %get-tuple-element.125), channel_id=1, source_target_pairs={{0,8},{4,12},{8,0},{12,4},{16,24},{20,28},{24,16},{28,20},{1,9},{5... | collective-permute-start | bytes 393224 | tf_op jit(solution)/shard_map/ppermute | solution.py:344
  52.8 7.1 %collective-permute-start.8 = (f32[1,16,2,8,128]{4,3,2,1,0:T(8,128)S(1)}, f32[1,16,2,8,128]{4,3,2,1,0:T(8,128)S(1)}, u32[]{:S(2)}, u32[]{:S(2)}) collective-permute-start(f32[1,16,2,8,128]{4,3,2,1,0:T(8,128)S(1)} %get-tuple-element.126), channel_id=1, source_target_pairs={{0,24},{4,28},{8,16},{12,20},{16,8},{20,12},{24,0},{28,4},{1,25},{... | collective-permute-start | bytes 393224 | tf_op jit(solution)/shard_map/ppermute | solution.py:344
  60.3 10.9 %collective-permute-start.11 = (f32[1,16,2,8,128]{4,3,2,1,0:T(8,128)S(1)}, f32[1,16,2,8,128]{4,3,2,1,0:T(8,128)S(1)}, u32[]{:S(2)}, u32[]{:S(2)}) collective-permute-start(f32[1,16,2,8,128]{4,3,2,1,0:T(8,128)S(1)} %bitcast.15), channel_id=1, source_target_pairs={{0,24},{4,28},{8,16},{12,20},{16,8},{20,12},{24,0},{28,4},{1,25},{... | collective-permute-start | bytes 393224 | tf_op jit(solution)/shard_map/ppermute | solution.py:344
  63.8 7.4 %collective-permute-start.10 = (f32[1,16,2,8,128]{4,3,2,1,0:T(8,128)S(1)}, f32[1,16,2,8,128]{4,3,2,1,0:T(8,128)S(1)}, u32[]{:S(2)}, u32[]{:S(2)}) collective-permute-start(f32[1,16,2,8,128]{4,3,2,1,0:T(8,128)S(1)} %bitcast.16), channel_id=1, source_target_pairs={{0,8},{4,12},{8,0},{12,4},{16,24},{20,28},{24,16},{28,20},{1,9},{5... | collective-permute-start | bytes 393224 | tf_op jit(solution)/shard_map/ppermute | solution.py:344
  64.9 9.3 %collective-permute-start.9 = (f32[1,16,2,8,128]{4,3,2,1,0:T(8,128)S(1)}, f32[1,16,2,8,128]{4,3,2,1,0:T(8,128)S(1)}, u32[]{:S(2)}, u32[]{:S(2)}) collective-permute-start(f32[1,16,2,8,128]{4,3,2,1,0:T(8,128)S(1)} %bitcast.17), channel_id=1, source_target_pairs={{0,16},{4,20},{8,24},{12,28},{16,0},{20,4},{24,8},{28,12},{1,17},{... | collective-permute-start | bytes 393224 | tf_op jit(solution)/shard_map/ppermute | solution.py:344
  74.3 10.5 %collective-permute-start.14 = (f32[4,16,2,8,128]{4,3,2,1,0:T(8,128)S(1)}, f32[4,16,2,8,128]{4,3,2,1,0:T(8,128)S(1)}, u32[]{:S(2)}, u32[]{:S(2)}) collective-permute-start(f32[4,16,2,8,128]{4,3,2,1,0:T(8,128)S(1)} %pad_maximum_fusion.refs_0_), channel_id=1, source_target_pairs={{0,1},{1,0},{2,3},{3,2},{4,5},{5,4},{6,7},{7,6},{8,9},{9,8},{10,11... | collective-permute-start | bytes 1572872 | tf_op jit(solution)/shard_map/ppermute | solution.py:344
  74.4 8.9 %collective-permute-start.13 = (f32[4,8,2,8,128]{4,3,2,1,0:T(8,128)S(1)}, f32[4,8,2,8,128]{4,3,2,1,0:T(8,128)S(1)}, u32[]{:S(2)}, u32[]{:S(2)}) collective-permute-start(f32[4,8,2,8,128]{4,3,2,1,0:T(8,128)S(1)} %get-tuple-element.192), channel_id=1, source_target_pairs={{0,2},{1,3},{2,0},{3,1},{4,6},{5,7},{6,4},{7,5},{8,10},{9,11},{10,... | collective-permute-start | bytes 786440 | tf_op jit(solution)/shard_map/ppermute | solution.py:344
  76.3 8.4 %collective-permute-start.12 = (f32[4,8,2,8,128]{4,3,2,1,0:T(8,128)S(1)}, f32[4,8,2,8,128]{4,3,2,1,0:T(8,128)S(1)}, u32[]{:S(2)}, u32[]{:S(2)}) collective-permute-start(f32[4,8,2,8,128]{4,3,2,1,0:T(8,128)S(1)} %get-tuple-element.193), channel_id=1, source_target_pairs={{0,4},{4,0},{8,12},{12,8},{16,20},{20,16},{24,28},{28,24},{1,5},{5... | collective-permute-start | bytes 786440 | tf_op jit(solution)/shard_map/ppermute | solution.py:344
  84.8 7.5 %collective-permute-start.17 = (f32[4,16,2,8,128]{4,3,2,1,0:T(8,128)S(1)}, f32[4,16,2,8,128]{4,3,2,1,0:T(8,128)S(1)}, u32[]{:S(2)}, u32[]{:S(2)}) collective-permute-start(f32[4,16,2,8,128]{4,3,2,1,0:T(8,128)S(1)} %constant_dynamic-update-slice_fusion.refs_1_), channel_id=1, source_target_pairs={{0,1},{1,0},{2,3},{3,2},{4,5},{5,4},{6,7},{7,6},{8,9},{9,8},{10,11... | collective-permute-start | bytes 1572872 | tf_op jit(solution)/shard_map/ppermute | solution.py:344
  84.9 14.4 %collective-permute-start.15 = (f32[2,4,8,2,8,128]{5,4,3,2,1,0:T(8,128)S(1)}, f32[2,4,8,2,8,128]{5,4,3,2,1,0:T(8,128)S(1)}, u32[]{:S(2)}, u32[]{:S(2)}) collective-permute-start(f32[2,4,8,2,8,128]{5,4,3,2,1,0:T(8,128)S(1)} %pad_maximum_fusion.1), channel_id=1, source_target_pairs={{0,2},{1,3},{2,0},{3,1},{4,6},{5,7},{6,4},{7,5},{8,10},{9,11},{10,... | collective-permute-start | bytes 1572872 | tf_op jit(solution)/shard_map/ppermute | solution.py:344
  85.4 14.1 %collective-permute-start.16 = (f32[2,4,8,2,8,128]{5,4,3,2,1,0:T(8,128)S(1)}, f32[2,4,8,2,8,128]{5,4,3,2,1,0:T(8,128)S(1)}, u32[]{:S(2)}, u32[]{:S(2)}) collective-permute-start(f32[2,4,8,2,8,128]{5,4,3,2,1,0:T(8,128)S(1)} %pad_maximum_fusion.2), channel_id=1, source_target_pairs={{0,4},{4,0},{8,12},{12,8},{16,20},{20,16},{24,28},{28,24},{1,5},{5... | collective-permute-start | bytes 1572872 | tf_op jit(solution)/shard_map/ppermute | solution.py:344
  99.5 1.9 %collective-permute-start.18 = (f32[2,4,8,2,8,128]{5,4,3,2,1,0:T(8,128)S(1)}, f32[2,4,8,2,8,128]{5,4,3,2,1,0:T(8,128)S(1)}, u32[]{:S(2)}, u32[]{:S(2)}) collective-permute-start(f32[2,4,8,2,8,128]{5,4,3,2,1,0:T(8,128)S(1)} %collective-permute-done.15.refs_2_), channel_id=1, source_target_pairs={{0,1},{1,0},{2,3},{3,2},{4,5},{5,4},{6,7},{7,6},{8,9},{9,8},{10,11... | collective-permute-start | bytes 1572872 | tf_op jit(solution)/shard_map/ppermute | solution.py:344
  99.5 2.7 %collective-permute-start.19 = (f32[2,4,8,2,8,128]{5,4,3,2,1,0:T(8,128)S(1)}, f32[2,4,8,2,8,128]{5,4,3,2,1,0:T(8,128)S(1)}, u32[]{:S(2)}, u32[]{:S(2)}) collective-permute-start(f32[2,4,8,2,8,128]{5,4,3,2,1,0:T(8,128)S(1)} %collective-permute-done.16.refs_3_), channel_id=1, source_target_pairs={{0,1},{1,0},{2,3},{3,2},{4,5},{5,4},{6,7},{7,6},{8,9},{9,8},{10,11... | collective-permute-start | bytes 1572872 | tf_op jit(solution)/shard_map/ppermute | solution.py:344

commit v6 on v5

--- a/solution.py
+++ b/solution.py
@@ -261,10 +261,10 @@
 
 
 def inverse_kernel(*refs, n_phi, width):
-    own, other = refs[:4], refs[4:8]
-    phi_ref, z_ref = refs[8:10]
+    own, other = refs[:6], refs[6:12]
+    phi_ref, z_ref = refs[12:14]
     out_ref, out_t_ref = refs[-2:]
-    refs = refs[10:-2]
+    refs = refs[14:-2]
     block, cycles, z_local, phi_local = out_ref.shape
     parts = len(refs) // (2 * cycles)
     span = z_local // parts
@@ -274,14 +274,14 @@
     at = pl.program_id(0) * block
 
     def slots(pieces, c, group):
-        v, ab1, a2, b2 = pieces
-        half = a2.shape[2]
+        v, ab1, a20, a21, b20, b21 = pieces
+        half = a20.shape[1]
         a_at, b_at = jnp.minimum(at + c, half - 1), jnp.maximum(at + c - half, 0)
         ab1 = ab1[:, at + c, group]
-        low = [v[:, at + c, group], jnp.where(first, ab1, b2[0, :, b_at, group])]
+        low = [v[:, at + c, group], jnp.where(first, ab1, b20[:, b_at, group])]
         high = [
-            jnp.where(first, a2[0, :, a_at, group], ab1),
-            jnp.where(first, a2[1, :, a_at, group], b2[1, :, b_at, group]),
+            jnp.where(first, a20[:, a_at, group], ab1),
+            jnp.where(first, a21[:, a_at, group], b21[:, b_at, group]),
         ]
         return [jnp.concatenate(rows, axis=0).reshape(modes, lanes) for rows in (low, high)]
 
@@ -323,7 +323,7 @@
     return pl.pallas_call(
         functools.partial(inverse_kernel, n_phi=n_phi, width=width),
         grid=(steps,),
-        in_specs=[held] * 8
+        in_specs=[held] * 12
         + [
             pl.BlockSpec(phi_table.shape, lambda o: (0, 0)),
             pl.BlockSpec(z_table.shape, lambda o: (0, 0)),
@@ -358,8 +358,6 @@
         if self.tables is None:
             small, _ = lax.optimization_barrier((self.small, sent))
             self.tables = self.prepare(*small)
-            got, self.tables = lax.optimization_barrier((got, self.tables))
-            return got
         for _ in range(min(count, len(self.todo))):
             r, p = self.todo.pop(0)
             inputs, _ = lax.optimization_barrier((self.inputs, sent))
@@ -413,7 +411,7 @@
     (a_sent,) = sums([[(term, (1,)) for term in a]])
     (b_sent,) = sums([[(term, (every, high)) for term in b]])
     got = (swap(a_sent, "phi", 2), swap(b_sent, "gz", 1))
-    a_got, b_got = filler.beside((a_sent, b_sent), got)
+    a_got, b_got = filler.beside((a_sent, b_sent), got, 2)
     a_sent, b_sent = sums(
         [[(term, (0, high)) for term in a] + [(a_got, (high,))]],
         [[(term, (1, low)) for term in b] + [(b_got, (1,))]],
@@ -449,13 +447,14 @@
         v = jnp.concatenate([v, *got], axis=0)
     half = v.shape[1] // 2
     a, b = v[:, :half], v[:, half:]
-    got = (swap(a, "gz", 1), swap(b, "phi", 2), swap(v, "phi", 1))
-    a1, b1, v_core = filler.beside((a, b), got)
+    first = (swap(a, "gz", 1), swap(b, "phi", 2))
+    a20, b20, v_core = swap(a, "phi", 2), swap(b, "gz", 1), swap(v, "phi", 1)
+    a1, b1 = filler.beside((a, b), first, len(filler.todo))
     ab1 = jnp.concatenate([a1, b1], axis=1)
-    a, b = jnp.stack([a, a1]), jnp.stack([b, b1])
-    got = (swap(a, "phi", 2), swap(b, "gz", 1), swap(ab1, "phi", 1))
-    a2, b2, ab1_core = filler.beside((a, b), got, len(filler.todo))
-    return (v, ab1, a2, b2), (v_core, ab1_core, swap(a2, "phi", 1), swap(b2, "phi", 1))
+    a21, b21 = swap(a1, "phi", 2), swap(b1, "gz", 1)
+    ab1_core, a20_core, b20_core = (swap(part, "phi", 1) for part in (ab1, a20, b20))
+    a21_core, b21_core = swap(a21, "phi", 1), swap(b21, "phi", 1)
+    return (v, ab1, a20, a21, b20, b21), (v_core, ab1_core, a20_core, a21_core, b20_core, b21_core)
 
 
 def gz_groups(n_gz):

time: 127 us -> 120 us (0.945)
  waiting for transfers between devices: 31.7 us -> 23.6 us
  starting transfers between devices: 21.5 us -> 23 us
    ppermute x20 -> x24, waiting for transfers between devices: 31.7 us -> 23.6 us  [swap(): return lax.ppermute(x, axis, [(i, i ^ bit) for i in range(count)])]
    ppermute x20 -> x24, starting transfers between devices: 21.5 us -> 23 us  [swap(): return lax.ppermute(x, axis, [(i, i ^ bit) for i in range(count)])]
  transfers between devices with their start and end apart: 20 -> 24, of which waited for: 13 -> 15; matrix products, arithmetic and copies ran while one was open for 0% -> 0% of each run, Pallas kernels for 22% -> 23%
where the time goes in v6:
time: 120 us
  Pallas kernels  72.6 us (60%)
  waiting for transfers between devices  23.6 us (20%)
  starting transfers between devices  23 us (19%)
    pallas_call x8, Pallas kernels, local_mix(): pl.pallas_call(local_kernel, grid=(steps,), in_specs=[block, block, pl.Bl...  25.3 us
    pallas_call x1, Pallas kernels, inverse(): pl.pallas_call(functools.partial(inverse_kernel, n_phi=n_phi, width=width...  24.6 us
    ppermute x24, waiting for transfers between devices, swap(): return lax.ppermute(x, axis, [(i, i ^ bit) for i in range(count)])  23.6 us
    ppermute x24, starting transfers between devices, swap(): return lax.ppermute(x, axis, [(i, i ^ bit) for i in range(count)])  23 us
    pallas_call x1, Pallas kernels, forward(): pl.pallas_call(functools.partial(forward_kernel, n_gz=n_gz, n_phi=n_phi),...  19.2 us
    pallas_call x1, Pallas kernels, tables(): pl.pallas_call(functools.partial(tables_kernel, n_gz=n_gz, n_phi=n_phi, s...  2.75 us
  transfers between devices with their start and end apart: 24, of which 15 were waited for; matrix products, arithmetic and copies ran while one was open for 0% of the time, Pallas kernels for 23%

profile of v6, /device:TPU:0, one launch (start us, length us, event | category | flops | bytes accessed | tf_op | source)
XLA Modules:
  0.0 120.3 jit_solution(8455241916711104055)
XLA Ops:
  0.6 19.2 %forward_transform.1 = (f32[2,8,8,2,8,128]{5,4,3,2,1,0:T(8,128)S(1)}, f32[2,8,8,2,8,128]{5,4,3,2,1,0:T(8,128)S(1)}, f32[2,8,8,2,8,128]{5,4,3,2,1,0:T(8,128)S(1)}, f32[2,8,8,2,8,128]{5,4,3,2,1,0:T(8,128)S(1)}) custom-call(s32[64]{0:T(128)} %z_modes.2, s32[64]{0:T(128)} %phi_modes.2, f32[16,4,256,256]{3,2,1,0:T(8,128)} %x_ref.9, f32[16,4,256,256]{3,2,1,0:T(8,128)} %t_ref.9), custom_call_target="tpu_custom_call" | custom-call | flops 12884901888 | bytes 33554432 | tf_op jit(solution)/shard_map/forward_transform/pallas_call | solution.py:174
  19.8 0.5 collective-permute-start
  20.3 0.1 collective-permute-start.2
  20.4 2.2 %collective-permute-done.refs_1_ = f32[2,8,8,2,8,128]{5,4,3,2,1,0:T(8,128)S(1)} collective-permute-done((f32[2,8,8,2,8,128]{5,4,3,2,1,0:T(8,128)S(1)}, f32[2,8,8,2,8,128]{5,4,3,2,1,0:T(8,128)S(1)}, u32[]{:S(2)}, u32[]{:S(2)}) %collective-permute-start) | collective-permute-done | bytes 1048608 | tf_op jit(solution)/shard_map/ppermute | solution.py:344
  22.7 0.1 add_terms.4
  22.7 2.9 %collective-permute-start.1 = (f32[8,8,2,8,128]{4,3,2,1,0:T(8,128)S(1)}, f32[8,8,2,8,128]{4,3,2,1,0:T(8,128)S(1)}, u32[]{:S(2)}, u32[]{:S(2)}) collective-permute-start(f32[8,8,2,8,128]{4,3,2,1,0:T(8,128)S(1)} %add_terms.4), channel_id=1, source_target_pairs={{0,2},{1,3},{2,0},{3,1},{4,6},{5,7},{6,4},{7,5},{8,10},{9,11},{10,... | collective-permute-start | bytes 1572872 | tf_op jit(solution)/shard_map/ppermute | solution.py:344
  25.6 0.0 collective-permute-done.2.refs_1_.refs_4_.refs_5_
  25.7 0.1 add_terms.5
  25.7 1.6 %collective-permute-start.3 = (f32[2,4,8,2,8,128]{5,4,3,2,1,0:T(8,128)S(1)}, f32[2,4,8,2,8,128]{5,4,3,2,1,0:T(8,128)S(1)}, u32[]{:S(2)}, u32[]{:S(2)}) collective-permute-start(f32[2,4,8,2,8,128]{5,4,3,2,1,0:T(8,128)S(1)} %add_terms.5), channel_id=1, source_target_pairs={{0,4},{4,0},{8,12},{12,8},{16,20},{20,16},{24,28},{28,24},{1,5},{5... | collective-permute-start | bytes 1572872 | tf_op jit(solution)/shard_map/ppermute | solution.py:344
  27.3 2.8 %small_tables.1 = (bf16[256,256]{1,0:T(8,128)(2,1)S(1)}, f32[16,8,256]{2,1,0:T(8,128)S(1)}, bf16[384,512]{1,0:T(8,128)(2,1)S(1)}, bf16[256,384]{1,0:T(8,128)(2,1...) custom-call(s32[64]{0:T(128)S(1)} %copy-done.4, s32[64]{0:T(128)S(1)} %copy-done.5, f32[16]{0:T(128)S(1)} %copy-done.6, ...), custom_call_target="tpu_custom_call" | custom-call | tf_op jit(solution)/shard_map/small_tables/pallas_call | solution.py:549
  30.1 3.3 %local_mix.9 = (f32[16,128,256]{2,1,0:T(8,128)S(1)}, f32[16,128,256]{2,1,0:T(8,128)S(1)}) custom-call(f32[16,4,256,256]{3,2,1,0:T(8,128)} %x_ref.9, f32[16,4,256,256]{3,2,1,0:T(8,128)} %t_ref.9, bf16[256,256]{1,0:T(8,128)(2,1)S(1)} %get-tuple-element.96.w_ref, f32[16,8,256]{2,1,0:T(8,128)S(1)} %get-tuple-element.97.bias_ref), custom_call_target="tpu_custom_call" | custom-call | flops 536870912 | bytes 4194304 | tf_op jit(solution)/shard_map/local_mix/pallas_call | solution.py:217
  33.5 3.1 %local_mix.8 = (f32[16,128,256]{2,1,0:T(8,128)S(1)}, f32[16,128,256]{2,1,0:T(8,128)S(1)}) custom-call(f32[16,4,256,256]{3,2,1,0:T(8,128)} %x_ref.9, f32[16,4,256,256]{3,2,1,0:T(8,128)} %t_ref.9, bf16[256,256]{1,0:T(8,128)(2,1)S(1)} %get-tuple-element.96.w_ref, f32[16,8,256]{2,1,0:T(8,128)S(1)} %get-tuple-element.97.bias_ref), custom_call_target="tpu_custom_call" | custom-call | flops 536870912 | bytes 4194304 | tf_op jit(solution)/shard_map/local_mix/pallas_call | solution.py:217
  36.6 1.2 %collective-permute-done.1.refs_2_ = f32[8,8,2,8,128]{4,3,2,1,0:T(8,128)S(1)} collective-permute-done((f32[8,8,2,8,128]{4,3,2,1,0:T(8,128)S(1)}, f32[8,8,2,8,128]{4,3,2,1,0:T(8,128)S(1)}, u32[]{:S(2)}, u32[]{:S(2)}) %collective-permute-start.1) | collective-permute-done | bytes 524320 | tf_op jit(solution)/shard_map/ppermute | solution.py:344
  37.9 1.6 %collective-permute-done.3.refs_5_.refs_6_ = f32[2,4,8,2,8,128]{5,4,3,2,1,0:T(8,128)S(1)} collective-permute-done((f32[2,4,8,2,8,128]{5,4,3,2,1,0:T(8,128)S(1)}, f32[2,4,8,2,8,128]{5,4,3,2,1,0:T(8,128)S(1)}, u32[]{:S(2)}, u32[]{:S(2)}) %collective-permute-start.3) | collective-permute-done | bytes 524320 | tf_op jit(solution)/shard_map/ppermute | solution.py:344
  39.5 0.1 add_terms.6
  39.6 1.7 %collective-permute-start.4 = (f32[4,8,2,8,128]{4,3,2,1,0:T(8,128)S(1)}, f32[4,8,2,8,128]{4,3,2,1,0:T(8,128)S(1)}, u32[]{:S(2)}, u32[]{:S(2)}) collective-permute-start(f32[4,8,2,8,128]{4,3,2,1,0:T(8,128)S(1)} %get-tuple-element.106), channel_id=1, source_target_pairs={{0,4},{4,0},{8,12},{12,8},{16,20},{20,16},{24,28},{28,24},{1,5},{5... | collective-permute-start | bytes 786440 | tf_op jit(solution)/shard_map/ppermute | solution.py:344
  41.3 1.5 %collective-permute-start.5 = (f32[4,8,2,8,128]{4,3,2,1,0:T(8,128)S(1)}, f32[4,8,2,8,128]{4,3,2,1,0:T(8,128)S(1)}, u32[]{:S(2)}, u32[]{:S(2)}) collective-permute-start(f32[4,8,2,8,128]{4,3,2,1,0:T(8,128)S(1)} %get-tuple-element.107), channel_id=1, source_target_pairs={{0,2},{1,3},{2,0},{3,1},{4,6},{5,7},{6,4},{7,5},{8,10},{9,11},{10,... | collective-permute-start | bytes 786440 | tf_op jit(solution)/shard_map/ppermute | solution.py:344
  42.8 3.1 %local_mix.10 = (f32[16,128,256]{2,1,0:T(8,128)S(1)}, f32[16,128,256]{2,1,0:T(8,128)S(1)}) custom-call(f32[16,4,256,256]{3,2,1,0:T(8,128)} %x_ref.9, f32[16,4,256,256]{3,2,1,0:T(8,128)} %t_ref.9, bf16[256,256]{1,0:T(8,128)(2,1)S(1)} %get-tuple-element.96.w_ref, f32[16,8,256]{2,1,0:T(8,128)S(1)} %get-tuple-element.97.bias_ref), custom_call_target="tpu_custom_call" | custom-call | flops 536870912 | bytes 4194304 | tf_op jit(solution)/shard_map/local_mix/pallas_call | solution.py:217
  45.9 1.0 collective-permute-done.4.refs_3_
  46.9 1.5 %collective-permute-done.5.refs_7_ = f32[4,8,2,8,128]{4,3,2,1,0:T(8,128)S(1)} collective-permute-done((f32[4,8,2,8,128]{4,3,2,1,0:T(8,128)S(1)}, f32[4,8,2,8,128]{4,3,2,1,0:T(8,128)S(1)}, u32[]{:S(2)}, u32[]{:S(2)}) %collective-permute-start.5) | collective-permute-done | bytes 262176 | tf_op jit(solution)/shard_map/ppermute | solution.py:344
  48.4 0.2 add_terms.7
  48.5 2.6 %collective-permute-start.6 = (f32[1,16,2,8,128]{4,3,2,1,0:T(8,128)S(1)}, f32[1,16,2,8,128]{4,3,2,1,0:T(8,128)S(1)}, u32[]{:S(2)}, u32[]{:S(2)}) collective-permute-start(f32[1,16,2,8,128]{4,3,2,1,0:T(8,128)S(1)} %get-tuple-element.115), channel_id=1, source_target_pairs={{0,16},{4,20},{8,24},{12,28},{16,0},{20,4},{24,8},{28,12},{1,17},{... | collective-permute-start | bytes 393224 | tf_op jit(solution)/shard_map/ppermute | solution.py:344
  51.2 1.6 %collective-permute-start.7 = (f32[1,16,2,8,128]{4,3,2,1,0:T(8,128)S(1)}, f32[1,16,2,8,128]{4,3,2,1,0:T(8,128)S(1)}, u32[]{:S(2)}, u32[]{:S(2)}) collective-permute-start(f32[1,16,2,8,128]{4,3,2,1,0:T(8,128)S(1)} %get-tuple-element.116), channel_id=1, source_target_pairs={{0,8},{4,12},{8,0},{12,4},{16,24},{20,28},{24,16},{28,20},{1,9},{5... | collective-permute-start | bytes 393224 | tf_op jit(solution)/shard_map/ppermute | solution.py:344
  52.8 0.2 collective-permute-start.8
  53.0 3.1 %local_mix.12 = (f32[16,128,256]{2,1,0:T(8,128)S(1)}, f32[16,128,256]{2,1,0:T(8,128)S(1)}) custom-call(f32[16,4,256,256]{3,2,1,0:T(8,128)} %x_ref.9, f32[16,4,256,256]{3,2,1,0:T(8,128)} %t_ref.9, bf16[256,256]{1,0:T(8,128)(2,1)S(1)} %get-tuple-element.96.w_ref, f32[16,8,256]{2,1,0:T(8,128)S(1)} %get-tuple-element.97.bias_ref), custom_call_target="tpu_custom_call" | custom-call | flops 536870912 | bytes 4194304 | tf_op jit(solution)/shard_map/local_mix/pallas_call | solution.py:217
  56.1 3.2 %local_mix.11 = (f32[16,128,256]{2,1,0:T(8,128)S(1)}, f32[16,128,256]{2,1,0:T(8,128)S(1)}) custom-call(f32[16,4,256,256]{3,2,1,0:T(8,128)} %x_ref.9, f32[16,4,256,256]{3,2,1,0:T(8,128)} %t_ref.9, bf16[256,256]{1,0:T(8,128)(2,1)S(1)} %get-tuple-element.96.w_ref, f32[16,8,256]{2,1,0:T(8,128)S(1)} %get-tuple-element.97.bias_ref), custom_call_target="tpu_custom_call" | custom-call | flops 536870912 | bytes 4194304 | tf_op jit(solution)/shard_map/local_mix/pallas_call | solution.py:217
  59.3 0.6 collective-permute-done.6
  59.9 0.0 collective-permute-done.7
  59.9 0.0 collective-permute-done.8
  59.9 0.4 mode_mix.1
  60.3 3.5 %collective-permute-start.11 = (f32[1,16,2,8,128]{4,3,2,1,0:T(8,128)S(1)}, f32[1,16,2,8,128]{4,3,2,1,0:T(8,128)S(1)}, u32[]{:S(2)}, u32[]{:S(2)}) collective-permute-start(f32[1,16,2,8,128]{4,3,2,1,0:T(8,128)S(1)} %bitcast.9), channel_id=1, source_target_pairs={{0,24},{4,28},{8,16},{12,20},{16,8},{20,12},{24,0},{28,4},{1,25},{... | collective-permute-start | bytes 393224 | tf_op jit(solution)/shard_map/ppermute | solution.py:344
  63.8 1.1 collective-permute-start.10
  64.9 0.0 collective-permute-start.9
  64.9 3.1 %local_mix.14 = (f32[16,128,256]{2,1,0:T(8,128)S(1)}, f32[16,128,256]{2,1,0:T(8,128)S(1)}) custom-call(f32[16,4,256,256]{3,2,1,0:T(8,128)} %x_ref.9, f32[16,4,256,256]{3,2,1,0:T(8,128)} %t_ref.9, bf16[256,256]{1,0:T(8,128)(2,1)S(1)} %get-tuple-element.96.w_ref, f32[16,8,256]{2,1,0:T(8,128)S(1)} %get-tuple-element.97.bias_ref), custom_call_target="tpu_custom_call" | custom-call | flops 536870912 | bytes 4194304 | tf_op jit(solution)/shard_map/local_mix/pallas_call | solution.py:217
  68.0 3.2 %local_mix.13 = (f32[16,128,256]{2,1,0:T(8,128)S(1)}, f32[16,128,256]{2,1,0:T(8,128)S(1)}) custom-call(f32[16,4,256,256]{3,2,1,0:T(8,128)} %x_ref.9, f32[16,4,256,256]{3,2,1,0:T(8,128)} %t_ref.9, bf16[256,256]{1,0:T(8,128)(2,1)S(1)} %get-tuple-element.96.w_ref, f32[16,8,256]{2,1,0:T(8,128)S(1)} %get-tuple-element.97.bias_ref), custom_call_target="tpu_custom_call" | custom-call | flops 536870912 | bytes 4194304 | tf_op jit(solution)/shard_map/local_mix/pallas_call | solution.py:217
  71.2 0.0 collective-permute-done.11
  71.2 0.0 collective-permute-done.10
  71.2 3.0 %collective-permute-done.9 = f32[1,16,2,8,128]{4,3,2,1,0:T(8,128)S(1)} collective-permute-done((f32[1,16,2,8,128]{4,3,2,1,0:T(8,128)S(1)}, f32[1,16,2,8,128]{4,3,2,1,0:T(8,128)S(1)}, u32[]{:S(2)}, u32[]{:S(2)}) %collective-permute-start.9) | collective-permute-done | bytes 131104 | tf_op jit(solution)/shard_map/ppermute | solution.py:344
  74.3 1.9 %collective-permute-start.13 = (f32[4,8,2,8,128]{4,3,2,1,0:T(8,128)S(1)}, f32[4,8,2,8,128]{4,3,2,1,0:T(8,128)S(1)}, u32[]{:S(2)}, u32[]{:S(2)}) collective-permute-start(f32[4,8,2,8,128]{4,3,2,1,0:T(8,128)S(1)} %get-tuple-element.168), channel_id=1, source_target_pairs={{0,2},{1,3},{2,0},{3,1},{4,6},{5,7},{6,4},{7,5},{8,10},{9,11},{10,... | collective-permute-start | bytes 786440 | tf_op jit(solution)/shard_map/ppermute | solution.py:344
  76.2 0.6 collective-permute-start.12
  76.8 1.5 %collective-permute-start.16 = (f32[4,8,2,8,128]{4,3,2,1,0:T(8,128)S(1)}, f32[4,8,2,8,128]{4,3,2,1,0:T(8,128)S(1)}, u32[]{:S(2)}, u32[]{:S(2)}) collective-permute-start(f32[4,8,2,8,128]{4,3,2,1,0:T(8,128)S(1)} %get-tuple-element.168), channel_id=1, source_target_pairs={{0,4},{4,0},{8,12},{12,8},{16,20},{20,16},{24,28},{28,24},{1,5},{5... | collective-permute-start | bytes 786440 | tf_op jit(solution)/shard_map/ppermute | solution.py:344
  78.2 0.2 collective-permute-start.14
  78.4 0.0 collective-permute-start.18
  78.4 3.1 %local_mix.15 = (f32[16,128,256]{2,1,0:T(8,128)S(1)}, f32[16,128,256]{2,1,0:T(8,128)S(1)}) custom-call(f32[16,4,256,256]{3,2,1,0:T(8,128)} %x_ref.9, f32[16,4,256,256]{3,2,1,0:T(8,128)} %t_ref.9, bf16[256,256]{1,0:T(8,128)(2,1)S(1)} %get-tuple-element.96.w_ref, f32[16,8,256]{2,1,0:T(8,128)S(1)} %get-tuple-element.97.bias_ref), custom_call_target="tpu_custom_call" | custom-call | flops 536870912 | bytes 4194304 | tf_op jit(solution)/shard_map/local_mix/pallas_call | solution.py:217
  81.6 2.0 %collective-permute-done.13 = f32[4,8,2,8,128]{4,3,2,1,0:T(8,128)S(1)} collective-permute-done((f32[4,8,2,8,128]{4,3,2,1,0:T(8,128)S(1)}, f32[4,8,2,8,128]{4,3,2,1,0:T(8,128)S(1)}, u32[]{:S(2)}, u32[]{:S(2)}) %collective-permute-start.13) | collective-permute-done | bytes 262176 | tf_op jit(solution)/shard_map/ppermute | solution.py:344
  83.6 1.8 %collective-permute-done.12 = f32[4,8,2,8,128]{4,3,2,1,0:T(8,128)S(1)} collective-permute-done((f32[4,8,2,8,128]{4,3,2,1,0:T(8,128)S(1)}, f32[4,8,2,8,128]{4,3,2,1,0:T(8,128)S(1)}, u32[]{:S(2)}, u32[]{:S(2)}) %collective-permute-start.12) | collective-permute-done | bytes 262176 | tf_op jit(solution)/shard_map/ppermute | solution.py:344
  85.4 0.2 collective-permute-start.15
  85.6 0.6 collective-permute-start.17
  86.2 4.5 %collective-permute-done.16.refs_4_ = f32[4,8,2,8,128]{4,3,2,1,0:T(8,128)S(1)} collective-permute-done((f32[4,8,2,8,128]{4,3,2,1,0:T(8,128)S(1)}, f32[4,8,2,8,128]{4,3,2,1,0:T(8,128)S(1)}, u32[]{:S(2)}, u32[]{:S(2)}) %collective-permute-start.16) | collective-permute-done | bytes 262176 | tf_op jit(solution)/shard_map/ppermute | solution.py:344
  90.7 0.0 collective-permute-start.22
  90.8 0.0 collective-permute-done.14.refs_2_
  90.8 0.6 collective-permute-start.19
  91.4 0.9 collective-permute-done.22.refs_10_
  92.3 0.1 collective-permute-start.20
  92.4 0.3 collective-permute-done.15.refs_3_
  92.7 0.1 collective-permute-start.21
  92.8 1.4 %collective-permute-done.17.refs_5_ = f32[4,8,2,8,128]{4,3,2,1,0:T(8,128)S(1)} collective-permute-done((f32[4,8,2,8,128]{4,3,2,1,0:T(8,128)S(1)}, f32[4,8,2,8,128]{4,3,2,1,0:T(8,128)S(1)}, u32[]{:S(2)}, u32[]{:S(2)}) %collective-permute-start.17) | collective-permute-done | bytes 262176 | tf_op jit(solution)/shard_map/ppermute | solution.py:344
  94.2 0.0 collective-permute-start.23
  94.2 0.0 collective-permute-done.20.refs_8_
  94.2 0.0 collective-permute-done.18.refs_6_
  94.2 0.1 collective-permute-done.21.refs_9_
  94.2 1.5 %collective-permute-done.23.refs_11_ = f32[4,8,2,8,128]{4,3,2,1,0:T(8,128)S(1)} collective-permute-done((f32[4,8,2,8,128]{4,3,2,1,0:T(8,128)S(1)}, f32[4,8,2,8,128]{4,3,2,1,0:T(8,128)S(1)}, u32[]{:S(2)}, u32[]{:S(2)}) %collective-permute-start.23) | collective-permute-done | bytes 262176 | tf_op jit(solution)/shard_map/ppermute | solution.py:344
  95.7 0.0 collective-permute-done.19.refs_7_
  95.7 24.6 %inverse_transform.1 = (f32[16,4,256,256]{3,2,1,0:T(8,128)}, f32[16,4,256,256]{3,2,1,0:T(8,128)}) custom-call(f32[4,16,2,8,128]{4,3,2,1,0:T(8,128)S(1)} %pad_maximum_fusion.refs_0_, f32[4,16,2,8,128]{4,3,2,1,0:T(8,128)S(1)} %constant_dynamic-update-slice_fusion.refs_1_, f32[4,8,2,8,128]{4,3,2,1,0:T(8,128)S(1)} %collective-permute-done.14.refs_2_, ...), custom_call_target="tpu_custom_call" | custom-call | flops 6710886400 | bytes 67108864 | tf_op jit(solution)/shard_map/inverse_transform/pallas_call | solution.py:323
  (19 shorter events, 0.2 us)
Async XLA Ops:
  19.8 2.8 %collective-permute-start = (f32[2,8,8,2,8,128]{5,4,3,2,1,0:T(8,128)S(1)}, f32[2,8,8,2,8,128]{5,4,3,2,1,0:T(8,128)S(1)}, u32[]{:S(2)}, u32[]{:S(2)}) collective-permute-start(f32[2,8,8,2,8,128]{5,4,3,2,1,0:T(8,128)S(1)} %get-tuple-element.86), channel_id=1, source_target_pairs={{0,1},{1,0},{2,3},{3,2},{4,5},{5,4},{6,7},{7,6},{8,9},{9,8},{10,11... | collective-permute-start | bytes 3145736 | tf_op jit(solution)/shard_map/ppermute | solution.py:344
  20.3 5.3 %collective-permute-start.2 = (f32[2,8,8,2,8,128]{5,4,3,2,1,0:T(8,128)S(1)}, f32[2,8,8,2,8,128]{5,4,3,2,1,0:T(8,128)S(1)}, u32[]{:S(2)}, u32[]{:S(2)}) collective-permute-start(f32[2,8,8,2,8,128]{5,4,3,2,1,0:T(8,128)S(1)} %get-tuple-element.88), channel_id=1, source_target_pairs={{0,1},{1,0},{2,3},{3,2},{4,5},{5,4},{6,7},{7,6},{8,9},{9,8},{10,11... | collective-permute-start | bytes 3145736 | tf_op jit(solution)/shard_map/ppermute | solution.py:344
  22.6 4.7 %copy-start = (f32[2,16,16,8,16]{4,3,2,1,0:T(8,128)S(1)}, f32[2,16,16,8,16]{4,3,2,1,0:T(8,128)}, u32[]{:S(2)}) copy-start(f32[2,16,16,8,16]{4,3,2,1,0:T(8,128)} %param.9) | copy-start | bytes 786436
  22.6 4.7 %copy-start.3 = (f32[16,16]{1,0:T(8,128)S(1)}, f32[16,16]{1,0:T(8,128)}, u32[]{:S(2)}) copy-start(f32[16,16]{1,0:T(8,128)} %weight_ref) | copy-start | bytes 3076
  22.6 4.7 %copy-start.4 = (s32[64]{0:T(128)S(1)}, s32[64]{0:T(128)}, u32[]{:S(2)}) copy-start(s32[64]{0:T(128)} %z_modes.2) | copy-start | bytes 772
  22.6 4.7 %copy-start.5 = (s32[64]{0:T(128)S(1)}, s32[64]{0:T(128)}, u32[]{:S(2)}) copy-start(s32[64]{0:T(128)} %phi_modes.2) | copy-start | bytes 772
  22.6 4.7 %copy-start.6 = (f32[16]{0:T(128)S(1)}, f32[16]{0:T(128)}, u32[]{:S(2)}) copy-start(f32[16]{0:T(128)} %bias) | copy-start | bytes 196
  22.7 15.2 %collective-permute-start.1 = (f32[8,8,2,8,128]{4,3,2,1,0:T(8,128)S(1)}, f32[8,8,2,8,128]{4,3,2,1,0:T(8,128)S(1)}, u32[]{:S(2)}, u32[]{:S(2)}) collective-permute-start(f32[8,8,2,8,128]{4,3,2,1,0:T(8,128)S(1)} %add_terms.4), channel_id=1, source_target_pairs={{0,2},{1,3},{2,0},{3,1},{4,6},{5,7},{6,4},{7,5},{8,10},{9,11},{10,... | collective-permute-start | bytes 1572872 | tf_op jit(solution)/shard_map/ppermute | solution.py:344
  25.7 13.7 %collective-permute-start.3 = (f32[2,4,8,2,8,128]{5,4,3,2,1,0:T(8,128)S(1)}, f32[2,4,8,2,8,128]{5,4,3,2,1,0:T(8,128)S(1)}, u32[]{:S(2)}, u32[]{:S(2)}) collective-permute-start(f32[2,4,8,2,8,128]{5,4,3,2,1,0:T(8,128)S(1)} %add_terms.5), channel_id=1, source_target_pairs={{0,4},{4,0},{8,12},{12,8},{16,20},{20,16},{24,28},{28,24},{1,5},{5... | collective-permute-start | bytes 1572872 | tf_op jit(solution)/shard_map/ppermute | solution.py:344
  30.1 3.4 %copy-start.1 = (bf16[384,512]{1,0:T(8,128)(2,1)}, bf16[384,512]{1,0:T(8,128)(2,1)S(1)}, u32[]{:S(2)}) copy-start(bf16[384,512]{1,0:T(8,128)(2,1)S(1)} %get-tuple-element.150.refs_12_) | copy-start | bytes 1179652
  30.1 3.4 %copy-start.2 = (bf16[256,384]{1,0:T(8,128)(2,1)}, bf16[256,384]{1,0:T(8,128)(2,1)S(1)}, u32[]{:S(2)}) copy-start(bf16[256,384]{1,0:T(8,128)(2,1)S(1)} %get-tuple-element.151.refs_13_) | copy-start | bytes 589828
  39.6 7.3 %collective-permute-start.4 = (f32[4,8,2,8,128]{4,3,2,1,0:T(8,128)S(1)}, f32[4,8,2,8,128]{4,3,2,1,0:T(8,128)S(1)}, u32[]{:S(2)}, u32[]{:S(2)}) collective-permute-start(f32[4,8,2,8,128]{4,3,2,1,0:T(8,128)S(1)} %get-tuple-element.106), channel_id=1, source_target_pairs={{0,4},{4,0},{8,12},{12,8},{16,20},{20,16},{24,28},{28,24},{1,5},{5... | collective-permute-start | bytes 786440 | tf_op jit(solution)/shard_map/ppermute | solution.py:344
  41.3 7.1 %collective-permute-start.5 = (f32[4,8,2,8,128]{4,3,2,1,0:T(8,128)S(1)}, f32[4,8,2,8,128]{4,3,2,1,0:T(8,128)S(1)}, u32[]{:S(2)}, u32[]{:S(2)}) collective-permute-start(f32[4,8,2,8,128]{4,3,2,1,0:T(8,128)S(1)} %get-tuple-element.107), channel_id=1, source_target_pairs={{0,2},{1,3},{2,0},{3,1},{4,6},{5,7},{6,4},{7,5},{8,10},{9,11},{10,... | collective-permute-start | bytes 786440 | tf_op jit(solution)/shard_map/ppermute | solution.py:344
  48.5 11.3 %collective-permute-start.6 = (f32[1,16,2,8,128]{4,3,2,1,0:T(8,128)S(1)}, f32[1,16,2,8,128]{4,3,2,1,0:T(8,128)S(1)}, u32[]{:S(2)}, u32[]{:S(2)}) collective-permute-start(f32[1,16,2,8,128]{4,3,2,1,0:T(8,128)S(1)} %get-tuple-element.115), channel_id=1, source_target_pairs={{0,16},{4,20},{8,24},{12,28},{16,0},{20,4},{24,8},{28,12},{1,17},{... | collective-permute-start | bytes 393224 | tf_op jit(solution)/shard_map/ppermute | solution.py:344
  51.2 8.7 %collective-permute-start.7 = (f32[1,16,2,8,128]{4,3,2,1,0:T(8,128)S(1)}, f32[1,16,2,8,128]{4,3,2,1,0:T(8,128)S(1)}, u32[]{:S(2)}, u32[]{:S(2)}) collective-permute-start(f32[1,16,2,8,128]{4,3,2,1,0:T(8,128)S(1)} %get-tuple-element.116), channel_id=1, source_target_pairs={{0,8},{4,12},{8,0},{12,4},{16,24},{20,28},{24,16},{28,20},{1,9},{5... | collective-permute-start | bytes 393224 | tf_op jit(solution)/shard_map/ppermute | solution.py:344
  52.8 7.1 %collective-permute-start.8 = (f32[1,16,2,8,128]{4,3,2,1,0:T(8,128)S(1)}, f32[1,16,2,8,128]{4,3,2,1,0:T(8,128)S(1)}, u32[]{:S(2)}, u32[]{:S(2)}) collective-permute-start(f32[1,16,2,8,128]{4,3,2,1,0:T(8,128)S(1)} %get-tuple-element.117), channel_id=1, source_target_pairs={{0,24},{4,28},{8,16},{12,20},{16,8},{20,12},{24,0},{28,4},{1,25},{... | collective-permute-start | bytes 393224 | tf_op jit(solution)/shard_map/ppermute | solution.py:344
  60.3 10.9 %collective-permute-start.11 = (f32[1,16,2,8,128]{4,3,2,1,0:T(8,128)S(1)}, f32[1,16,2,8,128]{4,3,2,1,0:T(8,128)S(1)}, u32[]{:S(2)}, u32[]{:S(2)}) collective-permute-start(f32[1,16,2,8,128]{4,3,2,1,0:T(8,128)S(1)} %bitcast.9), channel_id=1, source_target_pairs={{0,24},{4,28},{8,16},{12,20},{16,8},{20,12},{24,0},{28,4},{1,25},{... | collective-permute-start | bytes 393224 | tf_op jit(solution)/shard_map/ppermute | solution.py:344
  63.8 7.4 %collective-permute-start.10 = (f32[1,16,2,8,128]{4,3,2,1,0:T(8,128)S(1)}, f32[1,16,2,8,128]{4,3,2,1,0:T(8,128)S(1)}, u32[]{:S(2)}, u32[]{:S(2)}) collective-permute-start(f32[1,16,2,8,128]{4,3,2,1,0:T(8,128)S(1)} %bitcast.10), channel_id=1, source_target_pairs={{0,8},{4,12},{8,0},{12,4},{16,24},{20,28},{24,16},{28,20},{1,9},{5... | collective-permute-start | bytes 393224 | tf_op jit(solution)/shard_map/ppermute | solution.py:344
  64.9 9.3 %collective-permute-start.9 = (f32[1,16,2,8,128]{4,3,2,1,0:T(8,128)S(1)}, f32[1,16,2,8,128]{4,3,2,1,0:T(8,128)S(1)}, u32[]{:S(2)}, u32[]{:S(2)}) collective-permute-start(f32[1,16,2,8,128]{4,3,2,1,0:T(8,128)S(1)} %bitcast.11), channel_id=1, source_target_pairs={{0,16},{4,20},{8,24},{12,28},{16,0},{20,4},{24,8},{28,12},{1,17},{... | collective-permute-start | bytes 393224 | tf_op jit(solution)/shard_map/ppermute | solution.py:344
  74.3 9.3 %collective-permute-start.13 = (f32[4,8,2,8,128]{4,3,2,1,0:T(8,128)S(1)}, f32[4,8,2,8,128]{4,3,2,1,0:T(8,128)S(1)}, u32[]{:S(2)}, u32[]{:S(2)}) collective-permute-start(f32[4,8,2,8,128]{4,3,2,1,0:T(8,128)S(1)} %get-tuple-element.168), channel_id=1, source_target_pairs={{0,2},{1,3},{2,0},{3,1},{4,6},{5,7},{6,4},{7,5},{8,10},{9,11},{10,... | collective-permute-start | bytes 786440 | tf_op jit(solution)/shard_map/ppermute | solution.py:344
  76.2 9.2 %collective-permute-start.12 = (f32[4,8,2,8,128]{4,3,2,1,0:T(8,128)S(1)}, f32[4,8,2,8,128]{4,3,2,1,0:T(8,128)S(1)}, u32[]{:S(2)}, u32[]{:S(2)}) collective-permute-start(f32[4,8,2,8,128]{4,3,2,1,0:T(8,128)S(1)} %get-tuple-element.169), channel_id=1, source_target_pairs={{0,4},{4,0},{8,12},{12,8},{16,20},{20,16},{24,28},{28,24},{1,5},{5... | collective-permute-start | bytes 786440 | tf_op jit(solution)/shard_map/ppermute | solution.py:344
  76.8 14.0 %collective-permute-start.16 = (f32[4,8,2,8,128]{4,3,2,1,0:T(8,128)S(1)}, f32[4,8,2,8,128]{4,3,2,1,0:T(8,128)S(1)}, u32[]{:S(2)}, u32[]{:S(2)}) collective-permute-start(f32[4,8,2,8,128]{4,3,2,1,0:T(8,128)S(1)} %get-tuple-element.168), channel_id=1, source_target_pairs={{0,4},{4,0},{8,12},{12,8},{16,20},{20,16},{24,28},{28,24},{1,5},{5... | collective-permute-start | bytes 786440 | tf_op jit(solution)/shard_map/ppermute | solution.py:344
  78.2 12.6 %collective-permute-start.14 = (f32[4,8,2,8,128]{4,3,2,1,0:T(8,128)S(1)}, f32[4,8,2,8,128]{4,3,2,1,0:T(8,128)S(1)}, u32[]{:S(2)}, u32[]{:S(2)}) collective-permute-start(f32[4,8,2,8,128]{4,3,2,1,0:T(8,128)S(1)} %get-tuple-element.169), channel_id=1, source_target_pairs={{0,2},{1,3},{2,0},{3,1},{4,6},{5,7},{6,4},{7,5},{8,10},{9,11},{10,... | collective-permute-start | bytes 786440 | tf_op jit(solution)/shard_map/ppermute | solution.py:344
  78.4 15.8 %collective-permute-start.18 = (f32[4,16,2,8,128]{4,3,2,1,0:T(8,128)S(1)}, f32[4,16,2,8,128]{4,3,2,1,0:T(8,128)S(1)}, u32[]{:S(2)}, u32[]{:S(2)}) collective-permute-start(f32[4,16,2,8,128]{4,3,2,1,0:T(8,128)S(1)} %pad_maximum_fusion.refs_0_), channel_id=1, source_target_pairs={{0,1},{1,0},{2,3},{3,2},{4,5},{5,4},{6,7},{7,6},{8,9},{9,8},{10,11... | collective-permute-start | bytes 1572872 | tf_op jit(solution)/shard_map/ppermute | solution.py:344
  85.4 7.3 %collective-permute-start.15 = (f32[4,8,2,8,128]{4,3,2,1,0:T(8,128)S(1)}, f32[4,8,2,8,128]{4,3,2,1,0:T(8,128)S(1)}, u32[]{:S(2)}, u32[]{:S(2)}) collective-permute-start(f32[4,8,2,8,128]{4,3,2,1,0:T(8,128)S(1)} %collective-permute-done.12), channel_id=1, source_target_pairs={{0,2},{1,3},{2,0},{3,1},{4,6},{5,7},{6,4},{7,5},{8,10},{9,11},{10,... | collective-permute-start | bytes 786440 | tf_op jit(solution)/shard_map/ppermute | solution.py:344
  85.6 8.5 %collective-permute-start.17 = (f32[4,8,2,8,128]{4,3,2,1,0:T(8,128)S(1)}, f32[4,8,2,8,128]{4,3,2,1,0:T(8,128)S(1)}, u32[]{:S(2)}, u32[]{:S(2)}) collective-permute-start(f32[4,8,2,8,128]{4,3,2,1,0:T(8,128)S(1)} %collective-permute-done.13), channel_id=1, source_target_pairs={{0,4},{4,0},{8,12},{12,8},{16,20},{20,16},{24,28},{28,24},{1,5},{5... | collective-permute-start | bytes 786440 | tf_op jit(solution)/shard_map/ppermute | solution.py:344
  90.7 1.5 %collective-permute-start.22 = (f32[4,8,2,8,128]{4,3,2,1,0:T(8,128)S(1)}, f32[4,8,2,8,128]{4,3,2,1,0:T(8,128)S(1)}, u32[]{:S(2)}, u32[]{:S(2)}) collective-permute-start(f32[4,8,2,8,128]{4,3,2,1,0:T(8,128)S(1)} %collective-permute-done.16.refs_4_), channel_id=1, source_target_pairs={{0,1},{1,0},{2,3},{3,2},{4,5},{5,4},{6,7},{7,6},{8,9},{9,8},{10,11... | collective-permute-start | bytes 786440 | tf_op jit(solution)/shard_map/ppermute | solution.py:344
  90.8 4.9 %collective-permute-start.19 = (f32[4,16,2,8,128]{4,3,2,1,0:T(8,128)S(1)}, f32[4,16,2,8,128]{4,3,2,1,0:T(8,128)S(1)}, u32[]{:S(2)}, u32[]{:S(2)}) collective-permute-start(f32[4,16,2,8,128]{4,3,2,1,0:T(8,128)S(1)} %constant_dynamic-update-slice_fusion.refs_1_), channel_id=1, source_target_pairs={{0,1},{1,0},{2,3},{3,2},{4,5},{5,4},{6,7},{7,6},{8,9},{9,8},{10,11... | collective-permute-start | bytes 1572872 | tf_op jit(solution)/shard_map/ppermute | solution.py:344
  92.3 1.9 %collective-permute-start.20 = (f32[4,8,2,8,128]{4,3,2,1,0:T(8,128)S(1)}, f32[4,8,2,8,128]{4,3,2,1,0:T(8,128)S(1)}, u32[]{:S(2)}, u32[]{:S(2)}) collective-permute-start(f32[4,8,2,8,128]{4,3,2,1,0:T(8,128)S(1)} %collective-permute-done.14.refs_2_), channel_id=1, source_target_pairs={{0,1},{1,0},{2,3},{3,2},{4,5},{5,4},{6,7},{7,6},{8,9},{9,8},{10,11... | collective-permute-start | bytes 786440 | tf_op jit(solution)/shard_map/ppermute | solution.py:344
  92.7 1.5 %collective-permute-start.21 = (f32[4,8,2,8,128]{4,3,2,1,0:T(8,128)S(1)}, f32[4,8,2,8,128]{4,3,2,1,0:T(8,128)S(1)}, u32[]{:S(2)}, u32[]{:S(2)}) collective-permute-start(f32[4,8,2,8,128]{4,3,2,1,0:T(8,128)S(1)} %collective-permute-done.15.refs_3_), channel_id=1, source_target_pairs={{0,1},{1,0},{2,3},{3,2},{4,5},{5,4},{6,7},{7,6},{8,9},{9,8},{10,11... | collective-permute-start | bytes 786440 | tf_op jit(solution)/shard_map/ppermute | solution.py:344
  94.2 1.5 %collective-permute-start.23 = (f32[4,8,2,8,128]{4,3,2,1,0:T(8,128)S(1)}, f32[4,8,2,8,128]{4,3,2,1,0:T(8,128)S(1)}, u32[]{:S(2)}, u32[]{:S(2)}) collective-permute-start(f32[4,8,2,8,128]{4,3,2,1,0:T(8,128)S(1)} %collective-permute-done.17.refs_5_), channel_id=1, source_target_pairs={{0,1},{1,0},{2,3},{3,2},{4,5},{5,4},{6,7},{7,6},{8,9},{9,8},{10,11... | collective-permute-start | bytes 786440 | tf_op jit(solution)/shard_map/ppermute | solution.py:344

commit v7 on v6

--- a/solution.py
+++ b/solution.py
@@ -408,13 +408,14 @@
     every, low, high = slice(None), slice(n_gz // 2), slice(n_gz // 2, None)
     a = [a[0], swap(a[1], "phi", 1)]
     b = [b[0], swap(b[1], "phi", 1)]
-    (a_sent,) = sums([[(term, (1,)) for term in a]])
-    (b_sent,) = sums([[(term, (every, high)) for term in b]])
-    got = (swap(a_sent, "phi", 2), swap(b_sent, "gz", 1))
-    a_got, b_got = filler.beside((a_sent, b_sent), got, 2)
+    a_first, a_last = sums([[(term, (1, high)) for term in a]], [[(term, (1, low)) for term in a]])
+    b_first, b_last = sums([[(term, (1, high)) for term in b]], [[(term, (0, high)) for term in b]])
+    got = (swap(a_first, "phi", 2), swap(b_first, "gz", 1))
+    a_rest, b_rest = swap(a_last, "phi", 2), swap(b_last, "gz", 1)
+    a_got, b_got = filler.beside((a_first, b_first), got, 2)
     a_sent, b_sent = sums(
-        [[(term, (0, high)) for term in a] + [(a_got, (high,))]],
-        [[(term, (1, low)) for term in b] + [(b_got, (1,))]],
+        [[(term, (0, high)) for term in a] + [(a_got, (every,))]],
+        [[(term, (1, low)) for term in b] + [(b_got, (every,))]],
     )
     got = (swap(a_sent, "gz", 1), swap(b_sent, "phi", 2))
     a_new, b_new = filler.beside((a_sent, b_sent), got)
@@ -422,8 +423,8 @@
     def rest(i, size):
         rows = slice(i * size, (i + 1) * size)
         return [
-            [(term, (0, rows)) for term in a] + [(a_got, (rows,)), (a_new, (rows,))],
-            [(term, (0, rows)) for term in b] + [(b_got, (0, rows)), (b_new, (rows,))],
+            [(term, (0, rows)) for term in a] + [(a_rest, (rows,)), (a_new, (rows,))],
+            [(term, (0, rows)) for term in b] + [(b_rest, (rows,)), (b_new, (rows,))],
         ]
 
     left = n_gz // 2

time: 120 us -> 124 us (1.033)
  starting transfers between devices: 23 us -> 25.1 us
    ppermute x24 -> x26, starting transfers between devices: 23 us -> 25.1 us  [swap(): return lax.ppermute(x, axis, [(i, i ^ bit) for i in range(count)])]
    ppermute x24 -> x26, waiting for transfers between devices: 23.6 us -> 24.5 us  [swap(): return lax.ppermute(x, axis, [(i, i ^ bit) for i in range(count)])]
  transfers between devices with their start and end apart: 24 -> 26, of which waited for: 15 -> 14; matrix products, arithmetic and copies ran while one was open for 0% -> 0% of each run, Pallas kernels for 23% -> 23%
where the time goes in v7:
time: 124 us; the launch traced here: 123 us
  Pallas kernels  72.8 us (59%)
  starting transfers between devices  25.1 us (20%)
  waiting for transfers between devices  24.5 us (20%)
    pallas_call x8, Pallas kernels, local_mix(): pl.pallas_call(local_kernel, grid=(steps,), in_specs=[block, block, pl.Bl...  25.5 us
    ppermute x26, starting transfers between devices, swap(): return lax.ppermute(x, axis, [(i, i ^ bit) for i in range(count)])  25.1 us
    pallas_call x1, Pallas kernels, inverse(): pl.pallas_call(functools.partial(inverse_kernel, n_phi=n_phi, width=width...  24.6 us
    ppermute x26, waiting for transfers between devices, swap(): return lax.ppermute(x, axis, [(i, i ^ bit) for i in range(count)])  24.5 us
    pallas_call x1, Pallas kernels, forward(): pl.pallas_call(functools.partial(forward_kernel, n_gz=n_gz, n_phi=n_phi),...  19.2 us
    pallas_call x1, Pallas kernels, tables(): pl.pallas_call(functools.partial(tables_kernel, n_gz=n_gz, n_phi=n_phi, s...  2.75 us
  transfers between devices with their start and end apart: 26, of which 14 were waited for; matrix products, arithmetic and copies ran while one was open for 0% of the time, Pallas kernels for 23%

profile of v7, /device:TPU:0, one launch (start us, length us, event | category | flops | bytes accessed | tf_op | source)
XLA Modules:
  0.0 123.4 jit_solution(5547702623635984728)
XLA Ops:
  0.6 19.2 %forward_transform.1 = (f32[2,8,8,2,8,128]{5,4,3,2,1,0:T(8,128)S(1)}, f32[2,8,8,2,8,128]{5,4,3,2,1,0:T(8,128)S(1)}, f32[2,8,8,2,8,128]{5,4,3,2,1,0:T(8,128)S(1)}, f32[2,8,8,2,8,128]{5,4,3,2,1,0:T(8,128)S(1)}) custom-call(s32[64]{0:T(128)} %z_modes.2, s32[64]{0:T(128)} %phi_modes.2, f32[16,4,256,256]{3,2,1,0:T(8,128)} %x_ref.9, f32[16,4,256,256]{3,2,1,0:T(8,128)} %t_ref.9), custom_call_target="tpu_custom_call" | custom-call | flops 12884901888 | bytes 33554432 | tf_op jit(solution)/shard_map/forward_transform/pallas_call | solution.py:174
  19.8 0.5 collective-permute-start
  20.3 0.1 collective-permute-start.3
  20.4 2.2 %collective-permute-done.refs_1_ = f32[2,8,8,2,8,128]{5,4,3,2,1,0:T(8,128)S(1)} collective-permute-done((f32[2,8,8,2,8,128]{5,4,3,2,1,0:T(8,128)S(1)}, f32[2,8,8,2,8,128]{5,4,3,2,1,0:T(8,128)S(1)}, u32[]{:S(2)}, u32[]{:S(2)}) %collective-permute-start) | collective-permute-done | bytes 1048608 | tf_op jit(solution)/shard_map/ppermute | solution.py:344
  22.7 0.1 add_terms.4
  22.7 2.9 %collective-permute-start.2 = (f32[4,8,2,8,128]{4,3,2,1,0:T(8,128)S(1)}, f32[4,8,2,8,128]{4,3,2,1,0:T(8,128)S(1)}, u32[]{:S(2)}, u32[]{:S(2)}) collective-permute-start(f32[4,8,2,8,128]{4,3,2,1,0:T(8,128)S(1)} %get-tuple-element.92), channel_id=1, source_target_pairs={{0,2},{1,3},{2,0},{3,1},{4,6},{5,7},{6,4},{7,5},{8,10},{9,11},{10,... | collective-permute-start | bytes 786440 | tf_op jit(solution)/shard_map/ppermute | solution.py:344
  25.6 0.0 collective-permute-done.3.refs_1_.refs_4_.refs_5_
  25.7 0.1 add_terms.5
  25.7 1.6 %collective-permute-start.4 = (f32[4,8,2,8,128]{4,3,2,1,0:T(8,128)S(1)}, f32[4,8,2,8,128]{4,3,2,1,0:T(8,128)S(1)}, u32[]{:S(2)}, u32[]{:S(2)}) collective-permute-start(f32[4,8,2,8,128]{4,3,2,1,0:T(8,128)S(1)} %get-tuple-element.95), channel_id=1, source_target_pairs={{0,4},{4,0},{8,12},{12,8},{16,20},{20,16},{24,28},{28,24},{1,5},{5... | collective-permute-start | bytes 786440 | tf_op jit(solution)/shard_map/ppermute | solution.py:344
  27.3 2.8 %small_tables.1 = (bf16[256,256]{1,0:T(8,128)(2,1)S(1)}, f32[16,8,256]{2,1,0:T(8,128)S(1)}, bf16[384,512]{1,0:T(8,128)(2,1)S(1)}, bf16[256,384]{1,0:T(8,128)(2,1...) custom-call(s32[64]{0:T(128)S(1)} %copy-done.4, s32[64]{0:T(128)S(1)} %copy-done.5, f32[16]{0:T(128)S(1)} %copy-done.6, ...), custom_call_target="tpu_custom_call" | custom-call | tf_op jit(solution)/shard_map/small_tables/pallas_call | solution.py:550
  30.1 3.3 %local_mix.9 = (f32[16,128,256]{2,1,0:T(8,128)S(1)}, f32[16,128,256]{2,1,0:T(8,128)S(1)}) custom-call(f32[16,4,256,256]{3,2,1,0:T(8,128)} %x_ref.9, f32[16,4,256,256]{3,2,1,0:T(8,128)} %t_ref.9, bf16[256,256]{1,0:T(8,128)(2,1)S(1)} %get-tuple-element.103.w_ref, f32[16,8,256]{2,1,0:T(8,128)S(1)} %get-tuple-element.104.bias_ref), custom_call_target="tpu_custom_call" | custom-call | flops 536870912 | bytes 4194304 | tf_op jit(solution)/shard_map/local_mix/pallas_call | solution.py:217
  33.5 3.3 %local_mix.8 = (f32[16,128,256]{2,1,0:T(8,128)S(1)}, f32[16,128,256]{2,1,0:T(8,128)S(1)}) custom-call(f32[16,4,256,256]{3,2,1,0:T(8,128)} %x_ref.9, f32[16,4,256,256]{3,2,1,0:T(8,128)} %t_ref.9, bf16[256,256]{1,0:T(8,128)(2,1)S(1)} %get-tuple-element.103.w_ref, f32[16,8,256]{2,1,0:T(8,128)S(1)} %get-tuple-element.104.bias_ref), custom_call_target="tpu_custom_call" | custom-call | flops 536870912 | bytes 4194304 | tf_op jit(solution)/shard_map/local_mix/pallas_call | solution.py:217
  36.8 0.0 collective-permute-done.2.refs_2_
  36.8 0.0 collective-permute-done.4.refs_5_
  36.8 0.1 add_terms.6
  37.0 0.6 collective-permute-start.5
  37.5 1.3 %collective-permute-start.6 = (f32[4,8,2,8,128]{4,3,2,1,0:T(8,128)S(1)}, f32[4,8,2,8,128]{4,3,2,1,0:T(8,128)S(1)}, u32[]{:S(2)}, u32[]{:S(2)}) collective-permute-start(f32[4,8,2,8,128]{4,3,2,1,0:T(8,128)S(1)} %get-tuple-element.114), channel_id=1, source_target_pairs={{0,2},{1,3},{2,0},{3,1},{4,6},{5,7},{6,4},{7,5},{8,10},{9,11},{10,... | collective-permute-start | bytes 786440 | tf_op jit(solution)/shard_map/ppermute | solution.py:344
  38.9 0.7 collective-permute-start.1
  39.6 1.5 %collective-permute-start.7 = (f32[4,8,2,8,128]{4,3,2,1,0:T(8,128)S(1)}, f32[4,8,2,8,128]{4,3,2,1,0:T(8,128)S(1)}, u32[]{:S(2)}, u32[]{:S(2)}) collective-permute-start(f32[4,8,2,8,128]{4,3,2,1,0:T(8,128)S(1)} %get-tuple-element.120), channel_id=1, source_target_pairs={{0,4},{4,0},{8,12},{12,8},{16,20},{20,16},{24,28},{28,24},{1,5},{5... | collective-permute-start | bytes 786440 | tf_op jit(solution)/shard_map/ppermute | solution.py:344
  41.1 3.1 %local_mix.10 = (f32[16,128,256]{2,1,0:T(8,128)S(1)}, f32[16,128,256]{2,1,0:T(8,128)S(1)}) custom-call(f32[16,4,256,256]{3,2,1,0:T(8,128)} %x_ref.9, f32[16,4,256,256]{3,2,1,0:T(8,128)} %t_ref.9, bf16[256,256]{1,0:T(8,128)(2,1)S(1)} %get-tuple-element.103.w_ref, f32[16,8,256]{2,1,0:T(8,128)S(1)} %get-tuple-element.104.bias_ref), custom_call_target="tpu_custom_call" | custom-call | flops 536870912 | bytes 4194304 | tf_op jit(solution)/shard_map/local_mix/pallas_call | solution.py:217
  44.2 2.0 %collective-permute-done.5.refs_3_ = f32[4,8,2,8,128]{4,3,2,1,0:T(8,128)S(1)} collective-permute-done((f32[4,8,2,8,128]{4,3,2,1,0:T(8,128)S(1)}, f32[4,8,2,8,128]{4,3,2,1,0:T(8,128)S(1)}, u32[]{:S(2)}, u32[]{:S(2)}) %collective-permute-start.5) | collective-permute-done | bytes 262176 | tf_op jit(solution)/shard_map/ppermute | solution.py:344
  46.2 0.5 collective-permute-done.6.refs_7_
  46.8 3.9 %collective-permute-done.1.refs_2_ = f32[4,8,2,8,128]{4,3,2,1,0:T(8,128)S(1)} collective-permute-done((f32[4,8,2,8,128]{4,3,2,1,0:T(8,128)S(1)}, f32[4,8,2,8,128]{4,3,2,1,0:T(8,128)S(1)}, u32[]{:S(2)}, u32[]{:S(2)}) %collective-permute-start.1) | collective-permute-done | bytes 262176 | tf_op jit(solution)/shard_map/ppermute | solution.py:344
  50.6 0.0 collective-permute-done.7.refs_6_
  50.6 0.1 add_terms.7
  50.8 2.8 %collective-permute-start.8 = (f32[1,16,2,8,128]{4,3,2,1,0:T(8,128)S(1)}, f32[1,16,2,8,128]{4,3,2,1,0:T(8,128)S(1)}, u32[]{:S(2)}, u32[]{:S(2)}) collective-permute-start(f32[1,16,2,8,128]{4,3,2,1,0:T(8,128)S(1)} %get-tuple-element.123), channel_id=1, source_target_pairs={{0,16},{4,20},{8,24},{12,28},{16,0},{20,4},{24,8},{28,12},{1,17},{... | collective-permute-start | bytes 393224 | tf_op jit(solution)/shard_map/ppermute | solution.py:344
  53.6 1.6 %collective-permute-start.9 = (f32[1,16,2,8,128]{4,3,2,1,0:T(8,128)S(1)}, f32[1,16,2,8,128]{4,3,2,1,0:T(8,128)S(1)}, u32[]{:S(2)}, u32[]{:S(2)}) collective-permute-start(f32[1,16,2,8,128]{4,3,2,1,0:T(8,128)S(1)} %get-tuple-element.124), channel_id=1, source_target_pairs={{0,8},{4,12},{8,0},{12,4},{16,24},{20,28},{24,16},{28,20},{1,9},{5... | collective-permute-start | bytes 393224 | tf_op jit(solution)/shard_map/ppermute | solution.py:344
  55.2 0.1 collective-permute-start.10
  55.2 3.1 %local_mix.12 = (f32[16,128,256]{2,1,0:T(8,128)S(1)}, f32[16,128,256]{2,1,0:T(8,128)S(1)}) custom-call(f32[16,4,256,256]{3,2,1,0:T(8,128)} %x_ref.9, f32[16,4,256,256]{3,2,1,0:T(8,128)} %t_ref.9, bf16[256,256]{1,0:T(8,128)(2,1)S(1)} %get-tuple-element.103.w_ref, f32[16,8,256]{2,1,0:T(8,128)S(1)} %get-tuple-element.104.bias_ref), custom_call_target="tpu_custom_call" | custom-call | flops 536870912 | bytes 4194304 | tf_op jit(solution)/shard_map/local_mix/pallas_call | solution.py:217
  58.4 3.2 %local_mix.11 = (f32[16,128,256]{2,1,0:T(8,128)S(1)}, f32[16,128,256]{2,1,0:T(8,128)S(1)}) custom-call(f32[16,4,256,256]{3,2,1,0:T(8,128)} %x_ref.9, f32[16,4,256,256]{3,2,1,0:T(8,128)} %t_ref.9, bf16[256,256]{1,0:T(8,128)(2,1)S(1)} %get-tuple-element.103.w_ref, f32[16,8,256]{2,1,0:T(8,128)S(1)} %get-tuple-element.104.bias_ref), custom_call_target="tpu_custom_call" | custom-call | flops 536870912 | bytes 4194304 | tf_op jit(solution)/shard_map/local_mix/pallas_call | solution.py:217
  61.5 0.0 collective-permute-done.8
  61.5 0.0 collective-permute-done.9
  61.5 1.1 collective-permute-done.10
  62.7 0.4 mode_mix.1
  63.1 3.5 %collective-permute-start.13 = (f32[1,16,2,8,128]{4,3,2,1,0:T(8,128)S(1)}, f32[1,16,2,8,128]{4,3,2,1,0:T(8,128)S(1)}, u32[]{:S(2)}, u32[]{:S(2)}) collective-permute-start(f32[1,16,2,8,128]{4,3,2,1,0:T(8,128)S(1)} %bitcast.9), channel_id=1, source_target_pairs={{0,24},{4,28},{8,16},{12,20},{16,8},{20,12},{24,0},{28,4},{1,25},{... | collective-permute-start | bytes 393224 | tf_op jit(solution)/shard_map/ppermute | solution.py:344
  66.6 1.3 %collective-permute-start.12 = (f32[1,16,2,8,128]{4,3,2,1,0:T(8,128)S(1)}, f32[1,16,2,8,128]{4,3,2,1,0:T(8,128)S(1)}, u32[]{:S(2)}, u32[]{:S(2)}) collective-permute-start(f32[1,16,2,8,128]{4,3,2,1,0:T(8,128)S(1)} %bitcast.10), channel_id=1, source_target_pairs={{0,8},{4,12},{8,0},{12,4},{16,24},{20,28},{24,16},{28,20},{1,9},{5... | collective-permute-start | bytes 393224 | tf_op jit(solution)/shard_map/ppermute | solution.py:344
  67.9 0.0 collective-permute-start.11
  67.9 3.1 %local_mix.14 = (f32[16,128,256]{2,1,0:T(8,128)S(1)}, f32[16,128,256]{2,1,0:T(8,128)S(1)}) custom-call(f32[16,4,256,256]{3,2,1,0:T(8,128)} %x_ref.9, f32[16,4,256,256]{3,2,1,0:T(8,128)} %t_ref.9, bf16[256,256]{1,0:T(8,128)(2,1)S(1)} %get-tuple-element.103.w_ref, f32[16,8,256]{2,1,0:T(8,128)S(1)} %get-tuple-element.104.bias_ref), custom_call_target="tpu_custom_call" | custom-call | flops 536870912 | bytes 4194304 | tf_op jit(solution)/shard_map/local_mix/pallas_call | solution.py:217
  71.1 3.2 %local_mix.13 = (f32[16,128,256]{2,1,0:T(8,128)S(1)}, f32[16,128,256]{2,1,0:T(8,128)S(1)}) custom-call(f32[16,4,256,256]{3,2,1,0:T(8,128)} %x_ref.9, f32[16,4,256,256]{3,2,1,0:T(8,128)} %t_ref.9, bf16[256,256]{1,0:T(8,128)(2,1)S(1)} %get-tuple-element.103.w_ref, f32[16,8,256]{2,1,0:T(8,128)S(1)} %get-tuple-element.104.bias_ref), custom_call_target="tpu_custom_call" | custom-call | flops 536870912 | bytes 4194304 | tf_op jit(solution)/shard_map/local_mix/pallas_call | solution.py:217
  74.2 0.0 collective-permute-done.13
  74.2 0.0 collective-permute-done.12
  74.2 2.9 %collective-permute-done.11 = f32[1,16,2,8,128]{4,3,2,1,0:T(8,128)S(1)} collective-permute-done((f32[1,16,2,8,128]{4,3,2,1,0:T(8,128)S(1)}, f32[1,16,2,8,128]{4,3,2,1,0:T(8,128)S(1)}, u32[]{:S(2)}, u32[]{:S(2)}) %collective-permute-start.11) | collective-permute-done | bytes 131104 | tf_op jit(solution)/shard_map/ppermute | solution.py:344
  77.2 1.8 %collective-permute-start.15 = (f32[4,8,2,8,128]{4,3,2,1,0:T(8,128)S(1)}, f32[4,8,2,8,128]{4,3,2,1,0:T(8,128)S(1)}, u32[]{:S(2)}, u32[]{:S(2)}) collective-permute-start(f32[4,8,2,8,128]{4,3,2,1,0:T(8,128)S(1)} %get-tuple-element.176), channel_id=1, source_target_pairs={{0,2},{1,3},{2,0},{3,1},{4,6},{5,7},{6,4},{7,5},{8,10},{9,11},{10,... | collective-permute-start | bytes 786440 | tf_op jit(solution)/shard_map/ppermute | solution.py:344
  79.0 1.4 %collective-permute-start.14 = (f32[4,8,2,8,128]{4,3,2,1,0:T(8,128)S(1)}, f32[4,8,2,8,128]{4,3,2,1,0:T(8,128)S(1)}, u32[]{:S(2)}, u32[]{:S(2)}) collective-permute-start(f32[4,8,2,8,128]{4,3,2,1,0:T(8,128)S(1)} %get-tuple-element.177), channel_id=1, source_target_pairs={{0,4},{4,0},{8,12},{12,8},{16,20},{20,16},{24,28},{28,24},{1,5},{5... | collective-permute-start | bytes 786440 | tf_op jit(solution)/shard_map/ppermute | solution.py:344
  80.4 0.7 collective-permute-start.18
  81.0 0.3 collective-permute-start.16
  81.3 0.0 collective-permute-start.20
  81.3 3.1 %local_mix.15 = (f32[16,128,256]{2,1,0:T(8,128)S(1)}, f32[16,128,256]{2,1,0:T(8,128)S(1)}) custom-call(f32[16,4,256,256]{3,2,1,0:T(8,128)} %x_ref.9, f32[16,4,256,256]{3,2,1,0:T(8,128)} %t_ref.9, bf16[256,256]{1,0:T(8,128)(2,1)S(1)} %get-tuple-element.103.w_ref, f32[16,8,256]{2,1,0:T(8,128)S(1)} %get-tuple-element.104.bias_ref), custom_call_target="tpu_custom_call" | custom-call | flops 536870912 | bytes 4194304 | tf_op jit(solution)/shard_map/local_mix/pallas_call | solution.py:217
  84.5 2.0 %collective-permute-done.15 = f32[4,8,2,8,128]{4,3,2,1,0:T(8,128)S(1)} collective-permute-done((f32[4,8,2,8,128]{4,3,2,1,0:T(8,128)S(1)}, f32[4,8,2,8,128]{4,3,2,1,0:T(8,128)S(1)}, u32[]{:S(2)}, u32[]{:S(2)}) %collective-permute-start.15) | collective-permute-done | bytes 262176 | tf_op jit(solution)/shard_map/ppermute | solution.py:344
  86.5 1.7 %collective-permute-done.14 = f32[4,8,2,8,128]{4,3,2,1,0:T(8,128)S(1)} collective-permute-done((f32[4,8,2,8,128]{4,3,2,1,0:T(8,128)S(1)}, f32[4,8,2,8,128]{4,3,2,1,0:T(8,128)S(1)}, u32[]{:S(2)}, u32[]{:S(2)}) %collective-permute-start.14) | collective-permute-done | bytes 262176 | tf_op jit(solution)/shard_map/ppermute | solution.py:344
  88.2 0.3 collective-permute-start.17
  88.6 1.4 %collective-permute-start.19 = (f32[4,8,2,8,128]{4,3,2,1,0:T(8,128)S(1)}, f32[4,8,2,8,128]{4,3,2,1,0:T(8,128)S(1)}, u32[]{:S(2)}, u32[]{:S(2)}) collective-permute-start(f32[4,8,2,8,128]{4,3,2,1,0:T(8,128)S(1)} %collective-permute-done.15), channel_id=1, source_target_pairs={{0,4},{4,0},{8,12},{12,8},{16,20},{20,16},{24,28},{28,24},{1,5},{5... | collective-permute-start | bytes 786440 | tf_op jit(solution)/shard_map/ppermute | solution.py:344
  90.0 3.9 %collective-permute-done.18.refs_4_ = f32[4,8,2,8,128]{4,3,2,1,0:T(8,128)S(1)} collective-permute-done((f32[4,8,2,8,128]{4,3,2,1,0:T(8,128)S(1)}, f32[4,8,2,8,128]{4,3,2,1,0:T(8,128)S(1)}, u32[]{:S(2)}, u32[]{:S(2)}) %collective-permute-start.18) | collective-permute-done | bytes 262176 | tf_op jit(solution)/shard_map/ppermute | solution.py:344
  93.9 0.0 collective-permute-start.24
  93.9 0.0 collective-permute-done.16.refs_2_
  93.9 0.6 collective-permute-start.21
  94.5 0.9 collective-permute-done.24.refs_10_
  95.4 0.1 collective-permute-start.22
  95.5 0.3 collective-permute-done.17.refs_3_
  95.9 0.0 collective-permute-start.23
  95.9 1.4 %collective-permute-done.19.refs_5_ = f32[4,8,2,8,128]{4,3,2,1,0:T(8,128)S(1)} collective-permute-done((f32[4,8,2,8,128]{4,3,2,1,0:T(8,128)S(1)}, f32[4,8,2,8,128]{4,3,2,1,0:T(8,128)S(1)}, u32[]{:S(2)}, u32[]{:S(2)}) %collective-permute-start.19) | collective-permute-done | bytes 262176 | tf_op jit(solution)/shard_map/ppermute | solution.py:344
  97.3 0.1 collective-permute-done.23.refs_9_
  97.4 1.4 %collective-permute-done.25.refs_11_ = f32[4,8,2,8,128]{4,3,2,1,0:T(8,128)S(1)} collective-permute-done((f32[4,8,2,8,128]{4,3,2,1,0:T(8,128)S(1)}, f32[4,8,2,8,128]{4,3,2,1,0:T(8,128)S(1)}, u32[]{:S(2)}, u32[]{:S(2)}) %collective-permute-start.25) | collective-permute-done | bytes 262176 | tf_op jit(solution)/shard_map/ppermute | solution.py:344
  98.9 24.6 %inverse_transform.1 = (f32[16,4,256,256]{3,2,1,0:T(8,128)}, f32[16,4,256,256]{3,2,1,0:T(8,128)}) custom-call(f32[4,16,2,8,128]{4,3,2,1,0:T(8,128)S(1)} %pad_maximum_fusion.refs_0_, f32[4,16,2,8,128]{4,3,2,1,0:T(8,128)S(1)} %constant_dynamic-update-slice_fusion.refs_1_, f32[4,8,2,8,128]{4,3,2,1,0:T(8,128)S(1)} %collective-permute-done.16.refs_2_, ...), custom_call_target="tpu_custom_call" | custom-call | flops 6710886400 | bytes 67108864 | tf_op jit(solution)/shard_map/inverse_transform/pallas_call | solution.py:323
  (23 shorter events, 0.2 us)
Async XLA Ops:
  19.8 2.8 %collective-permute-start = (f32[2,8,8,2,8,128]{5,4,3,2,1,0:T(8,128)S(1)}, f32[2,8,8,2,8,128]{5,4,3,2,1,0:T(8,128)S(1)}, u32[]{:S(2)}, u32[]{:S(2)}) collective-permute-start(f32[2,8,8,2,8,128]{5,4,3,2,1,0:T(8,128)S(1)} %get-tuple-element.90), channel_id=1, source_target_pairs={{0,1},{1,0},{2,3},{3,2},{4,5},{5,4},{6,7},{7,6},{8,9},{9,8},{10,11... | collective-permute-start | bytes 3145736 | tf_op jit(solution)/shard_map/ppermute | solution.py:344
  20.3 5.3 %collective-permute-start.3 = (f32[2,8,8,2,8,128]{5,4,3,2,1,0:T(8,128)S(1)}, f32[2,8,8,2,8,128]{5,4,3,2,1,0:T(8,128)S(1)}, u32[]{:S(2)}, u32[]{:S(2)}) collective-permute-start(f32[2,8,8,2,8,128]{5,4,3,2,1,0:T(8,128)S(1)} %get-tuple-element.94), channel_id=1, source_target_pairs={{0,1},{1,0},{2,3},{3,2},{4,5},{5,4},{6,7},{7,6},{8,9},{9,8},{10,11... | collective-permute-start | bytes 3145736 | tf_op jit(solution)/shard_map/ppermute | solution.py:344
  22.6 4.7 %copy-start = (f32[2,16,16,8,16]{4,3,2,1,0:T(8,128)S(1)}, f32[2,16,16,8,16]{4,3,2,1,0:T(8,128)}, u32[]{:S(2)}) copy-start(f32[2,16,16,8,16]{4,3,2,1,0:T(8,128)} %param.9) | copy-start | bytes 786436
  22.6 4.7 %copy-start.3 = (f32[16,16]{1,0:T(8,128)S(1)}, f32[16,16]{1,0:T(8,128)}, u32[]{:S(2)}) copy-start(f32[16,16]{1,0:T(8,128)} %weight_ref) | copy-start | bytes 3076
  22.6 4.7 %copy-start.4 = (s32[64]{0:T(128)S(1)}, s32[64]{0:T(128)}, u32[]{:S(2)}) copy-start(s32[64]{0:T(128)} %z_modes.2) | copy-start | bytes 772
  22.6 4.7 %copy-start.5 = (s32[64]{0:T(128)S(1)}, s32[64]{0:T(128)}, u32[]{:S(2)}) copy-start(s32[64]{0:T(128)} %phi_modes.2) | copy-start | bytes 772
  22.6 4.7 %copy-start.6 = (f32[16]{0:T(128)S(1)}, f32[16]{0:T(128)}, u32[]{:S(2)}) copy-start(f32[16]{0:T(128)} %bias) | copy-start | bytes 196
  22.7 14.1 %collective-permute-start.2 = (f32[4,8,2,8,128]{4,3,2,1,0:T(8,128)S(1)}, f32[4,8,2,8,128]{4,3,2,1,0:T(8,128)S(1)}, u32[]{:S(2)}, u32[]{:S(2)}) collective-permute-start(f32[4,8,2,8,128]{4,3,2,1,0:T(8,128)S(1)} %get-tuple-element.92), channel_id=1, source_target_pairs={{0,2},{1,3},{2,0},{3,1},{4,6},{5,7},{6,4},{7,5},{8,10},{9,11},{10,... | collective-permute-start | bytes 786440 | tf_op jit(solution)/shard_map/ppermute | solution.py:344
  25.7 11.1 %collective-permute-start.4 = (f32[4,8,2,8,128]{4,3,2,1,0:T(8,128)S(1)}, f32[4,8,2,8,128]{4,3,2,1,0:T(8,128)S(1)}, u32[]{:S(2)}, u32[]{:S(2)}) collective-permute-start(f32[4,8,2,8,128]{4,3,2,1,0:T(8,128)S(1)} %get-tuple-element.95), channel_id=1, source_target_pairs={{0,4},{4,0},{8,12},{12,8},{16,20},{20,16},{24,28},{28,24},{1,5},{5... | collective-permute-start | bytes 786440 | tf_op jit(solution)/shard_map/ppermute | solution.py:344
  30.1 3.4 %copy-start.1 = (bf16[384,512]{1,0:T(8,128)(2,1)}, bf16[384,512]{1,0:T(8,128)(2,1)S(1)}, u32[]{:S(2)}) copy-start(bf16[384,512]{1,0:T(8,128)(2,1)S(1)} %get-tuple-element.158.refs_12_) | copy-start | bytes 1179652
  30.1 3.4 %copy-start.2 = (bf16[256,384]{1,0:T(8,128)(2,1)}, bf16[256,384]{1,0:T(8,128)(2,1)S(1)}, u32[]{:S(2)}) copy-start(bf16[256,384]{1,0:T(8,128)(2,1)S(1)} %get-tuple-element.159.refs_13_) | copy-start | bytes 589828
  37.0 9.3 %collective-permute-start.5 = (f32[4,8,2,8,128]{4,3,2,1,0:T(8,128)S(1)}, f32[4,8,2,8,128]{4,3,2,1,0:T(8,128)S(1)}, u32[]{:S(2)}, u32[]{:S(2)}) collective-permute-start(f32[4,8,2,8,128]{4,3,2,1,0:T(8,128)S(1)} %get-tuple-element.113), channel_id=1, source_target_pairs={{0,4},{4,0},{8,12},{12,8},{16,20},{20,16},{24,28},{28,24},{1,5},{5... | collective-permute-start | bytes 786440 | tf_op jit(solution)/shard_map/ppermute | solution.py:344
  37.5 9.2 %collective-permute-start.6 = (f32[4,8,2,8,128]{4,3,2,1,0:T(8,128)S(1)}, f32[4,8,2,8,128]{4,3,2,1,0:T(8,128)S(1)}, u32[]{:S(2)}, u32[]{:S(2)}) collective-permute-start(f32[4,8,2,8,128]{4,3,2,1,0:T(8,128)S(1)} %get-tuple-element.114), channel_id=1, source_target_pairs={{0,2},{1,3},{2,0},{3,1},{4,6},{5,7},{6,4},{7,5},{8,10},{9,11},{10,... | collective-permute-start | bytes 786440 | tf_op jit(solution)/shard_map/ppermute | solution.py:344
  38.9 11.8 %collective-permute-start.1 = (f32[4,8,2,8,128]{4,3,2,1,0:T(8,128)S(1)}, f32[4,8,2,8,128]{4,3,2,1,0:T(8,128)S(1)}, u32[]{:S(2)}, u32[]{:S(2)}) collective-permute-start(f32[4,8,2,8,128]{4,3,2,1,0:T(8,128)S(1)} %get-tuple-element.91), channel_id=1, source_target_pairs={{0,2},{1,3},{2,0},{3,1},{4,6},{5,7},{6,4},{7,5},{8,10},{9,11},{10,... | collective-permute-start | bytes 786440 | tf_op jit(solution)/shard_map/ppermute | solution.py:344
  39.6 11.1 %collective-permute-start.7 = (f32[4,8,2,8,128]{4,3,2,1,0:T(8,128)S(1)}, f32[4,8,2,8,128]{4,3,2,1,0:T(8,128)S(1)}, u32[]{:S(2)}, u32[]{:S(2)}) collective-permute-start(f32[4,8,2,8,128]{4,3,2,1,0:T(8,128)S(1)} %get-tuple-element.120), channel_id=1, source_target_pairs={{0,4},{4,0},{8,12},{12,8},{16,20},{20,16},{24,28},{28,24},{1,5},{5... | collective-permute-start | bytes 786440 | tf_op jit(solution)/shard_map/ppermute | solution.py:344
  50.8 10.8 %collective-permute-start.8 = (f32[1,16,2,8,128]{4,3,2,1,0:T(8,128)S(1)}, f32[1,16,2,8,128]{4,3,2,1,0:T(8,128)S(1)}, u32[]{:S(2)}, u32[]{:S(2)}) collective-permute-start(f32[1,16,2,8,128]{4,3,2,1,0:T(8,128)S(1)} %get-tuple-element.123), channel_id=1, source_target_pairs={{0,16},{4,20},{8,24},{12,28},{16,0},{20,4},{24,8},{28,12},{1,17},{... | collective-permute-start | bytes 393224 | tf_op jit(solution)/shard_map/ppermute | solution.py:344
  53.6 8.0 %collective-permute-start.9 = (f32[1,16,2,8,128]{4,3,2,1,0:T(8,128)S(1)}, f32[1,16,2,8,128]{4,3,2,1,0:T(8,128)S(1)}, u32[]{:S(2)}, u32[]{:S(2)}) collective-permute-start(f32[1,16,2,8,128]{4,3,2,1,0:T(8,128)S(1)} %get-tuple-element.124), channel_id=1, source_target_pairs={{0,8},{4,12},{8,0},{12,4},{16,24},{20,28},{24,16},{28,20},{1,9},{5... | collective-permute-start | bytes 393224 | tf_op jit(solution)/shard_map/ppermute | solution.py:344
  55.2 7.5 %collective-permute-start.10 = (f32[1,16,2,8,128]{4,3,2,1,0:T(8,128)S(1)}, f32[1,16,2,8,128]{4,3,2,1,0:T(8,128)S(1)}, u32[]{:S(2)}, u32[]{:S(2)}) collective-permute-start(f32[1,16,2,8,128]{4,3,2,1,0:T(8,128)S(1)} %get-tuple-element.125), channel_id=1, source_target_pairs={{0,24},{4,28},{8,16},{12,20},{16,8},{20,12},{24,0},{28,4},{1,25},{... | collective-permute-start | bytes 393224 | tf_op jit(solution)/shard_map/ppermute | solution.py:344
  63.1 11.1 %collective-permute-start.13 = (f32[1,16,2,8,128]{4,3,2,1,0:T(8,128)S(1)}, f32[1,16,2,8,128]{4,3,2,1,0:T(8,128)S(1)}, u32[]{:S(2)}, u32[]{:S(2)}) collective-permute-start(f32[1,16,2,8,128]{4,3,2,1,0:T(8,128)S(1)} %bitcast.9), channel_id=1, source_target_pairs={{0,24},{4,28},{8,16},{12,20},{16,8},{20,12},{24,0},{28,4},{1,25},{... | collective-permute-start | bytes 393224 | tf_op jit(solution)/shard_map/ppermute | solution.py:344
  66.6 7.6 %collective-permute-start.12 = (f32[1,16,2,8,128]{4,3,2,1,0:T(8,128)S(1)}, f32[1,16,2,8,128]{4,3,2,1,0:T(8,128)S(1)}, u32[]{:S(2)}, u32[]{:S(2)}) collective-permute-start(f32[1,16,2,8,128]{4,3,2,1,0:T(8,128)S(1)} %bitcast.10), channel_id=1, source_target_pairs={{0,8},{4,12},{8,0},{12,4},{16,24},{20,28},{24,16},{28,20},{1,9},{5... | collective-permute-start | bytes 393224 | tf_op jit(solution)/shard_map/ppermute | solution.py:344
  67.9 9.2 %collective-permute-start.11 = (f32[1,16,2,8,128]{4,3,2,1,0:T(8,128)S(1)}, f32[1,16,2,8,128]{4,3,2,1,0:T(8,128)S(1)}, u32[]{:S(2)}, u32[]{:S(2)}) collective-permute-start(f32[1,16,2,8,128]{4,3,2,1,0:T(8,128)S(1)} %bitcast.11), channel_id=1, source_target_pairs={{0,16},{4,20},{8,24},{12,28},{16,0},{20,4},{24,8},{28,12},{1,17},{... | collective-permute-start | bytes 393224 | tf_op jit(solution)/shard_map/ppermute | solution.py:344
  77.2 9.3 %collective-permute-start.15 = (f32[4,8,2,8,128]{4,3,2,1,0:T(8,128)S(1)}, f32[4,8,2,8,128]{4,3,2,1,0:T(8,128)S(1)}, u32[]{:S(2)}, u32[]{:S(2)}) collective-permute-start(f32[4,8,2,8,128]{4,3,2,1,0:T(8,128)S(1)} %get-tuple-element.176), channel_id=1, source_target_pairs={{0,2},{1,3},{2,0},{3,1},{4,6},{5,7},{6,4},{7,5},{8,10},{9,11},{10,... | collective-permute-start | bytes 786440 | tf_op jit(solution)/shard_map/ppermute | solution.py:344
  79.0 9.2 %collective-permute-start.14 = (f32[4,8,2,8,128]{4,3,2,1,0:T(8,128)S(1)}, f32[4,8,2,8,128]{4,3,2,1,0:T(8,128)S(1)}, u32[]{:S(2)}, u32[]{:S(2)}) collective-permute-start(f32[4,8,2,8,128]{4,3,2,1,0:T(8,128)S(1)} %get-tuple-element.177), channel_id=1, source_target_pairs={{0,4},{4,0},{8,12},{12,8},{16,20},{20,16},{24,28},{28,24},{1,5},{5... | collective-permute-start | bytes 786440 | tf_op jit(solution)/shard_map/ppermute | solution.py:344
  80.4 13.5 %collective-permute-start.18 = (f32[4,8,2,8,128]{4,3,2,1,0:T(8,128)S(1)}, f32[4,8,2,8,128]{4,3,2,1,0:T(8,128)S(1)}, u32[]{:S(2)}, u32[]{:S(2)}) collective-permute-start(f32[4,8,2,8,128]{4,3,2,1,0:T(8,128)S(1)} %get-tuple-element.176), channel_id=1, source_target_pairs={{0,4},{4,0},{8,12},{12,8},{16,20},{20,16},{24,28},{28,24},{1,5},{5... | collective-permute-start | bytes 786440 | tf_op jit(solution)/shard_map/ppermute | solution.py:344
  81.0 12.9 %collective-permute-start.16 = (f32[4,8,2,8,128]{4,3,2,1,0:T(8,128)S(1)}, f32[4,8,2,8,128]{4,3,2,1,0:T(8,128)S(1)}, u32[]{:S(2)}, u32[]{:S(2)}) collective-permute-start(f32[4,8,2,8,128]{4,3,2,1,0:T(8,128)S(1)} %get-tuple-element.177), channel_id=1, source_target_pairs={{0,2},{1,3},{2,0},{3,1},{4,6},{5,7},{6,4},{7,5},{8,10},{9,11},{10,... | collective-permute-start | bytes 786440 | tf_op jit(solution)/shard_map/ppermute | solution.py:344
  81.3 16.0 %collective-permute-start.20 = (f32[4,16,2,8,128]{4,3,2,1,0:T(8,128)S(1)}, f32[4,16,2,8,128]{4,3,2,1,0:T(8,128)S(1)}, u32[]{:S(2)}, u32[]{:S(2)}) collective-permute-start(f32[4,16,2,8,128]{4,3,2,1,0:T(8,128)S(1)} %pad_maximum_fusion.refs_0_), channel_id=1, source_target_pairs={{0,1},{1,0},{2,3},{3,2},{4,5},{5,4},{6,7},{7,6},{8,9},{9,8},{10,11... | collective-permute-start | bytes 1572872 | tf_op jit(solution)/shard_map/ppermute | solution.py:344
  88.2 7.6 %collective-permute-start.17 = (f32[4,8,2,8,128]{4,3,2,1,0:T(8,128)S(1)}, f32[4,8,2,8,128]{4,3,2,1,0:T(8,128)S(1)}, u32[]{:S(2)}, u32[]{:S(2)}) collective-permute-start(f32[4,8,2,8,128]{4,3,2,1,0:T(8,128)S(1)} %collective-permute-done.14), channel_id=1, source_target_pairs={{0,2},{1,3},{2,0},{3,1},{4,6},{5,7},{6,4},{7,5},{8,10},{9,11},{10,... | collective-permute-start | bytes 786440 | tf_op jit(solution)/shard_map/ppermute | solution.py:344
  88.6 8.8 %collective-permute-start.19 = (f32[4,8,2,8,128]{4,3,2,1,0:T(8,128)S(1)}, f32[4,8,2,8,128]{4,3,2,1,0:T(8,128)S(1)}, u32[]{:S(2)}, u32[]{:S(2)}) collective-permute-start(f32[4,8,2,8,128]{4,3,2,1,0:T(8,128)S(1)} %collective-permute-done.15), channel_id=1, source_target_pairs={{0,4},{4,0},{8,12},{12,8},{16,20},{20,16},{24,28},{28,24},{1,5},{5... | collective-permute-start | bytes 786440 | tf_op jit(solution)/shard_map/ppermute | solution.py:344
  93.9 1.5 %collective-permute-start.24 = (f32[4,8,2,8,128]{4,3,2,1,0:T(8,128)S(1)}, f32[4,8,2,8,128]{4,3,2,1,0:T(8,128)S(1)}, u32[]{:S(2)}, u32[]{:S(2)}) collective-permute-start(f32[4,8,2,8,128]{4,3,2,1,0:T(8,128)S(1)} %collective-permute-done.18.refs_4_), channel_id=1, source_target_pairs={{0,1},{1,0},{2,3},{3,2},{4,5},{5,4},{6,7},{7,6},{8,9},{9,8},{10,11... | collective-permute-start | bytes 786440 | tf_op jit(solution)/shard_map/ppermute | solution.py:344
  93.9 4.9 %collective-permute-start.21 = (f32[4,16,2,8,128]{4,3,2,1,0:T(8,128)S(1)}, f32[4,16,2,8,128]{4,3,2,1,0:T(8,128)S(1)}, u32[]{:S(2)}, u32[]{:S(2)}) collective-permute-start(f32[4,16,2,8,128]{4,3,2,1,0:T(8,128)S(1)} %constant_dynamic-update-slice_fusion.refs_1_), channel_id=1, source_target_pairs={{0,1},{1,0},{2,3},{3,2},{4,5},{5,4},{6,7},{7,6},{8,9},{9,8},{10,11... | collective-permute-start | bytes 1572872 | tf_op jit(solution)/shard_map/ppermute | solution.py:344
  95.4 1.9 %collective-permute-start.22 = (f32[4,8,2,8,128]{4,3,2,1,0:T(8,128)S(1)}, f32[4,8,2,8,128]{4,3,2,1,0:T(8,128)S(1)}, u32[]{:S(2)}, u32[]{:S(2)}) collective-permute-start(f32[4,8,2,8,128]{4,3,2,1,0:T(8,128)S(1)} %collective-permute-done.16.refs_2_), channel_id=1, source_target_pairs={{0,1},{1,0},{2,3},{3,2},{4,5},{5,4},{6,7},{7,6},{8,9},{9,8},{10,11... | collective-permute-start | bytes 786440 | tf_op jit(solution)/shard_map/ppermute | solution.py:344
  95.9 1.5 %collective-permute-start.23 = (f32[4,8,2,8,128]{4,3,2,1,0:T(8,128)S(1)}, f32[4,8,2,8,128]{4,3,2,1,0:T(8,128)S(1)}, u32[]{:S(2)}, u32[]{:S(2)}) collective-permute-start(f32[4,8,2,8,128]{4,3,2,1,0:T(8,128)S(1)} %collective-permute-done.17.refs_3_), channel_id=1, source_target_pairs={{0,1},{1,0},{2,3},{3,2},{4,5},{5,4},{6,7},{7,6},{8,9},{9,8},{10,11... | collective-permute-start | bytes 786440 | tf_op jit(solution)/shard_map/ppermute | solution.py:344
  97.3 1.5 %collective-permute-start.25 = (f32[4,8,2,8,128]{4,3,2,1,0:T(8,128)S(1)}, f32[4,8,2,8,128]{4,3,2,1,0:T(8,128)S(1)}, u32[]{:S(2)}, u32[]{:S(2)}) collective-permute-start(f32[4,8,2,8,128]{4,3,2,1,0:T(8,128)S(1)} %collective-permute-done.19.refs_5_), channel_id=1, source_target_pairs={{0,1},{1,0},{2,3},{3,2},{4,5},{5,4},{6,7},{7,6},{8,9},{9,8},{10,11... | collective-permute-start | bytes 786440 | tf_op jit(solution)/shard_map/ppermute | solution.py:344
